TPU v7x, 32 devices: a whole 2x2x4 slice. The times are simulated.
32 devices in a mesh: probe: 2 (over x), slab: 16 (over z, y, core).
Axes of the slice: x: 2, y: 2, z: 4, core: 2. Of those that a mesh axis runs over, the one named last changes fastest.
Arguments:
- probes: float32 [3, 512, 16384], P(None, 'probe', 'slab'), may hold values from -6 to 6
- viscosity: float32 [16384], P('slab'), may hold values from 0.8 to 1.25
- coupling: float32 [4, 3, 3, 16384], P(None, None, None, 'slab'), may hold values from -0.06 to 0.06
- misfit_weight: float32 [3, 16384], P(None, 'slab'), may hold values from 0.7 to 1.4
- band_offsets: int32 [4], replicated, may hold values from -4 to 4, as said below
Outputs:
- basis: float32 [3, 512, 16384], P(None, 'probe', 'slab')
- r_factor: float32 [512, 512], P('probe')
Inputs may be any that keep to these rules, and one draw needn't show every extreme that they name: `band_offsets`: 4 distinct nonzero offsets; both -4 and 4 are among them.
All inputs are finite; a program needn't handle non-finite values.
Results may differ from a plain program's by a relative error of at most 0.0003.
Values sent between devices are 32-bit elements; how exact they have to be, the bound alone decides.
No kernel may reach another device: no remote copies, remote signals or barrier semaphores. Data moves between devices by JAX's collectives and lax.ppermute only.
A program may use at most 64 MiB of HBM per device.

v0:
```python
import jax
import jax.numpy as jnp
from jax import lax
from jax.sharding import PartitionSpec as P

REACH = 4
BANDS = 4


def extended(block, sides, width):
    for axis, dim in sides:
        count = lax.axis_size(axis)
        forward = [(i, i + 1) for i in range(count - 1)]
        backward = [(target, source) for source, target in forward]
        low = lax.ppermute(
            lax.slice_in_dim(block, block.shape[dim] - width, None, axis=dim), axis, forward
        )
        high = lax.ppermute(lax.slice_in_dim(block, 0, width, axis=dim), axis, backward)
        block = jnp.concatenate([low, block, high], axis=dim)
    return block


def small_cholesky(matrix):
    size = matrix.shape[0]
    places = jnp.arange(size, dtype=jnp.int32)

    def column_step(index, lower):
        row_j = lax.dynamic_index_in_dim(lower, index, 0, keepdims=False)
        col_a = lax.dynamic_index_in_dim(matrix, index, 1, keepdims=False)
        column = col_a - jnp.dot(lower, row_j, precision=lax.Precision.HIGHEST)
        pivot = jnp.sqrt(jnp.sum(jnp.where(places == index, column, 0.0)))
        filled = jnp.where(places > index, column / pivot, jnp.where(places == index, pivot, 0.0))
        marker = (places == index).astype(matrix.dtype)
        return lower + filled[:, None] * marker[None, :]

    return lax.fori_loop(0, size, column_step, jnp.zeros_like(matrix))


def small_lower_inverse(lower):
    size = lower.shape[0]
    places = jnp.arange(size, dtype=jnp.int32)

    def row_step(index, inverse):
        row_l = lax.dynamic_index_in_dim(lower, index, 0, keepdims=False)
        diag_value = jnp.sum(jnp.where(places == index, row_l, 0.0))
        marker = (places == index).astype(lower.dtype)
        strict = jnp.where(places < index, row_l, 0.0)
        new_row = (marker - jnp.dot(strict, inverse, precision=lax.Precision.HIGHEST)) / diag_value
        return inverse + marker[:, None] * new_row[None, :]

    return lax.fori_loop(0, size, row_step, jnp.zeros_like(lower))


def factorize(gram):
    size = gram.shape[0]
    width = 64
    count = size // width
    work = gram
    lower_blocks = {}
    inverse_diag = []
    for outer in range(count):
        lo = outer * width
        diag_block = work[lo : lo + width, lo : lo + width]
        diag_lower = small_cholesky(diag_block)
        diag_inverse = small_lower_inverse(diag_lower)
        lower_blocks[outer, outer] = diag_lower
        inverse_diag.append(diag_inverse)
        if outer + 1 < count:
            below = jnp.dot(
                work[lo + width :, lo : lo + width], diag_inverse.T, precision=lax.Precision.HIGHEST
            )
            for inner in range(outer + 1, count):
                start = (inner - outer - 1) * width
                lower_blocks[inner, outer] = below[start : start + width]
            trailing = work[lo + width :, lo + width :] - jnp.dot(
                below, below.T, precision=lax.Precision.HIGHEST
            )
            work = work.at[lo + width :, lo + width :].set(trailing)
    zero_block = jnp.zeros((width, width), dtype=gram.dtype)
    lower_rows = []
    for inner in range(count):
        lower_rows.append(
            jnp.concatenate(
                [lower_blocks.get((inner, outer), zero_block) for outer in range(count)], 1
            )
        )
    lower = jnp.concatenate(lower_rows, 0)
    inverse_blocks = {}
    for outer in range(count):
        inverse_blocks[outer, outer] = inverse_diag[outer]
        for inner in range(outer + 1, count):
            total = jnp.zeros((width, width), dtype=gram.dtype)
            for middle in range(outer, inner):
                total = total + jnp.dot(
                    lower_blocks[inner, middle],
                    inverse_blocks[middle, outer],
                    precision=lax.Precision.HIGHEST,
                )
            inverse_blocks[inner, outer] = 0.0 - jnp.dot(
                inverse_diag[inner], total, precision=lax.Precision.HIGHEST
            )
    inverse_rows = []
    for inner in range(count):
        inverse_rows.append(
            jnp.concatenate(
                [inverse_blocks.get((inner, outer), zero_block) for outer in range(count)], 1
            )
        )
    lower_inverse = jnp.concatenate(inverse_rows, 0)
    return (lower.T, lower_inverse.T)


def tangent_ext(padded, base_start, length, visc_ext, coup_ext, offsets):
    summed = [lax.dynamic_slice_in_dim(padded[comp], base_start, length, 1) for comp in range(3)]
    for which_band in range(BANDS):
        start = base_start + offsets[which_band]
        shifted = lax.dynamic_slice_in_dim(padded, start, length, 2)
        for out_comp in range(3):
            for in_comp in range(3):
                summed[out_comp] = (
                    summed[out_comp]
                    + coup_ext[which_band, out_comp, in_comp][None, :] * shifted[in_comp]
                )
    return visc_ext[None, None, :] * jnp.stack(summed)


def adjoint_ext(scaled_ext, coup_ext, offsets, cells):
    result = scaled_ext[:, :, REACH : REACH + cells]
    for which_band in range(BANDS):
        parts = []
        for in_comp in range(3):
            acc = coup_ext[which_band, 0, in_comp][None, :] * scaled_ext[0]
            acc = acc + coup_ext[which_band, 1, in_comp][None, :] * scaled_ext[1]
            acc = acc + coup_ext[which_band, 2, in_comp][None, :] * scaled_ext[2]
            parts.append(acc)
        start = REACH - offsets[which_band]
        result = result + lax.dynamic_slice_in_dim(jnp.stack(parts), start, cells, 2)
    return result


def body(probes, viscosity, coupling, misfit_weight, band_offsets):
    cells = probes.shape[2]
    columns = probes.shape[1]
    stacked = jnp.concatenate(
        [coupling.reshape(9 * BANDS, cells), viscosity[None, :], misfit_weight], 0
    )
    coef_ext = extended(stacked, (("slab", 1),), REACH)
    coup_ext = coef_ext[: 9 * BANDS].reshape(BANDS, 3, 3, cells + 2 * REACH)
    visc_ext = coef_ext[9 * BANDS]
    weight_ext = coef_ext[9 * BANDS + 1 : 9 * BANDS + 4]
    visc_own = visc_ext[REACH : REACH + cells]
    weight_own = weight_ext[:, REACH : REACH + cells]
    values = probes
    for turn in range(2):
        padded = extended(values, (("slab", 2),), REACH)
        image = tangent_ext(padded, REACH, cells, visc_own, coupling, band_offsets)
        scaled = visc_own[None, None, :] * (weight_own[:, None, :] * image)
        scaled_ext = extended(scaled, (("slab", 2),), REACH)
        values = adjoint_ext(scaled_ext, coup_ext, band_offsets, cells)
    unknowns = 3 * cells * lax.axis_size("slab")
    mine = lax.axis_index("probe") * columns
    gram_part = jnp.einsum(
        "kpc,kqc->pq",
        values,
        lax.all_gather(values, "probe", axis=1, tiled=True),
        precision=lax.Precision.HIGHEST,
    )
    gram_part = lax.psum(gram_part, "slab") / unknowns
    gram = lax.all_gather(gram_part, "probe", axis=0, tiled=True)
    upper, r_inverse = factorize(gram)
    piece = lax.all_gather(values, "probe", axis=1, tiled=True)
    block = lax.dynamic_slice(r_inverse, (0, mine), (piece.shape[1], columns))
    basis = jnp.einsum("kqc,qp->kpc", piece, block, precision=lax.Precision.HIGHEST)
    r_rows = lax.dynamic_slice_in_dim(upper, mine, columns, 0)
    return (basis, r_rows)


def solution(mesh):
    return jax.shard_map(
        body,
        mesh=mesh,
        in_specs=(
            P(None, "probe", "slab"),
            P("slab"),
            P(None, None, None, "slab"),
            P(None, "slab"),
            P(),
        ),
        out_specs=(P(None, "probe", "slab"), P("probe", None)),
        check_vma=False,
    )
```

profile of v0, /device:TPU:0, one launch (start us, length us, event | category | flops | bytes accessed | tf_op | source)
XLA Modules:
  0.0 2017.6 jit_solution(10542304875931568321)
XLA Ops:
  75.1 7.9 collective-permute-start.6
  104.4 10.0 collective-permute-start.8
  127.1 7.0 fusion.194
  134.1 88.3 %all-gather.3.cloned.1.call-done = f32[3,512,1024]{2,1,0:T(8,128)} async-done(((f32[3,256,1024]{2,1,0:T(8,128)}), f32[3,512,1024]{2,1,0:T(8,128)}) %all-gather.3.cloned.1.call-update) | async-done | bytes 6291472 | tf_op jit(solution)/shard_map/all_gather | solution.py:165
  222.5 8.3 convolution_bitcast_fusion.17
  230.9 90.2 %all-reduce.4.cloned.1.call-done = f32[256,512]{1,0:T(8,128)} async-done(((f32[256,512]{1,0:T(8,128)}), f32[256,512]{1,0:T(8,128)}) %all-reduce.4.cloned.1.call-update) | async-done | bytes 524304 | tf_op jit(solution)/shard_map/psum | solution.py:168
  323.2 21.8 %all-gather.5.cloned.1.call-done = f32[512,512]{1,0:T(8,128)} async-done(((f32[256,512]{1,0:T(8,128)}), f32[512,512]{1,0:T(8,128)}) %all-gather.5.cloned.1.call-update) | async-done | bytes 1048592 | tf_op jit(solution)/shard_map/all_gather | solution.py:169
  345.9 101.4 %while.247 = (s32[]{:T(128)}, f32[64,64]{1,0:T(8,128)S(1)}, f32[64,64]{0,1:T(8,128)S(1)}, s32[]{:T(128)}, s32[]{:T(128)}) while((s32[]{:T(128)}, f32[64,64]{1,0:T(8,128)S(1)}, f32[64,64]{0,1:T(8,128)S(1)}, s32[]{:T(128)}, s32[]{:T(128)}) %tuple.698), condition=%wide.region_3.4_spmd.clone.clone, body=%wide.region_1.3_spmd.clone.clone.sunk | while | flops 66242 | bytes 102496 | solution.py:36
  447.3 94.9 %while.248 = (s32[]{:T(128)}, f32[64,64]{1,0:T(8,128)S(1)}, f32[64,64]{1,0:T(8,128)S(1)}, s32[]{:T(128)}, s32[]{:T(128)}) while((s32[]{:T(128)}, f32[64,64]{1,0:T(8,128)S(1)}, f32[64,64]{1,0:T(8,128)S(1)}, s32[]{:T(128)}, s32[]{:T(128)}) %tuple.701), condition=%wide.region_6.7_spmd.clone.clone, body=%wide.region_4.6_spmd.clone.clone.sunk | while | flops 66242 | bytes 70480 | solution.py:51
  545.3 99.6 %while.249 = (s32[]{:T(128)}, f32[64,64]{1,0:T(8,128)S(1)}, f32[64,64]{0,1:T(8,128)S(1)}, s32[]{:T(128)}, s32[]{:T(128)}) while((s32[]{:T(128)}, f32[64,64]{1,0:T(8,128)S(1)}, f32[64,64]{0,1:T(8,128)S(1)}, s32[]{:T(128)}, s32[]{:T(128)}) %tuple.704), condition=%wide.region_9.10_spmd.clone.clone, body=%wide.region_7.9_spmd.clone.clone.sunk | while | flops 66242 | bytes 102496 | solution.py:36
  644.9 101.3 %while.250 = (s32[]{:T(128)}, f32[64,64]{1,0:T(8,128)S(1)}, f32[64,64]{1,0:T(8,128)S(1)}, s32[]{:T(128)}, s32[]{:T(128)}) while((s32[]{:T(128)}, f32[64,64]{1,0:T(8,128)S(1)}, f32[64,64]{1,0:T(8,128)S(1)}, s32[]{:T(128)}, s32[]{:T(128)}) %tuple.707), condition=%wide.region_12.13_spmd.clone.clone, body=%wide.region_10.12_spmd.clone.clone.sunk | while | flops 66242 | bytes 70480 | solution.py:51
  747.4 108.7 %while.251 = (s32[]{:T(128)}, f32[64,64]{1,0:T(8,128)S(1)}, f32[64,64]{0,1:T(8,128)S(1)}, s32[]{:T(128)}, s32[]{:T(128)}) while((s32[]{:T(128)}, f32[64,64]{1,0:T(8,128)S(1)}, f32[64,64]{0,1:T(8,128)S(1)}, s32[]{:T(128)}, s32[]{:T(128)}) %tuple.710), condition=%wide.region_15.16_spmd.clone.clone, body=%wide.region_13.15_spmd.clone.clone.sunk | while | flops 66242 | bytes 102496 | solution.py:36
  856.2 95.7 %while.252 = (s32[]{:T(128)}, f32[64,64]{1,0:T(8,128)S(1)}, f32[64,64]{1,0:T(8,128)S(1)}, s32[]{:T(128)}, s32[]{:T(128)}) while((s32[]{:T(128)}, f32[64,64]{1,0:T(8,128)S(1)}, f32[64,64]{1,0:T(8,128)S(1)}, s32[]{:T(128)}, s32[]{:T(128)}) %tuple.713), condition=%wide.region_18.19_spmd.clone.clone, body=%wide.region_16.18_spmd.clone.clone.sunk | while | flops 66242 | bytes 70480 | solution.py:51
  952.9 95.9 %while.253 = (s32[]{:T(128)}, f32[64,64]{1,0:T(8,128)S(1)}, f32[64,64]{0,1:T(8,128)S(1)}, s32[]{:T(128)}, s32[]{:T(128)}) while((s32[]{:T(128)}, f32[64,64]{1,0:T(8,128)S(1)}, f32[64,64]{0,1:T(8,128)S(1)}, s32[]{:T(128)}, s32[]{:T(128)}) %tuple.716), condition=%wide.region_21.22_spmd.clone.clone, body=%wide.region_19.21_spmd.clone.clone.sunk | while | flops 66242 | bytes 102496 | solution.py:36
  1048.8 96.6 %while.254 = (s32[]{:T(128)}, f32[64,64]{1,0:T(8,128)S(1)}, f32[64,64]{1,0:T(8,128)S(1)}, s32[]{:T(128)}, s32[]{:T(128)}) while((s32[]{:T(128)}, f32[64,64]{1,0:T(8,128)S(1)}, f32[64,64]{1,0:T(8,128)S(1)}, s32[]{:T(128)}, s32[]{:T(128)}) %tuple.719), condition=%wide.region_24.25_spmd.clone.clone, body=%wide.region_22.24_spmd.clone.clone.sunk | while | flops 66242 | bytes 70480 | solution.py:51
  1146.2 108.7 %while.255 = (s32[]{:T(128)}, f32[64,64]{1,0:T(8,128)S(1)}, f32[64,64]{0,1:T(8,128)S(1)}, s32[]{:T(128)}, s32[]{:T(128)}) while((s32[]{:T(128)}, f32[64,64]{1,0:T(8,128)S(1)}, f32[64,64]{0,1:T(8,128)S(1)}, s32[]{:T(128)}, s32[]{:T(128)}) %tuple.722), condition=%wide.region_27.28_spmd.clone.clone, body=%wide.region_25.27_spmd.clone.clone.sunk | while | flops 66242 | bytes 102496 | solution.py:36
  1255.0 95.6 %while.256 = (s32[]{:T(128)}, f32[64,64]{1,0:T(8,128)S(1)}, f32[64,64]{1,0:T(8,128)S(1)}, s32[]{:T(128)}, s32[]{:T(128)}) while((s32[]{:T(128)}, f32[64,64]{1,0:T(8,128)S(1)}, f32[64,64]{1,0:T(8,128)S(1)}, s32[]{:T(128)}, s32[]{:T(128)}) %tuple.725), condition=%wide.region_30.31_spmd.clone.clone, body=%wide.region_28.30_spmd.clone.clone.sunk | while | flops 66242 | bytes 70480 | solution.py:51
  1351.3 95.6 %while.257 = (s32[]{:T(128)}, f32[64,64]{1,0:T(8,128)S(1)}, f32[64,64]{0,1:T(8,128)S(1)}, s32[]{:T(128)}, s32[]{:T(128)}) while((s32[]{:T(128)}, f32[64,64]{1,0:T(8,128)S(1)}, f32[64,64]{0,1:T(8,128)S(1)}, s32[]{:T(128)}, s32[]{:T(128)}) %tuple.728), condition=%wide.region_33.34_spmd.clone.clone, body=%wide.region_31.33_spmd.clone.clone.sunk | while | flops 66242 | bytes 102496 | solution.py:36
  1446.9 96.7 %while.258 = (s32[]{:T(128)}, f32[64,64]{1,0:T(8,128)S(1)}, f32[64,64]{1,0:T(8,128)S(1)}, s32[]{:T(128)}, s32[]{:T(128)}) while((s32[]{:T(128)}, f32[64,64]{1,0:T(8,128)S(1)}, f32[64,64]{1,0:T(8,128)S(1)}, s32[]{:T(128)}, s32[]{:T(128)}) %tuple.731), condition=%wide.region_36.37_spmd.clone.clone, body=%wide.region_34.36_spmd.clone.clone.sunk | while | flops 66242 | bytes 70480 | solution.py:51
  1544.2 102.0 %while.259 = (s32[]{:T(128)}, f32[64,64]{1,0:T(8,128)S(1)}, f32[64,64]{0,1:T(8,128)S(1)}, s32[]{:T(128)}, s32[]{:T(128)}) while((s32[]{:T(128)}, f32[64,64]{1,0:T(8,128)S(1)}, f32[64,64]{0,1:T(8,128)S(1)}, s32[]{:T(128)}, s32[]{:T(128)}) %tuple.734), condition=%wide.region_39.40_spmd.clone.clone, body=%wide.region_37.39_spmd.clone.clone.sunk | while | flops 66242 | bytes 102496 | solution.py:36
  1646.2 101.5 %while.260 = (s32[]{:T(128)}, f32[64,64]{1,0:T(8,128)S(1)}, f32[64,64]{1,0:T(8,128)S(1)}, s32[]{:T(128)}, s32[]{:T(128)}) while((s32[]{:T(128)}, f32[64,64]{1,0:T(8,128)S(1)}, f32[64,64]{1,0:T(8,128)S(1)}, s32[]{:T(128)}, s32[]{:T(128)}) %tuple.737), condition=%wide.region_42.43_spmd.clone.clone, body=%wide.region_40.42_spmd.clone.clone.sunk | while | flops 66242 | bytes 70480 | solution.py:51
  1769.8 100.1 %while.261 = (s32[]{:T(128)}, f32[64,64]{1,0:T(8,128)S(1)}, f32[64,64]{0,1:T(8,128)S(1)}, s32[]{:T(128)}, s32[]{:T(128)}) while((s32[]{:T(128)}, f32[64,64]{1,0:T(8,128)S(1)}, f32[64,64]{0,1:T(8,128)S(1)}, s32[]{:T(128)}, s32[]{:T(128)}) %tuple.740), condition=%wide.region_45.46_spmd.clone.clone, body=%wide.region_43.45_spmd.clone.clone.sunk | while | flops 66242 | bytes 102496 | solution.py:36
  1894.4 94.9 %while.262 = (s32[]{:T(128)}, f32[64,64]{1,0:T(8,128)S(1)}, f32[64,64]{1,0:T(8,128)S(1)}, s32[]{:T(128)}, s32[]{:T(128)}) while((s32[]{:T(128)}, f32[64,64]{1,0:T(8,128)S(1)}, f32[64,64]{1,0:T(8,128)S(1)}, s32[]{:T(128)}, s32[]{:T(128)}) %tuple.743), condition=%wide.region_48.49_spmd.clone.clone, body=%wide.region_46.48_spmd.clone.clone.sunk | while | flops 66242 | bytes 70480 | solution.py:51
  2001.6 9.0 convolution_bitcast_fusion.16
  (5286 shorter events, 1391.2 us)
Async XLA Ops:
  7.2 215.3 %all-gather.3.cloned.1.call-start = ((), (), s32[]{:S(2)}) async-start(), calls=%async_computation | async-start | bytes 9437184 | tf_op jit(solution)/shard_map/all_gather | solution.py:165
  8.6 24.3 %collective-permute-start = (f32[3,256,4]{2,1,0:T(8,128)S(1)}, f32[3,256,4]{2,1,0:T(8,128)S(1)}, u32[]{:S(2)}, u32[]{:S(2)}) collective-permute-start(f32[3,256,4]{2,1,0:T(8,128)S(1)} %get-tuple-element.2063), channel_id=1, source_target_pairs={{0,1},{1,2},{2,3},{3,4},{4,5},{5,6},{6,7},{7,8},{8,9},{9,10},{10,1... | collective-permute-start | bytes 36872 | tf_op jit(solution)/shard_map/ppermute | solution.py:15
  11.0 22.6 %collective-permute-start.1 = (f32[3,256,4]{2,1,0:T(8,128)S(1)}, f32[3,256,4]{2,1,0:T(8,128)}, u32[]{:S(2)}, u32[]{:S(2)}) collective-permute-start(f32[3,256,4]{2,1,0:T(8,128)S(1)} %get-tuple-element.2062), channel_id=1, source_target_pairs={{1,0},{2,1},{3,2},{4,3},{5,4},{6,5},{7,6},{8,7},{9,8},{10,9},{11,1... | collective-permute-start | bytes 36872 | tf_op jit(solution)/shard_map/ppermute | solution.py:18
  12.6 19.2 collective-permute-start.2
  17.7 14.0 collective-permute-start.3
  50.9 7.5 collective-permute-start.4
  55.2 5.0 collective-permute-start.5
  75.1 9.2 collective-permute-start.6
  82.9 3.7 collective-permute-start.7
  104.4 11.3 collective-permute-start.8
  114.4 3.7 collective-permute-start.9
  134.1 187.0 %all-reduce.4.cloned.1.call-start = ((), (), s32[]{:S(2)}) async-start(), calls=%async_computation.1 | async-start | bytes 1048576 | tf_op jit(solution)/shard_map/psum | solution.py:168
  230.8 114.2 %all-gather.5.cloned.1.call-start = ((), (), s32[]{:S(2)}) async-start(), calls=%async_computation.2 | async-start | bytes 1572864 | tf_op jit(solution)/shard_map/all_gather | solution.py:169
  345.9 198.4 %copy-start.16 = (f32[512,512]{1,0:T(8,128)S(1)}, f32[512,512]{1,0:T(8,128)}, u32[]{:S(2)}) copy-start(f32[512,512]{1,0:T(8,128)} %all-gather.5.cloned.1.call-done) | copy-start | bytes 3145732
  1759.5 111.2 %copy-start.24 = (f32[64,512]{0,1:T(8,128)S(1)}, f32[64,512]{0,1:T(8,128)}, u32[]{:S(2)}) copy-start(f32[64,512]{0,1:T(8,128)} %get-tuple-element.2103) | copy-start | bytes 393220
  1759.5 111.1 %copy-start.26 = (f32[64,512]{0,1:T(8,128)S(1)}, f32[64,512]{0,1:T(8,128)}, u32[]{:S(2)}) copy-start(f32[64,512]{0,1:T(8,128)} %get-tuple-element.2104) | copy-start | bytes 393220
  1759.5 111.1 %copy-start.28 = (f32[64,512]{0,1:T(8,128)S(1)}, f32[64,512]{0,1:T(8,128)}, u32[]{:S(2)}) copy-start(f32[64,512]{0,1:T(8,128)} %get-tuple-element.2105) | copy-start | bytes 393220
  1759.5 111.1 %copy-start.30 = (f32[64,512]{0,1:T(8,128)S(1)}, f32[64,512]{0,1:T(8,128)}, u32[]{:S(2)}) copy-start(f32[64,512]{0,1:T(8,128)} %get-tuple-element.2106) | copy-start | bytes 393220
  1889.5 101.6 %copy-start.52 = (f32[64,64]{0,1:T(8,128)S(1)}, f32[64,64]{0,1:T(8,128)}, u32[]{:S(2)}) copy-start(f32[64,64]{0,1:T(8,128)} %copy.91) | copy-start | bytes 49156
  1890.4 100.7 %copy-start.51 = (f32[64,64]{0,1:T(8,128)S(1)}, f32[64,64]{0,1:T(8,128)}, u32[]{:S(2)}) copy-start(f32[64,64]{0,1:T(8,128)} %copy.83) | copy-start | bytes 49156
  1891.0 100.2 %copy-start.50 = (f32[64,64]{0,1:T(8,128)S(1)}, f32[64,64]{0,1:T(8,128)}, u32[]{:S(2)}) copy-start(f32[64,64]{0,1:T(8,128)} %copy.76) | copy-start | bytes 49156
  1891.2 100.6 %copy-start.44 = (f32[64,64]{0,1:T(8,128)S(1)}, f32[64,64]{0,1:T(8,128)}, u32[]{:S(2)}) copy-start(f32[64,64]{0,1:T(8,128)} %copy.61) | copy-start | bytes 49156
  1893.3 99.3 %copy-start.41 = (f32[64,64]{0,1:T(8,128)S(1)}, f32[64,64]{0,1:T(8,128)}, u32[]{:S(2)}) copy-start(f32[64,64]{0,1:T(8,128)} %copy.105) | copy-start | bytes 49156
  1893.3 99.2 %copy-start.42 = (f32[64,64]{0,1:T(8,128)S(1)}, f32[64,64]{0,1:T(8,128)}, u32[]{:S(2)}) copy-start(f32[64,64]{0,1:T(8,128)} %copy.65) | copy-start | bytes 49156
  (193 other events, 875.4 us)
Sparse Core Ops, SparseCore 0:
  134.2 88.2 all-gather.2
  230.9 90.0 all-reduce.3
  323.2 21.7 all-gather.4
where the time goes:
time: 2040 us; the launch traced here: 2020 us
  matrix products  876 us (43%)
  other arithmetic  468 us (23%)
  loops' own time  355 us (17%)
  waiting for transfers between devices  205 us (10%)
  local copies, waits for them, and re-layouts  48.5 us (2%)
  starting transfers between devices  36.2 us (2%)
  between operations  28.7 us (1%)
    dot_general x512, matrix products, column_step(): column = col_a - jnp.dot(lower, row_j, precision=lax.Precision.HIGHEST)  409 us
    dot_general x512, matrix products, row_step(): jnp.dot(strict, inverse, precision=lax.Precision.HIGHEST)  401 us
    another operation x8, loops' own time, small_cholesky(): return lax.fori_loop(0, size, column_step, jnp.zeros_like(matrix))  354 us
    reduce_sum x512, other arithmetic, row_step(): diag_value = jnp.sum(jnp.where(places == index, row_l, 0.0))  333 us
    psum x1, waiting for transfers between devices, body(): gram_part = lax.psum(gram_part, 'slab') / unknowns  90.2 us
    all_gather x1, waiting for transfers between devices, body(): lax.all_gather(values, 'probe', axis=1, tiled=True)  88.3 us

commit v1 on v0

v1 whole, which is shorter than its diff:
```python
import functools

import jax
import jax.numpy as jnp
from jax import lax
from jax.experimental import pallas as pl
from jax.experimental.pallas import tpu as pltpu
from jax.sharding import PartitionSpec as P

REACH = 4
BANDS = 4
HALO = 4 * REACH
TERMS = 9 * BANDS
COEFS = TERMS + 4
TILE = 128
EXACT = lax.Precision.HIGHEST
CLOSE = lax.Precision.HIGH
VMEM = pl.BlockSpec(memory_space=pltpu.VMEM)
PARAMS = pltpu.CompilerParams(vmem_limit_bytes=48 * 2**20)


def pack_kernel(first_ref, last_ref, coef_ref, low_ref, high_ref):
    rows, cells = first_ref.shape[1], coef_ref.shape[1]
    for comp in range(3):
        spot = slice(HALO * comp, HALO * comp + HALO)
        low_ref[spot, :] = first_ref[comp].T[:HALO]
        high_ref[spot, :] = last_ref[comp].T[TILE - HALO :]
    blank = jnp.zeros((rows - COEFS, TILE), jnp.float32)
    spot = slice(3 * HALO, 4 * HALO)
    low_ref[spot, :] = jnp.concatenate([coef_ref[:, :TILE], blank], 0).T[:HALO]
    high_ref[spot, :] = jnp.concatenate([coef_ref[:, cells - TILE :], blank], 0).T[TILE - HALO :]


def pack_edges(probes, coefs):
    _, rows, cells = probes.shape
    edge = jax.ShapeDtypeStruct((4 * HALO, rows), jnp.float32)
    last = cells // TILE - 1
    return pl.pallas_call(
        pack_kernel,
        grid=(1,),
        in_specs=[
            pl.BlockSpec((3, rows, TILE), lambda i: (0, 0, 0)),
            pl.BlockSpec((3, rows, TILE), lambda i: (0, 0, last)),
            pl.BlockSpec((COEFS, cells), lambda i: (0, 0)),
        ],
        out_specs=[pl.BlockSpec((4 * HALO, rows), lambda i: (0, 0))] * 2,
        out_shape=[edge, edge],
        compiler_params=PARAMS,
    )(probes, probes, coefs)


def turned(x, amount):
    if isinstance(amount, int):
        return pltpu.roll(x, (TILE - amount) % TILE, 1)
    return pltpu.roll(x, lax.rem(TILE - amount, TILE), 1)


def moved(tiles, amount, lane):
    turns = [turned(t, amount) for t in tiles]
    return [
        jnp.where(lane < TILE - amount, turns[i], turns[min(i + 1, len(tiles) - 1)])
        for i in range(len(tiles))
    ]


def stretch(own, ends, lane):
    turns = [turned(t, TILE - HALO) for t in own]
    middle = [jnp.where(lane < HALO, turns[i], turns[i + 1]) for i in range(len(own) - 1)]
    return [jnp.where(lane < HALO, ends, turns[0])] + middle + [jnp.where(lane < HALO, turns[-1], ends)]


def panel_kernel(off_ref, x_ref, coef_ref, low_ref, high_ref, out_ref, ends_ref, tab_ref, mid_ref, in_ref):
    _, rows, cells = x_ref.shape
    count = cells // TILE
    lane = lax.broadcasted_iota(jnp.int32, (8, TILE), 1)
    offs = [off_ref[b] for b in range(BANDS)]

    blank = jnp.zeros((TILE - 2 * HALO, rows), jnp.float32)
    for comp in range(4):
        spot = slice(HALO * comp, HALO * comp + HALO)
        ends_ref[comp] = jnp.concatenate([low_ref[spot, :], high_ref[spot, :], blank], 0).T

    for group in range(COEFS // 8):
        spot = slice(8 * group, 8 * group + 8)
        ext = stretch(
            [coef_ref[spot, TILE * i : TILE * i + TILE] for i in range(count)], ends_ref[3, spot, :], lane
        )
        by_step = {(0, b): moved(ext, REACH, lane) for b in range(BANDS)}
        by_step.update({(2, b): moved(ext, 3 * REACH, lane) for b in range(BANDS)})
        for b in range(BANDS):
            by_step[1, b] = moved(ext, 2 * REACH - offs[b], lane)
            by_step[3, b] = moved(ext, 4 * REACH - offs[b], lane)
        for j in range(8):
            row = 8 * group + j
            if row >= TERMS:
                continue
            for step in range(4):
                for i in range(count + 1):
                    tile = by_step[step, row // 9][i]
                    tab_ref[step, row, :, TILE * i : TILE * i + TILE] = jnp.broadcast_to(
                        tile[j : j + 1, :], (8, TILE)
                    )
        if group == COEFS // 8 - 1:
            for half, step in enumerate((0, 2)):
                for i in range(count + 1):
                    tile = by_step[step, 0][i]
                    visc = jnp.broadcast_to(tile[4:5, :], (8, TILE))
                    for comp in range(3):
                        weight = jnp.broadcast_to(tile[5 + comp : 6 + comp, :], (8, TILE))
                        mid_ref[half, comp, :, TILE * i : TILE * i + TILE] = visc * visc * weight
            between = moved(ext, 2 * REACH, lane)
            for at, i in enumerate((0, count)):
                inside = jnp.broadcast_to(between[i][4:5, :], (8, TILE)) != 0.0
                in_ref[at] = jnp.where(inside, 1.0, 0.0)

    masks = {}
    for sign in (1, -1):
        for b in range(BANDS):
            masks[sign, b] = lane < TILE - (REACH + sign * offs[b])
    center = lane < TILE - REACH

    def apply(tiles, step, outs):
        sign = 1 if step % 2 == 0 else -1
        result = [[], [], []]

        def turns_of(i):
            return [
                [turned(tiles[m][i], REACH)]
                + [turned(tiles[m][i], REACH + sign * offs[b]) for b in range(BANDS)]
                for m in range(3)
            ]

        ahead = turns_of(0)
        for i in range(outs):
            here = ahead
            ahead = turns_of(i + 1) if i + 1 < len(tiles[0]) else here
            shifted = [
                [jnp.where(center, here[m][0], ahead[m][0])]
                + [jnp.where(masks[sign, b], here[m][1 + b], ahead[m][1 + b]) for b in range(BANDS)]
                for m in range(3)
            ]
            for k in range(3):
                total = shifted[k][0]
                for b in range(BANDS):
                    for m in range(3):
                        term = 9 * b + (3 * k + m if sign == 1 else 3 * m + k)
                        total = total + tab_ref[step, term, :, TILE * i : TILE * i + TILE] * shifted[m][1 + b]
                if step % 2 == 0:
                    total = total * mid_ref[step // 2, k, :, TILE * i : TILE * i + TILE]
                if step == 1 and i == 0:
                    total = total * in_ref[0]
                if step == 1 and i == count:
                    total = total * in_ref[1]
                result[k].append(total)
        return result

    def group_step(g, carry):
        spot = pl.ds(pl.multiple_of(8 * g, 8), 8)
        tiles = [
            stretch(
                [x_ref[m, spot, TILE * i : TILE * i + TILE] for i in range(count)], ends_ref[m, spot, :], lane
            )
            for m in range(3)
        ]
        for step in range(4):
            tiles = apply(tiles, step, count + 1 if step < 3 else count)
        for m in range(3):
            for i in range(count):
                out_ref[m, spot, TILE * i : TILE * i + TILE] = tiles[m][i]
        return carry

    lax.fori_loop(0, rows // 8, group_step, 0)


def panel_of(probes, coefs, low, high, offsets):
    _, rows, cells = probes.shape
    wide = cells + TILE
    return pl.pallas_call(
        panel_kernel,
        in_specs=[pl.BlockSpec(memory_space=pltpu.SMEM)] + [VMEM] * 4,
        out_specs=VMEM,
        out_shape=jax.ShapeDtypeStruct(probes.shape, jnp.float32),
        scratch_shapes=[
            pltpu.VMEM((4, rows, TILE), jnp.float32),
            pltpu.VMEM((4, TERMS, 8, wide), jnp.float32),
            pltpu.VMEM((2, 3, 8, wide), jnp.float32),
            pltpu.VMEM((2, 8, TILE), jnp.float32),
        ],
        compiler_params=PARAMS,
    )(offsets, probes, coefs, low, high)


def over_lanes(x, j):
    return jnp.broadcast_to(x[:, j : j + 1], (8, TILE))


def over_rows(x, i):
    return jnp.broadcast_to(x[i : i + 1, :], (8, TILE))


def factor_tile(a_ref, e_ref):
    blocks = TILE // 8
    rows = lax.broadcasted_iota(jnp.int32, (8, TILE), 0)
    lanes = lax.broadcasted_iota(jnp.int32, (8, TILE), 1)
    a = [a_ref[8 * t : 8 * t + 8, :] for t in range(blocks)]
    e = [jnp.where(lanes == rows + 8 * t, 1.0, 0.0) for t in range(blocks)]
    below = [rows >= i for i in range(8)]
    for s in range(blocks):
        columns = [over_lanes(a[s], 8 * s + j) for j in range(8)]
        d = {(i, j): over_rows(columns[j], i) for j in range(8) for i in range(j, 8)}
        inv, low = [], {}
        for j in range(8):
            inv.append(lax.rsqrt(d[j, j]))
            for i in range(j + 1, 8):
                low[i, j] = d[i, j] * inv[j]
            for k in range(j + 1, 8):
                for i in range(k, 8):
                    d[i, k] = d[i, k] - low[i, j] * low[k, j]
        w = {}
        for k in range(8):
            w[k, k] = inv[k]
            for i in range(k + 1, 8):
                total = low[i, k] * w[k, k]
                for m in range(k + 1, i):
                    total = total + low[i, m] * w[m, k]
                w[i, k] = -inv[i] * total
        upper = side = None
        for k in range(8):
            mix = jnp.where(below[k], w[k, k], 0.0)
            for i in range(k + 1, 8):
                mix = jnp.where(below[i], w[i, k], mix)
            u, f = mix * over_rows(a[s], k), mix * over_rows(e[s], k)
            upper, side = (u, f) if k == 0 else (upper + u, side + f)
        a[s], e[s] = upper, side
        upper_rows = [over_rows(upper, i) for i in range(8)]
        side_rows = [over_rows(side, i) for i in range(8)]
        for t in range(s + 1, blocks):
            columns = [over_lanes(a[t], 8 * s + j) for j in range(8)]
            for i in range(8):
                factor = w[i, 0] * columns[0]
                for k in range(1, i + 1):
                    factor = factor + w[i, k] * columns[k]
                a[t] = a[t] - factor * upper_rows[i]
                e[t] = e[t] - factor * side_rows[i]
    for t in range(blocks):
        a_ref[8 * t : 8 * t + 8, :] = jnp.where(lanes >= rows + 8 * t, a[t], 0.0)
        e_ref[8 * t : 8 * t + 8, :] = e[t]


def factor_kernel(g_ref, r_ref, x_ref, work, tile_a, tile_e):
    size = g_ref.shape[0]
    dot = functools.partial(jnp.dot, precision=EXACT, preferred_element_type=jnp.float32)

    def outer(left, right):
        return lax.dot_general(
            left, right, (((0,), (0,)), ((), ())), precision=EXACT, preferred_element_type=jnp.float32
        )

    work[...] = g_ref[...]
    rows = lax.broadcasted_iota(jnp.int32, (size, size), 0)
    columns = lax.broadcasted_iota(jnp.int32, (size, size), 1)
    x_ref[...] = jnp.where(rows == columns, 1.0, 0.0)
    lanes = lax.broadcasted_iota(jnp.int32, (TILE, size), 1)

    def block_step(b, carry):
        start = pl.multiple_of(b * TILE, TILE)
        spot = pl.ds(start, TILE)
        tile_a[...] = work[spot, spot]
        factor_tile(tile_a, tile_e)
        inverse = tile_e[...]
        right = jnp.where(lanes >= start + TILE, dot(inverse, work[spot, :]), 0.0)
        side = dot(inverse, x_ref[spot, :])
        r_ref[spot, :] = right
        r_ref[spot, spot] = tile_a[...]
        x_ref[spot, :] = side
        work[...] = work[...] - outer(right, right)
        x_ref[...] = x_ref[...] - outer(right, side)
        return carry

    lax.fori_loop(0, size // TILE, block_step, 0)


def factorize(gram):
    size = gram.shape[0]
    square = jax.ShapeDtypeStruct((size, size), jnp.float32)
    return pl.pallas_call(
        factor_kernel,
        in_specs=[VMEM],
        out_specs=[VMEM, VMEM],
        out_shape=[square, square],
        scratch_shapes=[
            pltpu.VMEM((size, size), jnp.float32),
            pltpu.VMEM((TILE, TILE), jnp.float32),
            pltpu.VMEM((TILE, TILE), jnp.float32),
        ],
        compiler_params=PARAMS,
    )(gram)


def partners(axis, bit):
    return [(i, i ^ bit) for i in range(lax.axis_size(axis))]


def bits_of(axis):
    bits, bit = [], 1
    while bit < lax.axis_size(axis):
        bits.append(bit)
        bit *= 2
    return bits


def scatter_sum(block, axis):
    me = lax.axis_index(axis)
    for bit in bits_of(axis):
        half = block.shape[0] // 2
        upper = (me // bit) % 2
        keep = lax.dynamic_slice_in_dim(block, upper * half, half, 0)
        give = lax.dynamic_slice_in_dim(block, (1 - upper) * half, half, 0)
        block = keep + lax.ppermute(give, axis, partners(axis, bit))
    return block


def gather_back(block, axis, dim):
    me = lax.axis_index(axis)
    for bit in reversed(bits_of(axis)):
        other = lax.ppermute(block, axis, partners(axis, bit))
        upper = (me // bit) % 2 == 1
        block = jnp.concatenate(
            [jnp.where(upper, other, block), jnp.where(upper, block, other)], dim
        )
    return block


def body(probes, viscosity, coupling, misfit_weight, band_offsets):
    _, columns, cells = probes.shape
    slabs, groups = lax.axis_size("slab"), lax.axis_size("probe")
    me = lax.axis_index("probe")
    coefs = jnp.concatenate([coupling.reshape(TERMS, cells), viscosity[None, :], misfit_weight], 0)
    first, last = pack_edges(probes, coefs)
    forward = [(i, i + 1) for i in range(slabs - 1)]
    low = lax.ppermute(last, "slab", forward)
    high = lax.ppermute(first, "slab", [(b, a) for a, b in forward])
    panel = panel_of(probes, coefs, low, high, band_offsets)

    blocks = [panel] + [
        lax.ppermute(panel, "probe", [(i, (i + d) % groups) for i in range(groups)])
        for d in range(1, groups)
    ]
    part = jnp.zeros((groups, columns, columns), jnp.float32)
    for d, block in enumerate(blocks):
        product = jnp.einsum("kpc,kqc->pq", panel, block, precision=CLOSE)
        part = lax.dynamic_update_slice(part, product[None], ((me - d) % groups, 0, 0))
    part = part.transpose(1, 0, 2).reshape(columns, groups * columns) / (3 * cells * slabs)
    share = scatter_sum(part, "slab")
    share = gather_back(share[None], "probe", 0)
    gram = gather_back(share, "slab", 1).reshape(groups * columns, groups * columns)

    upper, inverse = factorize(gram)
    mine = lax.dynamic_slice_in_dim(inverse, me * columns, columns, 0).reshape(columns, groups, columns)
    basis = jnp.zeros_like(panel)
    for d, block in enumerate(blocks):
        mix = lax.dynamic_index_in_dim(mine, (me - d) % groups, 1, keepdims=False)
        basis = basis + jnp.einsum("pq,kqc->kpc", mix, block, precision=CLOSE)
    return basis, lax.dynamic_slice_in_dim(upper, me * columns, columns, 0)


def solution(mesh):
    return jax.shard_map(
        body,
        mesh=mesh,
        in_specs=(
            P(None, "probe", "slab"),
            P("slab"),
            P(None, None, None, "slab"),
            P(None, "slab"),
            P(),
        ),
        out_specs=(P(None, "probe", "slab"), P("probe", None)),
        check_vma=False,
    )
```

time: 2040 us -> 218 us (0.11); the launches traced: 2020 us -> 216 us
  matrix products: 876 us -> 13.7 us
  other arithmetic: 468 us -> 7.27 us
  loops' own time: 355 us -> 0 us
  waiting for transfers between devices: 205 us -> 87.5 us
  Pallas kernels: 0 us -> 56.4 us
  between operations: 28.7 us -> 0.87 us
  local copies, waits for them, and re-layouts: 48.5 us -> 27 us
    dot_general x1152 -> x4, matrix products: 876 us -> 13.7 us  [the longest x2 8.99 us: body(): basis = basis + jnp.einsum('pq,kqc->kpc', mix, block, precision=CLOSE)]
    another operation x16 -> x0, loops' own time: 355 us -> none  [the longest x8 354 us: small_cholesky(): return lax.fori_loop(0, size, column_step, jnp.zeros_like(matrix))]
    reduce_sum x512 -> x0, other arithmetic: 333 us -> none  [row_step(): diag_value = jnp.sum(jnp.where(places == index, row_l, 0.0))]
    all_gather x2 -> x0, waiting for transfers between devices: 110 us -> none  [the longest x1 88.3 us: body(): lax.all_gather(values, 'probe', axis=1, tiled=True)]
    add x1034 -> x3, other arithmetic: 99.1 us -> 2 us  [scatter_sum(): block = keep + lax.ppermute(give, axis, partners(axis, bit))]
    psum x1 -> x0, waiting for transfers between devices: 90.2 us -> none  [body(): gram_part = lax.psum(gram_part, 'slab') / unknowns]
    ppermute x10 -> x12, waiting for transfers between devices: 4.43 us -> 87.5 us  [the longest x1 58 us: body(): lax.ppermute(panel, 'probe', [(i, (i + d) % groups) for i in range(groups)])]
    pallas_call x0 -> x3, Pallas kernels: none -> 56.4 us  [the longest x1 30.5 us: factorize(): pl.pallas_call(factor_kernel, in_specs=[VMEM], out_specs=[VMEM, VMEM], ou...]
where the time goes in v1:
time: 218 us; the launch traced here: 216 us
  waiting for transfers between devices  87.5 us (40%)
  Pallas kernels  56.4 us (26%)
  local copies, waits for them, and re-layouts  27 us (12%)
  starting transfers between devices  23.6 us (11%)
  matrix products  13.7 us (6%)
  other arithmetic  7.27 us (3%)
    ppermute x1, waiting for transfers between devices, body(): lax.ppermute(panel, 'probe', [(i, (i + d) % groups) for i in range(groups)])  58 us
    pallas_call x1, Pallas kernels, factorize(): pl.pallas_call(factor_kernel, in_specs=[VMEM], out_specs=[VMEM, VMEM], ou...  30.5 us
    pallas_call x1, Pallas kernels, panel_of(): pl.pallas_call(panel_kernel, in_specs=[pl.BlockSpec(memory_space=pltpu.SM...  25.7 us
    ppermute x5, waiting for transfers between devices, gather_back(): other = lax.ppermute(block, axis, partners(axis, bit))  15.9 us
    dynamic_update_slice x2, local copies, waits for them, and re-layouts, body(): lax.dynamic_update_slice(part, product[None], ((me - d) % groups, 0, 0))  12.6 us
    ppermute x4, starting transfers between devices, scatter_sum(): block = keep + lax.ppermute(give, axis, partners(axis, bit))  10.8 us
    ppermute x4, waiting for transfers between devices, scatter_sum(): block = keep + lax.ppermute(give, axis, partners(axis, bit))  9.56 us
    dot_general x2, matrix products, body(): basis = basis + jnp.einsum('pq,kqc->kpc', mix, block, precision=CLOSE)  8.99 us
  transfers between devices with their start and end apart: 12, of which 11 were waited for; matrix products, arithmetic and copies ran while one was open for 4% of the time, Pallas kernels for 0%

profile of v1, /device:TPU:0, one launch (start us, length us, event | category | flops | bytes accessed | tf_op | source)
XLA Modules:
  0.0 216.5 jit_solution(8054917076882869208)
XLA Ops:
  4.7 2.4 %collective-permute-start = (f32[64,256]{1,0:T(8,128)S(1)}, f32[64,256]{1,0:T(8,128)S(1)}, u32[]{:S(2)}, u32[]{:S(2)}) collective-permute-start(f32[64,256]{1,0:T(8,128)S(1)} %get-tuple-element.6), channel_id=1, source_target_pairs={{0,1},{1,2},{2,3},{3,4},{4,5},{5,6},{6,7},{7,8},{8,9},{9,10},{10,1... | collective-permute-start | bytes 196616 | tf_op jit(solution)/shard_map/ppermute | solution.py:341
  8.3 4.0 %collective-permute-done.1.high_ref = f32[64,256]{1,0:T(8,128)S(1)} collective-permute-done((f32[64,256]{1,0:T(8,128)S(1)}, f32[64,256]{1,0:T(8,128)S(1)}, u32[]{:S(2)}, u32[]{:S(2)}) %collective-permute-start.1) | collective-permute-done | bytes 65568 | tf_op jit(solution)/shard_map/ppermute | solution.py:342
  12.3 25.7 %shard_map.69 = f32[3,256,1024]{2,1,0:T(8,128)S(1)} custom-call(s32[4]{0:T(128)S(1)} %copy-done.1, f32[3,256,1024]{2,1,0:T(8,128)} %x_ref.1, f32[40,1024]{1,0:T(8,128)S(1)} %pad_maximum_fusion.3.coef_ref, f32[64,256]{1,0:T(8,128)S(1)} %collective-permute-done.low_ref, f32[64,256]{1,0:T(8,128)S(1)} %collective-permute-done.1.high_ref), custom_call_target="tpu_custom_call" | custom-call | tf_op jit(solution)/shard_map/pallas_call | solution.py:178
  42.8 6.3 %dynamic_update_slice.6 = f32[2,256,256]{2,0,1:T(2,128)} dynamic-update-slice(f32[2,256,256]{2,0,1:T(2,128)} %broadcast_in_dim.16, f32[1,256,256]{2,0,1:T(1,128)} %copy.14, s32[]{:T(128)S(6)} %select_n.167, s32[]{:T(128)} %constant.122.clone.1, s32[]{:T(128)} %constant.122.clone.1) | dynamic-update-slice | bytes 524292 | tf_op jit(solution)/shard_map/dynamic_update_slice | solution.py:352
  49.1 58.0 %collective-permute-done.2 = f32[3,256,1024]{2,1,0:T(8,128)} collective-permute-done((f32[3,256,1024]{2,1,0:T(8,128)S(1)}, f32[3,256,1024]{2,1,0:T(8,128)}, u32[]{:S(2)}, u32[]{:S(2)}) %collective-permute-start.2) | collective-permute-done | bytes 3145760 | tf_op jit(solution)/shard_map/ppermute | solution.py:346
  107.1 3.3 %convolution_bitcast_fusion = f32[1,256,256]{1,2,0:T(8,128)S(1)} fusion(f32[3,256,1024]{2,1,0:T(8,128)S(1)} %shard_map.69, f32[3,256,1024]{2,1,0:T(8,128)} %collective-permute-done.2), kind=kOutput, calls=%fused_computation.1 | convolution fusion | flops 1207959552 | bytes 6553600 | tf_op jit(solution)/shard_map/kpc,kqc->pq/dot_general | solution.py:351
  111.3 6.3 %dynamic_update_slice.7 = f32[2,256,256]{2,0,1:T(2,128)} dynamic-update-slice(f32[2,256,256]{2,0,1:T(2,128)} %dynamic_update_slice.6, f32[1,256,256]{2,0,1:T(1,128)} %copy.15, s32[]{:T(128)S(6)} %select_n.169, s32[]{:T(128)} %constant.122.clone.1, s32[]{:T(128)} %constant.122.clone.1) | dynamic-update-slice | bytes 524292 | tf_op jit(solution)/shard_map/dynamic_update_slice | solution.py:352
  124.1 2.9 %collective-permute-start.4 = (f32[64,512]{1,0:T(8,128)S(1)}, f32[64,512]{1,0:T(8,128)}, u32[]{:S(2)}, u32[]{:S(2)}) collective-permute-start(f32[64,512]{1,0:T(8,128)S(1)} %constant_dynamic-slice_fusion.4), channel_id=1, source_target_pairs={{0,2},{1,3},{2,0},{3,1},{4,6},{5,7},{6,4},{7,5},{8,10},{9,11},{10,... | collective-permute-start | bytes 393224 | tf_op jit(solution)/shard_map/ppermute | solution.py:319
  126.9 4.1 %collective-permute-done.4 = f32[64,512]{1,0:T(8,128)} collective-permute-done((f32[64,512]{1,0:T(8,128)S(1)}, f32[64,512]{1,0:T(8,128)}, u32[]{:S(2)}, u32[]{:S(2)}) %collective-permute-start.4) | collective-permute-done | bytes 131104 | tf_op jit(solution)/shard_map/ppermute | solution.py:319
  132.0 2.9 %collective-permute-start.5 = (f32[32,512]{1,0:T(8,128)S(1)}, f32[32,512]{1,0:T(8,128)S(1)}, u32[]{:S(2)}, u32[]{:S(2)}) collective-permute-start(f32[32,512]{1,0:T(8,128)S(1)} %constant_dynamic-slice_fusion.3), channel_id=1, source_target_pairs={{0,4},{1,5},{2,6},{3,7},{4,0},{5,1},{6,2},{7,3},{8,12},{9,13},{10,... | collective-permute-start | bytes 196616 | tf_op jit(solution)/shard_map/ppermute | solution.py:319
  134.9 2.2 %collective-permute-done.5 = f32[32,512]{1,0:T(8,128)S(1)} collective-permute-done((f32[32,512]{1,0:T(8,128)S(1)}, f32[32,512]{1,0:T(8,128)S(1)}, u32[]{:S(2)}, u32[]{:S(2)}) %collective-permute-start.5) | collective-permute-done | bytes 65568 | tf_op jit(solution)/shard_map/ppermute | solution.py:319
  137.2 3.1 %collective-permute-start.6 = (f32[16,512]{1,0:T(8,128)S(1)}, f32[16,512]{1,0:T(8,128)S(1)}, u32[]{:S(2)}, u32[]{:S(2)}) collective-permute-start(f32[16,512]{1,0:T(8,128)S(1)} %constant_dynamic-slice_fusion.2), channel_id=1, source_target_pairs={{0,8},{1,9},{2,10},{3,11},{4,12},{5,13},{6,14},{7,15},{8,0},{9,1},... | collective-permute-start | bytes 98312 | tf_op jit(solution)/shard_map/ppermute | solution.py:319
  143.7 2.4 %collective-permute-done.7 = f32[1,16,512]{2,1,0:T(8,128)S(1)} collective-permute-done((f32[1,16,512]{2,1,0:T(8,128)S(1)}, f32[1,16,512]{2,1,0:T(8,128)S(1)}, u32[]{:S(2)}, u32[]{:S(2)}) %collective-permute-start.7) | collective-permute-done | bytes 32800 | tf_op jit(solution)/shard_map/ppermute | solution.py:326
  146.1 3.0 %collective-permute-start.8 = (f32[2,16,512]{2,1,0:T(8,128)S(1)}, f32[2,16,512]{2,1,0:T(8,128)S(1)}, u32[]{:S(2)}, u32[]{:S(2)}) collective-permute-start(f32[2,16,512]{2,1,0:T(8,128)S(1)} %pad_maximum_fusion.5), channel_id=1, source_target_pairs={{0,8},{1,9},{2,10},{3,11},{4,12},{5,13},{6,14},{7,15},{8,0},{9,1},... | collective-permute-start | bytes 196616 | tf_op jit(solution)/shard_map/ppermute | solution.py:326
  149.1 2.4 %collective-permute-done.8 = f32[2,16,512]{2,1,0:T(8,128)S(1)} collective-permute-done((f32[2,16,512]{2,1,0:T(8,128)S(1)}, f32[2,16,512]{2,1,0:T(8,128)S(1)}, u32[]{:S(2)}, u32[]{:S(2)}) %collective-permute-start.8) | collective-permute-done | bytes 65568 | tf_op jit(solution)/shard_map/ppermute | solution.py:326
  151.5 2.5 %collective-permute-start.9 = (f32[2,32,512]{2,1,0:T(8,128)S(1)}, f32[2,32,512]{2,1,0:T(8,128)S(1)}, u32[]{:S(2)}, u32[]{:S(2)}) collective-permute-start(f32[2,32,512]{2,1,0:T(8,128)S(1)} %pad_maximum_fusion.4), channel_id=1, source_target_pairs={{0,4},{1,5},{2,6},{3,7},{4,0},{5,1},{6,2},{7,3},{8,12},{9,13},{10,... | collective-permute-start | bytes 393224 | tf_op jit(solution)/shard_map/ppermute | solution.py:326
  154.0 2.9 %collective-permute-done.9 = f32[2,32,512]{2,1,0:T(8,128)S(1)} collective-permute-done((f32[2,32,512]{2,1,0:T(8,128)S(1)}, f32[2,32,512]{2,1,0:T(8,128)S(1)}, u32[]{:S(2)}, u32[]{:S(2)}) %collective-permute-start.9) | collective-permute-done | bytes 131104 | tf_op jit(solution)/shard_map/ppermute | solution.py:326
  158.3 6.0 %collective-permute-done.10 = f32[2,64,512]{2,1,0:T(8,128)} collective-permute-done((f32[2,64,512]{2,1,0:T(8,128)S(1)}, f32[2,64,512]{2,1,0:T(8,128)}, u32[]{:S(2)}, u32[]{:S(2)}) %collective-permute-start.10) | collective-permute-done | bytes 262176 | tf_op jit(solution)/shard_map/ppermute | solution.py:326
  166.8 2.2 %collective-permute-done.11 = f32[2,128,512]{2,1,0:T(8,128)} collective-permute-done((f32[2,128,512]{2,1,0:T(8,128)}, f32[2,128,512]{2,1,0:T(8,128)}, u32[]{:S(2)}, u32[]{:S(2)}) %collective-permute-start.11) | collective-permute-done | bytes 524320 | tf_op jit(solution)/shard_map/ppermute | solution.py:326
  170.4 30.5 %shard_map.70 = (f32[512,512]{1,0:T(8,128)S(1)}, f32[512,512]{1,0:T(8,128)S(1)}) custom-call(f32[512,512]{1,0:T(8,128)S(1)} %bitcast.32), custom_call_target="tpu_custom_call" | custom-call | tf_op jit(solution)/shard_map/pallas_call | solution.py:286
  201.9 2.0 copy.16
  203.9 4.7 %fusion = f32[3,1024,256]{2,1,0:T(8,128)S(1)} fusion(f32[3,256,1024]{2,1,0:T(8,128)} %collective-permute-done.2, f32[256,2,256]{0,2,1:T(8,128)} %bitcast.36, s32[]{:T(128)S(6)} %select_n.169), kind=kOutput, calls=%fused_computation.6 | convolution fusion | flops 1207959552 | bytes 6553604 | tf_op jit(solution)/shard_map/pq,kqc->kpc/dot_general | solution.py:363
  208.6 4.3 %add_bitcast_fusion = f32[3,256,1024]{1,2,0:T(8,128)} fusion(f32[3,1024,256]{2,1,0:T(8,128)S(1)} %fusion, f32[3,256,1024]{2,1,0:T(8,128)S(1)} %shard_map.69, f32[256,2,256]{0,2,1:T(8,128)S(1)} %bitcast.37, s32[]{:T(128)S(6)} %select_n.167), kind=kOutput, calls=%fused_computation | convolution fusion | flops 1208745984 | bytes 9699332 | tf_op jit(solution)/shard_map/pq,kqc->kpc/dot_general | solution.py:363
  212.9 3.5 %copy.21 = f32[3,256,1024]{2,1,0:T(8,128)} copy(f32[3,256,1024]{1,2,0:T(8,128)} %add_bitcast_fusion) | data formatting | bytes 6291456
  (50 shorter events, 27.9 us)
Async XLA Ops:
  2.5 1.9 copy-start
  4.4 7.9 %copy-start.1 = (s32[4]{0:T(128)S(1)}, s32[4]{0:T(128)}, u32[]{:S(2)}) copy-start(s32[4]{0:T(128)} %off_ref.1) | copy-start | bytes 52
  4.7 3.7 %collective-permute-start = (f32[64,256]{1,0:T(8,128)S(1)}, f32[64,256]{1,0:T(8,128)S(1)}, u32[]{:S(2)}, u32[]{:S(2)}) collective-permute-start(f32[64,256]{1,0:T(8,128)S(1)} %get-tuple-element.6), channel_id=1, source_target_pairs={{0,1},{1,2},{2,3},{3,4},{4,5},{5,6},{6,7},{7,8},{8,9},{9,10},{10,1... | collective-permute-start | bytes 196616 | tf_op jit(solution)/shard_map/ppermute | solution.py:341
  7.0 5.3 %collective-permute-start.1 = (f32[64,256]{1,0:T(8,128)S(1)}, f32[64,256]{1,0:T(8,128)S(1)}, u32[]{:S(2)}, u32[]{:S(2)}) collective-permute-start(f32[64,256]{1,0:T(8,128)S(1)} %get-tuple-element.7), channel_id=1, source_target_pairs={{1,0},{2,1},{3,2},{4,3},{5,4},{6,5},{7,6},{8,7},{9,8},{10,9},{11,1... | collective-permute-start | bytes 196616 | tf_op jit(solution)/shard_map/ppermute | solution.py:342
  38.0 69.1 %collective-permute-start.2 = (f32[3,256,1024]{2,1,0:T(8,128)S(1)}, f32[3,256,1024]{2,1,0:T(8,128)}, u32[]{:S(2)}, u32[]{:S(2)}) collective-permute-start(f32[3,256,1024]{2,1,0:T(8,128)S(1)} %shard_map.69), channel_id=1, source_target_pairs={{0,16},{16,0},{1,17},{17,1},{2,18},{18,2},{3,19},{19,3},{4,20},{20... | collective-permute-start | bytes 9437192 | tf_op jit(solution)/shard_map/ppermute | solution.py:346
  118.9 0.8 copy-start.3
  119.8 3.2 %collective-permute-start.3 = (f32[128,512]{1,0:T(8,128)S(1)}, f32[128,512]{1,0:T(8,128)}, u32[]{:S(2)}, u32[]{:S(2)}) collective-permute-start(f32[128,512]{1,0:T(8,128)S(1)} %constant_dynamic-slice_fusion.5), channel_id=1, source_target_pairs={{0,1},{1,0},{2,3},{3,2},{4,5},{5,4},{6,7},{7,6},{8,9},{9,8},{10,11... | collective-permute-start | bytes 786440 | tf_op jit(solution)/shard_map/ppermute | solution.py:319
  124.1 7.0 %collective-permute-start.4 = (f32[64,512]{1,0:T(8,128)S(1)}, f32[64,512]{1,0:T(8,128)}, u32[]{:S(2)}, u32[]{:S(2)}) collective-permute-start(f32[64,512]{1,0:T(8,128)S(1)} %constant_dynamic-slice_fusion.4), channel_id=1, source_target_pairs={{0,2},{1,3},{2,0},{3,1},{4,6},{5,7},{6,4},{7,5},{8,10},{9,11},{10,... | collective-permute-start | bytes 393224 | tf_op jit(solution)/shard_map/ppermute | solution.py:319
  132.0 5.1 %collective-permute-start.5 = (f32[32,512]{1,0:T(8,128)S(1)}, f32[32,512]{1,0:T(8,128)S(1)}, u32[]{:S(2)}, u32[]{:S(2)}) collective-permute-start(f32[32,512]{1,0:T(8,128)S(1)} %constant_dynamic-slice_fusion.3), channel_id=1, source_target_pairs={{0,4},{1,5},{2,6},{3,7},{4,0},{5,1},{6,2},{7,3},{8,12},{9,13},{10,... | collective-permute-start | bytes 196616 | tf_op jit(solution)/shard_map/ppermute | solution.py:319
  137.2 5.0 %collective-permute-start.6 = (f32[16,512]{1,0:T(8,128)S(1)}, f32[16,512]{1,0:T(8,128)S(1)}, u32[]{:S(2)}, u32[]{:S(2)}) collective-permute-start(f32[16,512]{1,0:T(8,128)S(1)} %constant_dynamic-slice_fusion.2), channel_id=1, source_target_pairs={{0,8},{1,9},{2,10},{3,11},{4,12},{5,13},{6,14},{7,15},{8,0},{9,1},... | collective-permute-start | bytes 98312 | tf_op jit(solution)/shard_map/ppermute | solution.py:319
  142.2 3.9 %collective-permute-start.7 = (f32[1,16,512]{2,1,0:T(8,128)S(1)}, f32[1,16,512]{2,1,0:T(8,128)S(1)}, u32[]{:S(2)}, u32[]{:S(2)}) collective-permute-start(f32[1,16,512]{2,1,0:T(8,128)S(1)} %add_bitcast_fusion.1), channel_id=1, source_target_pairs={{0,16},{16,0},{1,17},{17,1},{2,18},{18,2},{3,19},{19,3},{4,20},{20... | collective-permute-start | bytes 98312 | tf_op jit(solution)/shard_map/ppermute | solution.py:326
  146.1 5.4 %collective-permute-start.8 = (f32[2,16,512]{2,1,0:T(8,128)S(1)}, f32[2,16,512]{2,1,0:T(8,128)S(1)}, u32[]{:S(2)}, u32[]{:S(2)}) collective-permute-start(f32[2,16,512]{2,1,0:T(8,128)S(1)} %pad_maximum_fusion.5), channel_id=1, source_target_pairs={{0,8},{1,9},{2,10},{3,11},{4,12},{5,13},{6,14},{7,15},{8,0},{9,1},... | collective-permute-start | bytes 196616 | tf_op jit(solution)/shard_map/ppermute | solution.py:326
  151.5 5.5 %collective-permute-start.9 = (f32[2,32,512]{2,1,0:T(8,128)S(1)}, f32[2,32,512]{2,1,0:T(8,128)S(1)}, u32[]{:S(2)}, u32[]{:S(2)}) collective-permute-start(f32[2,32,512]{2,1,0:T(8,128)S(1)} %pad_maximum_fusion.4), channel_id=1, source_target_pairs={{0,4},{1,5},{2,6},{3,7},{4,0},{5,1},{6,2},{7,3},{8,12},{9,13},{10,... | collective-permute-start | bytes 393224 | tf_op jit(solution)/shard_map/ppermute | solution.py:326
  157.0 0.7 copy-start.5
  157.7 6.5 %collective-permute-start.10 = (f32[2,64,512]{2,1,0:T(8,128)S(1)}, f32[2,64,512]{2,1,0:T(8,128)}, u32[]{:S(2)}, u32[]{:S(2)}) collective-permute-start(f32[2,64,512]{2,1,0:T(8,128)S(1)} %pad_maximum_fusion.2), channel_id=1, source_target_pairs={{0,2},{1,3},{2,0},{3,1},{4,6},{5,7},{6,4},{7,5},{8,10},{9,11},{10,... | collective-permute-start | bytes 786440 | tf_op jit(solution)/shard_map/ppermute | solution.py:326
  165.3 0.7 copy-start.2
  166.8 2.3 %collective-permute-start.11 = (f32[2,128,512]{2,1,0:T(8,128)}, f32[2,128,512]{2,1,0:T(8,128)}, u32[]{:S(2)}, u32[]{:S(2)}) collective-permute-start(f32[2,128,512]{2,1,0:T(8,128)} %pad_maximum_fusion.1), channel_id=1, source_target_pairs={{0,1},{1,0},{2,3},{3,2},{4,5},{5,4},{6,7},{7,6},{8,9},{9,8},{10,11... | collective-permute-start | bytes 1572872 | tf_op jit(solution)/shard_map/ppermute | solution.py:326
  203.9 4.7 %copy-start.4 = (f32[256,512]{0,1:T(8,128)S(1)}, f32[256,512]{0,1:T(8,128)}, u32[]{:S(2)}) copy-start(f32[256,512]{0,1:T(8,128)} %copy.16) | copy-start | bytes 1572868

commit v2 on v1

--- a/solution.py
+++ b/solution.py
@@ -19,34 +19,47 @@
 PARAMS = pltpu.CompilerParams(vmem_limit_bytes=48 * 2**20)
 
 
-def pack_kernel(first_ref, last_ref, coef_ref, low_ref, high_ref):
+def pack_kernel(first_ref, before_ref, after_ref, last_ref, coef_ref, low_ref, mid_ref, high_ref):
     rows, cells = first_ref.shape[1], coef_ref.shape[1]
-    for comp in range(3):
-        spot = slice(HALO * comp, HALO * comp + HALO)
-        low_ref[spot, :] = first_ref[comp].T[:HALO]
-        high_ref[spot, :] = last_ref[comp].T[TILE - HALO :]
     blank = jnp.zeros((rows - COEFS, TILE), jnp.float32)
-    spot = slice(3 * HALO, 4 * HALO)
-    low_ref[spot, :] = jnp.concatenate([coef_ref[:, :TILE], blank], 0).T[:HALO]
-    high_ref[spot, :] = jnp.concatenate([coef_ref[:, cells - TILE :], blank], 0).T[TILE - HALO :]
+
+    def pack(out_ref, x_ref, start, spot):
+        for comp in range(3):
+            out_ref[HALO * comp : HALO * comp + HALO, :] = x_ref[comp].T[spot]
+        coef = jnp.concatenate([coef_ref[:, start : start + TILE], blank], 0)
+        out_ref[3 * HALO : 4 * HALO, :] = coef.T[spot]
+
+    head, tail = slice(0, HALO), slice(TILE - HALO, TILE)
+    pack(low_ref, first_ref, 0, head)
+    pack(high_ref, last_ref, cells - TILE, tail)
+    is_first = lax.axis_index("probe") == 0
+
+    @pl.when(is_first)
+    def _():
+        pack(mid_ref, after_ref, cells // 2, head)
+
+    @pl.when(jnp.logical_not(is_first))
+    def _():
+        pack(mid_ref, before_ref, cells // 2 - TILE, tail)
 
 
 def pack_edges(probes, coefs):
     _, rows, cells = probes.shape
     edge = jax.ShapeDtypeStruct((4 * HALO, rows), jnp.float32)
-    last = cells // TILE - 1
+    half = cells // TILE // 2
+
+    def tile(at):
+        return pl.BlockSpec((3, rows, TILE), lambda i: (0, 0, at))
+
     return pl.pallas_call(
         pack_kernel,
         grid=(1,),
-        in_specs=[
-            pl.BlockSpec((3, rows, TILE), lambda i: (0, 0, 0)),
-            pl.BlockSpec((3, rows, TILE), lambda i: (0, 0, last)),
-            pl.BlockSpec((COEFS, cells), lambda i: (0, 0)),
-        ],
-        out_specs=[pl.BlockSpec((4 * HALO, rows), lambda i: (0, 0))] * 2,
-        out_shape=[edge, edge],
+        in_specs=[tile(0), tile(half - 1), tile(half), tile(2 * half - 1)]
+        + [pl.BlockSpec((COEFS, cells), lambda i: (0, 0))],
+        out_specs=[pl.BlockSpec((4 * HALO, rows), lambda i: (0, 0))] * 3,
+        out_shape=[edge] * 3,
         compiler_params=PARAMS,
-    )(probes, probes, coefs)
+    )(probes, probes, probes, probes, coefs)
 
 
 def turned(x, amount):
@@ -69,8 +82,9 @@
     return [jnp.where(lane < HALO, ends, turns[0])] + middle + [jnp.where(lane < HALO, turns[-1], ends)]
 
 
-def panel_kernel(off_ref, x_ref, coef_ref, low_ref, high_ref, out_ref, ends_ref, tab_ref, mid_ref, in_ref):
+def panel_steps(off_ref, x_ref, coef_ref, low_ref, high_ref, out_refs, ends_ref, tab_ref, mid_ref, in_ref):
     _, rows, cells = x_ref.shape
+    share = cells // TILE // len(out_refs)
     count = cells // TILE
     lane = lax.broadcasted_iota(jnp.int32, (8, TILE), 1)
     offs = [off_ref[b] for b in range(BANDS)]
@@ -166,28 +180,118 @@
             tiles = apply(tiles, step, count + 1 if step < 3 else count)
         for m in range(3):
             for i in range(count):
-                out_ref[m, spot, TILE * i : TILE * i + TILE] = tiles[m][i]
+                out_refs[i // share][m, spot, pl.ds(TILE * (i % share), TILE)] = tiles[m][i]
         return carry
 
     lax.fori_loop(0, rows // 8, group_step, 0)
 
 
-def panel_of(probes, coefs, low, high, offsets):
+def panel_scratch(rows, cells):
+    wide = cells + TILE
+    return [
+        pltpu.VMEM((4, rows, TILE), jnp.float32),
+        pltpu.VMEM((4, TERMS, 8, wide), jnp.float32),
+        pltpu.VMEM((2, 3, 8, wide), jnp.float32),
+        pltpu.VMEM((2, 8, TILE), jnp.float32),
+    ]
+
+
+SMEM = pl.BlockSpec(memory_space=pltpu.SMEM)
+
+
+def pieces(x):
+    high = x.astype(jnp.bfloat16)
+    return high, (x - high.astype(jnp.float32)).astype(jnp.bfloat16)
+
+
+def close_dot(left, right, over):
+    dot = functools.partial(lax.dot_general, dimension_numbers=((over, ((), ()))), preferred_element_type=jnp.float32)
+    return dot(left[0], right[0]) + (dot(left[0], right[1]) + dot(left[1], right[0]))
+
+
+ALONG = ((1,), (1,))
+PLAIN = ((1,), (0,))
+
+
+def own_kernel(scale, *refs):
+    *ins, first_ref, second_ref, gram_ref = refs[:8]
+    panel_steps(*ins, (first_ref, second_ref), *refs[8:])
+    total = None
+    for ref in (first_ref, second_ref):
+        for k in range(3):
+            x = pieces(ref[k])
+            part = close_dot(x, x, ALONG)
+            total = part if total is None else total + part
+    gram_ref[...] = total * scale
+
+
+def panel_of(probes, coefs, low, high, offsets, scale):
     _, rows, cells = probes.shape
-    wide = cells + TILE
+    half = jax.ShapeDtypeStruct((3, rows, cells // 2), jnp.float32)
     return pl.pallas_call(
-        panel_kernel,
-        in_specs=[pl.BlockSpec(memory_space=pltpu.SMEM)] + [VMEM] * 4,
-        out_specs=VMEM,
-        out_shape=jax.ShapeDtypeStruct(probes.shape, jnp.float32),
-        scratch_shapes=[
-            pltpu.VMEM((4, rows, TILE), jnp.float32),
-            pltpu.VMEM((4, TERMS, 8, wide), jnp.float32),
-            pltpu.VMEM((2, 3, 8, wide), jnp.float32),
-            pltpu.VMEM((2, 8, TILE), jnp.float32),
-        ],
+        functools.partial(own_kernel, scale),
+        in_specs=[SMEM] + [VMEM] * 4,
+        out_specs=[VMEM] * 3,
+        out_shape=[half, half, jax.ShapeDtypeStruct((rows, rows), jnp.float32)],
+        scratch_shapes=panel_scratch(rows, cells),
         compiler_params=PARAMS,
     )(offsets, probes, coefs, low, high)
+
+
+def reversed_bits(place, count):
+    result, bit = 0, 1
+    while bit < count:
+        result = 2 * result + (place // bit) % 2
+        bit *= 2
+    return result
+
+
+def block_at(place, count):
+    return lax.bitwise_xor(lax.axis_index("slab"), jnp.int32(reversed_bits(place, count)))
+
+
+def cross_kernel(scale, count, *refs):
+    *ins, first_ref, second_ref, gram_ref, other_ref, out_ref = refs[:10]
+    panel_steps(*ins, (other_ref,), *refs[10:-1])
+    work = refs[-1]
+    rows = gram_ref.shape[0]
+    is_first = lax.axis_index("probe") == 0
+
+    def product(left, right):
+        total = None
+        for k in range(3):
+            part = close_dot(pieces(left[k]), pieces(right[k]), ALONG)
+            total = part if total is None else total + part
+        work[...] = total * scale
+
+    @pl.when(is_first)
+    def _():
+        product(second_ref, other_ref)
+
+    @pl.when(jnp.logical_not(is_first))
+    def _():
+        product(other_ref, first_ref)
+
+    share = rows // count
+    for place in range(count):
+        spot = pl.ds(pl.multiple_of(block_at(place, count) * share, share), share)
+        out_ref[share * place : share * place + share, :rows] = gram_ref[spot, :]
+        out_ref[share * place : share * place + share, rows:] = work[spot, :]
+
+
+def cross_of(half, coefs, low, high, offsets, first, second, gram, scale, count):
+    _, rows, cells = half.shape
+    return pl.pallas_call(
+        functools.partial(cross_kernel, scale, count),
+        in_specs=[SMEM] + [VMEM] * 7,
+        out_specs=[VMEM] * 2,
+        out_shape=[
+            jax.ShapeDtypeStruct(half.shape, jnp.float32),
+            jax.ShapeDtypeStruct((rows, 2 * rows), jnp.float32),
+        ],
+        scratch_shapes=panel_scratch(rows, cells) + [pltpu.VMEM((rows, rows), jnp.float32)],
+        compiler_params=PARAMS,
+    )(offsets, half, coefs, low, high, first, second, gram)
 
 
 def over_lanes(x, j):
@@ -247,8 +351,8 @@
         e_ref[8 * t : 8 * t + 8, :] = e[t]
 
 
-def factor_kernel(g_ref, r_ref, x_ref, work, tile_a, tile_e):
-    size = g_ref.shape[0]
+def factor_steps(work, r_ref, x_ref, tile_a, tile_e):
+    size = work.shape[0]
     dot = functools.partial(jnp.dot, precision=EXACT, preferred_element_type=jnp.float32)
 
     def outer(left, right):
@@ -256,7 +360,6 @@
             left, right, (((0,), (0,)), ((), ())), precision=EXACT, preferred_element_type=jnp.float32
         )
 
-    work[...] = g_ref[...]
     rows = lax.broadcasted_iota(jnp.int32, (size, size), 0)
     columns = lax.broadcasted_iota(jnp.int32, (size, size), 1)
     x_ref[...] = jnp.where(rows == columns, 1.0, 0.0)
@@ -280,6 +383,15 @@
     lax.fori_loop(0, size // TILE, block_step, 0)
 
 
+def factor_scratch(size):
+    return [pltpu.VMEM((size, size), jnp.float32)] + [pltpu.VMEM((TILE, TILE), jnp.float32)] * 2
+
+
+def factor_kernel(g_ref, r_ref, x_ref, work, tile_a, tile_e):
+    work[...] = g_ref[...]
+    factor_steps(work, r_ref, x_ref, tile_a, tile_e)
+
+
 def factorize(gram):
     size = gram.shape[0]
     square = jax.ShapeDtypeStruct((size, size), jnp.float32)
@@ -288,13 +400,70 @@
         in_specs=[VMEM],
         out_specs=[VMEM, VMEM],
         out_shape=[square, square],
-        scratch_shapes=[
-            pltpu.VMEM((size, size), jnp.float32),
-            pltpu.VMEM((TILE, TILE), jnp.float32),
-            pltpu.VMEM((TILE, TILE), jnp.float32),
-        ],
+        scratch_shapes=factor_scratch(size),
         compiler_params=PARAMS,
     )(gram)
+
+
+def pair_kernel(count, g_ref, r_ref, own_ref, other_ref, work, tile_a, tile_e, r_all, x_all):
+    rows = r_ref.shape[0]
+    share = rows // count
+    work[rows:, :rows] = jnp.zeros((rows, rows), jnp.float32)
+    for place in range(count):
+        start = pl.multiple_of(block_at(place, count) * share, share)
+        here = slice(share * place, share * place + share)
+        work[pl.ds(start, share), :] = g_ref[here, : 2 * rows]
+        work[pl.ds(rows + start, share), rows:] = g_ref[here, 2 * rows :]
+    factor_steps(work, r_all, x_all, tile_a, tile_e)
+    is_first = lax.axis_index("probe") == 0
+
+    @pl.when(is_first)
+    def _():
+        r_ref[...] = r_all[:rows, :]
+        own_ref[...] = x_all[:rows, :rows]
+        other_ref[...] = jnp.zeros((rows, rows), jnp.float32)
+
+    @pl.when(jnp.logical_not(is_first))
+    def _():
+        r_ref[...] = r_all[rows:, :]
+        own_ref[...] = x_all[rows:, rows:]
+        other_ref[...] = x_all[rows:, :rows]
+
+
+def factorize_pair(travelled, count):
+    rows = travelled.shape[0]
+    square = jax.ShapeDtypeStruct((rows, rows), jnp.float32)
+    return pl.pallas_call(
+        functools.partial(pair_kernel, count),
+        in_specs=[VMEM],
+        out_specs=[VMEM] * 3,
+        out_shape=[jax.ShapeDtypeStruct((rows, 2 * rows), jnp.float32), square, square],
+        scratch_shapes=factor_scratch(2 * rows) + [pltpu.VMEM((2 * rows, 2 * rows), jnp.float32)] * 2,
+        compiler_params=PARAMS,
+    )(travelled)
+
+
+def basis_kernel(own_ref, other_ref, first_ref, second_ref, front_ref, back_ref, out_ref):
+    half = first_ref.shape[2]
+    own, other = pieces(own_ref[...]), pieces(other_ref[...])
+    for at, (mine, theirs) in enumerate(((first_ref, front_ref), (second_ref, back_ref))):
+        out_ref[0, :, half * at : half * at + half] = close_dot(own, pieces(mine[0]), PLAIN) + close_dot(
+            other, pieces(theirs[0]), PLAIN
+        )
+
+
+def basis_of(own, other, first, second, front, back):
+    _, rows, half = first.shape
+    weights = pl.BlockSpec((rows, rows), lambda k: (0, 0))
+    panel = pl.BlockSpec((1, rows, half), lambda k: (k, 0, 0))
+    return pl.pallas_call(
+        basis_kernel,
+        grid=(3,),
+        in_specs=[weights] * 2 + [panel] * 4,
+        out_specs=pl.BlockSpec((1, rows, 2 * half), lambda k: (k, 0, 0)),
+        out_shape=jax.ShapeDtypeStruct((3, rows, 2 * half), jnp.float32),
+        compiler_params=PARAMS,
+    )(own, other, first, second, front, back)
 
 
 def partners(axis, bit):
@@ -310,58 +479,78 @@
 
 
 def scatter_sum(block, axis):
-    me = lax.axis_index(axis)
     for bit in bits_of(axis):
         half = block.shape[0] // 2
-        upper = (me // bit) % 2
-        keep = lax.dynamic_slice_in_dim(block, upper * half, half, 0)
-        give = lax.dynamic_slice_in_dim(block, (1 - upper) * half, half, 0)
-        block = keep + lax.ppermute(give, axis, partners(axis, bit))
+        block = block[:half] + lax.ppermute(block[half:], axis, partners(axis, bit))
     return block
 
 
-def gather_back(block, axis, dim):
-    me = lax.axis_index(axis)
+def gather_back(block, axis):
     for bit in reversed(bits_of(axis)):
-        other = lax.ppermute(block, axis, partners(axis, bit))
-        upper = (me // bit) % 2 == 1
-        block = jnp.concatenate(
-            [jnp.where(upper, other, block), jnp.where(upper, block, other)], dim
-        )
+        block = jnp.concatenate([block, lax.ppermute(block, axis, partners(axis, bit))], 0)
     return block
 
 
-def body(probes, viscosity, coupling, misfit_weight, band_offsets):
+def swapped(block):
+    return lax.ppermute(block, "probe", [(0, 1), (1, 0)])
+
+
+def pair_body(probes, coefs, offsets):
+    _, columns, cells = probes.shape
+    slabs = lax.axis_size("slab")
+    scale = 1.0 / (3 * cells * slabs)
+    is_first = lax.axis_index("probe") == 0
+    half = cells // 2
+    theirs = swapped(jnp.where(is_first, probes[:, :, :half], probes[:, :, half:]))
+    first, mid, last = pack_edges(probes, coefs)
+    forward = [(i, i + 1) for i in range(slabs - 1)]
+    low = lax.ppermute(last, "slab", forward)
+    high = lax.ppermute(first, "slab", [(b, a) for a, b in forward])
+    ends = swapped(jnp.where(is_first, jnp.concatenate([low, mid], 0), jnp.concatenate([mid, high], 0)))
+    front, back, gram = panel_of(probes, coefs, low, high, offsets, scale)
+    their_back = lax.ppermute(back, "probe", [(0, 1)])
+    half_coefs = jnp.where(is_first, coefs[:, half:], coefs[:, :half])
+    their_front, sums = cross_of(
+        theirs, half_coefs, ends[: 4 * HALO], ends[4 * HALO :], offsets, front, back, gram, scale, slabs
+    )
+    share = scatter_sum(sums, "slab")
+    other = swapped(share)
+    share = jnp.concatenate(
+        [
+            jnp.where(is_first, share[:, :columns], other[:, :columns]),
+            share[:, columns:] + other[:, columns:],
+            jnp.where(is_first, other[:, :columns], share[:, :columns]),
+        ],
+        1,
+    )
+    r_rows, own, other = factorize_pair(gather_back(share, "slab"), slabs)
+    return basis_of(own, other, front, back, their_front, their_back), r_rows
+
+
+def whole_body(probes, coefs, offsets):
     _, columns, cells = probes.shape
     slabs, groups = lax.axis_size("slab"), lax.axis_size("probe")
     me = lax.axis_index("probe")
-    coefs = jnp.concatenate([coupling.reshape(TERMS, cells), viscosity[None, :], misfit_weight], 0)
-    first, last = pack_edges(probes, coefs)
+    scale = 1.0 / (3 * cells * slabs)
+    first, _, last = pack_edges(probes, coefs)
     forward = [(i, i + 1) for i in range(slabs - 1)]
     low = lax.ppermute(last, "slab", forward)
     high = lax.ppermute(first, "slab", [(b, a) for a, b in forward])
-    panel = panel_of(probes, coefs, low, high, band_offsets)
-
-    blocks = [panel] + [
-        lax.ppermute(panel, "probe", [(i, (i + d) % groups) for i in range(groups)])
-        for d in range(1, groups)
-    ]
-    part = jnp.zeros((groups, columns, columns), jnp.float32)
-    for d, block in enumerate(blocks):
-        product = jnp.einsum("kpc,kqc->pq", panel, block, precision=CLOSE)
-        part = lax.dynamic_update_slice(part, product[None], ((me - d) % groups, 0, 0))
-    part = part.transpose(1, 0, 2).reshape(columns, groups * columns) / (3 * cells * slabs)
-    share = scatter_sum(part, "slab")
-    share = gather_back(share[None], "probe", 0)
-    gram = gather_back(share, "slab", 1).reshape(groups * columns, groups * columns)
-
+    front, back, _ = panel_of(probes, coefs, low, high, offsets, scale)
+    panel = jnp.concatenate([front, back], 2)
+    everyone = lax.all_gather(panel, "probe", axis=1, tiled=True)
+    part = scale * jnp.einsum("kpc,kqc->pq", panel, everyone, precision=CLOSE)
+    gram = lax.all_gather(lax.psum(part, "slab"), "probe", axis=0, tiled=True)
     upper, inverse = factorize(gram)
-    mine = lax.dynamic_slice_in_dim(inverse, me * columns, columns, 0).reshape(columns, groups, columns)
-    basis = jnp.zeros_like(panel)
-    for d, block in enumerate(blocks):
-        mix = lax.dynamic_index_in_dim(mine, (me - d) % groups, 1, keepdims=False)
-        basis = basis + jnp.einsum("pq,kqc->kpc", mix, block, precision=CLOSE)
+    mine = lax.dynamic_slice_in_dim(inverse, me * columns, columns, 0)
+    basis = jnp.einsum("pq,kqc->kpc", mine, everyone, precision=CLOSE)
     return basis, lax.dynamic_slice_in_dim(upper, me * columns, columns, 0)
+
+
+def body(probes, viscosity, coupling, misfit_weight, band_offsets):
+    coefs = jnp.concatenate([coupling.reshape(TERMS, -1), viscosity[None, :], misfit_weight], 0)
+    run = pair_body if lax.axis_size("probe") == 2 else whole_body
+    return run(probes, coefs, band_offsets)
 
 
 def solution(mesh):

time: 218 us -> 147 us (0.67)
  waiting for transfers between devices: 87.5 us -> 25.6 us
  Pallas kernels: 56.4 us -> 88.6 us
  local copies, waits for them, and re-layouts: 27 us -> 2.63 us
  matrix products: 13.7 us -> 0 us
  other arithmetic: 7.27 us -> 3.71 us
    ppermute x12 -> x14, waiting for transfers between devices: 87.5 us -> 25.6 us  [the longest x4 10.5 us: gather_back(): lax.ppermute(block, axis, partners(axis, bit))]
    pallas_call x3 -> x5, Pallas kernels: 56.4 us -> 88.6 us  [the longest x1 31.2 us: factorize_pair(): pl.pallas_call(functools.partial(pair_kernel, count), in_specs=[VMEM], ou...]
    dot_general x4 -> x0, matrix products: 13.7 us -> none  [the longest x2 8.99 us: body(): basis = basis + jnp.einsum('pq,kqc->kpc', mix, block, precision=CLOSE)]
    dynamic_update_slice x2 -> x0, local copies, waits for them, and re-layouts: 12.6 us -> none  [body(): lax.dynamic_update_slice(part, product[None], ((me - d) % groups, 0, 0))]
    unnamed x15 -> x20, local copies, waits for them, and re-layouts: 8.62 us -> 2.48 us
    dynamic_slice x6 -> x0, local copies, waits for them, and re-layouts: 3.14 us -> none  [the longest x1 2.03 us: body(): lax.dynamic_slice_in_dim(inverse, me * columns, columns, 0)]
    broadcast_in_dim x3 -> x0, local copies, waits for them, and re-layouts: 2.6 us -> none  [the longest x2 1.67 us: body(): product[None]]
    ppermute x12 -> x14, starting transfers between devices: 23.6 us -> 25.3 us  [the longest x4 8 us: scatter_sum(): block = block[:half] + lax.ppermute(block[half:], axis, partners(axis, bit))]
  transfers between devices with their start and end apart: 12 -> 14, of which waited for: 11 -> 10; matrix products, arithmetic and copies ran while one was open for 4% -> 0% of each run, Pallas kernels for 0% -> 40%
where the time goes in v2:
time: 147 us
  Pallas kernels  88.6 us (60%)
  waiting for transfers between devices  25.6 us (17%)
  starting transfers between devices  25.3 us (17%)
  other arithmetic  3.71 us (3%)
  local copies, waits for them, and re-layouts  2.63 us (2%)
    pallas_call x1, Pallas kernels, factorize_pair(): pl.pallas_call(functools.partial(pair_kernel, count), in_specs=[VMEM], ou...  31.2 us
    pallas_call x1, Pallas kernels, panel_of(): pl.pallas_call(functools.partial(own_kernel, scale), in_specs=[SMEM] + [V...  27.1 us
    pallas_call x1, Pallas kernels, cross_of(): pl.pallas_call(functools.partial(cross_kernel, scale, count), in_specs=[S...  24.4 us
    ppermute x4, waiting for transfers between devices, gather_back(): lax.ppermute(block, axis, partners(axis, bit))  10.5 us
    ppermute x4, waiting for transfers between devices, scatter_sum(): block = block[:half] + lax.ppermute(block[half:], axis, partners(axis, bit))  10.1 us
    ppermute x4, starting transfers between devices, scatter_sum(): block = block[:half] + lax.ppermute(block[half:], axis, partners(axis, bit))  8 us
    ppermute x4, starting transfers between devices, gather_back(): lax.ppermute(block, axis, partners(axis, bit))  6.69 us
    pallas_call x1, Pallas kernels, basis_of(): pl.pallas_call(basis_kernel, grid=(3,), in_specs=[weights] * 2 + [panel]...  5.46 us
  transfers between devices with their start and end apart: 14, of which 10 were waited for; matrix products, arithmetic and copies ran while one was open for 0% of the time, Pallas kernels for 40%

profile of v2, /device:TPU:0, one launch (start us, length us, event | category | flops | bytes accessed | tf_op | source)
XLA Modules:
  0.0 146.7 jit_solution(4506986082556288221)
XLA Ops:
  0.7 3.5 %slice_select_fusion = f32[3,256,512]{2,1,0:T(8,128)} fusion(f32[3,256,1024]{2,1,0:T(8,128)} %refs_1_.1, pred[]{:T(512)S(6)} %eq.3), kind=kLoop, calls=%fused_computation | loop fusion | flops 393216 | bytes 4718593 | tf_op jit(solution)/shard_map/jit(_where)/select_n | solution.py:504
  4.2 2.9 %collective-permute-start = (f32[3,256,512]{2,1,0:T(8,128)}, f32[3,256,512]{2,1,0:T(8,128)}, u32[]{:S(2)}, u32[]{:S(2)}) collective-permute-start(f32[3,256,512]{2,1,0:T(8,128)} %slice_select_fusion), channel_id=1, source_target_pairs={{0,16},{16,0},{1,17},{17,1},{2,18},{18,2},{3,19},{19,3},{4,20},{20... | collective-permute-start | bytes 4718600 | tf_op jit(solution)/shard_map/ppermute | solution.py:495
  7.8 1.5 collective-permute-start.1
  10.6 3.4 %collective-permute-done.2.refs_4_ = f32[64,256]{1,0:T(8,128)S(1)} collective-permute-done((f32[64,256]{1,0:T(8,128)S(1)}, f32[64,256]{1,0:T(8,128)S(1)}, u32[]{:S(2)}, u32[]{:S(2)}) %collective-permute-start.2) | collective-permute-done | bytes 65568 | tf_op jit(solution)/shard_map/ppermute | solution.py:508
  14.8 27.1 %shard_map.69 = (f32[3,256,512]{2,1,0:T(8,128)S(1)}, f32[3,256,512]{2,1,0:T(8,128)S(1)}, f32[256,256]{1,0:T(8,128)S(1)}) custom-call(s32[4]{0:T(128)S(1)} %copy-done.3, f32[3,256,1024]{2,1,0:T(8,128)} %refs_1_.1, f32[40,1024]{1,0:T(8,128)S(1)} %pad_maximum_fusion.2.coef_ref.refs_2_, f32[64,256]{1,0:T(8,128)S(1)} %collective-permute-done.1.refs_3_, ...), custom_call_target="tpu_custom_call" | custom-call | tf_op jit(solution)/shard_map/pallas_call | solution.py:231
  43.1 1.5 %collective-permute-done.3 = f32[128,256]{1,0:T(8,128)S(1)} collective-permute-done((f32[128,256]{1,0:T(8,128)S(1)}, f32[128,256]{1,0:T(8,128)S(1)}, u32[]{:S(2)}, u32[]{:S(2)}) %collective-permute-start.3) | collective-permute-done | bytes 131104 | tf_op jit(solution)/shard_map/ppermute | solution.py:495
  44.6 24.4 %shard_map.70 = (f32[3,256,512]{2,1,0:T(8,128)S(1)}, f32[256,512]{1,0:T(8,128)S(1)}) custom-call(s32[4]{0:T(128)S(1)} %copy-done.3, f32[3,256,512]{2,1,0:T(8,128)} %collective-permute-done.refs_1_, f32[40,512]{1,0:T(8,128)S(1)} %slice_select_fusion.1.refs_2_, f32[64,256]{1,0:T(8,128)S(1)} %get-tuple-element.25.refs_3_, ...), custom_call_target="tpu_custom_call" | custom-call | tf_op jit(solution)/shard_map/pallas_call | solution.py:284
  69.0 1.6 %collective-permute-start.4 = (f32[128,512]{1,0:T(8,128)S(1)}, f32[128,512]{1,0:T(8,128)S(1)}, u32[]{:S(2)}, u32[]{:S(2)}) collective-permute-start(f32[128,512]{1,0:T(8,128)S(1)} %slice.63), channel_id=1, source_target_pairs={{0,1},{1,0},{2,3},{3,2},{4,5},{5,4},{6,7},{7,6},{8,9},{9,8},{10,11... | collective-permute-start | bytes 786440 | tf_op jit(solution)/shard_map/ppermute | solution.py:484
  71.9 2.1 %collective-permute-start.5 = (f32[64,512]{1,0:T(8,128)S(1)}, f32[64,512]{1,0:T(8,128)S(1)}, u32[]{:S(2)}, u32[]{:S(2)}) collective-permute-start(f32[64,512]{1,0:T(8,128)S(1)} %slice.79), channel_id=1, source_target_pairs={{0,2},{1,3},{2,0},{3,1},{4,6},{5,7},{6,4},{7,5},{8,10},{9,11},{10,... | collective-permute-start | bytes 393224 | tf_op jit(solution)/shard_map/ppermute | solution.py:484
  74.0 4.0 %collective-permute-done.5 = f32[64,512]{1,0:T(8,128)S(1)} collective-permute-done((f32[64,512]{1,0:T(8,128)S(1)}, f32[64,512]{1,0:T(8,128)S(1)}, u32[]{:S(2)}, u32[]{:S(2)}) %collective-permute-start.5) | collective-permute-done | bytes 131104 | tf_op jit(solution)/shard_map/ppermute | solution.py:484
  78.0 1.6 %collective-permute-start.6 = (f32[32,512]{1,0:T(8,128)S(1)}, f32[32,512]{1,0:T(8,128)S(1)}, u32[]{:S(2)}, u32[]{:S(2)}) collective-permute-start(f32[32,512]{1,0:T(8,128)S(1)} %slice.81), channel_id=1, source_target_pairs={{0,4},{1,5},{2,6},{3,7},{4,0},{5,1},{6,2},{7,3},{8,12},{9,13},{10,... | collective-permute-start | bytes 196616 | tf_op jit(solution)/shard_map/ppermute | solution.py:484
  79.7 2.7 %collective-permute-done.6 = f32[32,512]{1,0:T(8,128)S(1)} collective-permute-done((f32[32,512]{1,0:T(8,128)S(1)}, f32[32,512]{1,0:T(8,128)S(1)}, u32[]{:S(2)}, u32[]{:S(2)}) %collective-permute-start.6) | collective-permute-done | bytes 65568 | tf_op jit(solution)/shard_map/ppermute | solution.py:484
  82.4 2.6 %collective-permute-start.7 = (f32[16,512]{1,0:T(8,128)S(1)}, f32[16,512]{1,0:T(8,128)S(1)}, u32[]{:S(2)}, u32[]{:S(2)}) collective-permute-start(f32[16,512]{1,0:T(8,128)S(1)} %slice.83), channel_id=1, source_target_pairs={{0,8},{1,9},{2,10},{3,11},{4,12},{5,13},{6,14},{7,15},{8,0},{9,1},... | collective-permute-start | bytes 98312 | tf_op jit(solution)/shard_map/ppermute | solution.py:484
  85.0 2.2 %collective-permute-done.7 = f32[16,512]{1,0:T(8,128)S(1)} collective-permute-done((f32[16,512]{1,0:T(8,128)S(1)}, f32[16,512]{1,0:T(8,128)S(1)}, u32[]{:S(2)}, u32[]{:S(2)}) %collective-permute-start.7) | collective-permute-done | bytes 32800 | tf_op jit(solution)/shard_map/ppermute | solution.py:484
  88.7 2.8 %collective-permute-start.13 = (f32[3,256,512]{2,1,0:T(8,128)S(1)}, f32[3,256,512]{2,1,0:T(8,128)S(1)}, u32[]{:S(2)}, u32[]{:S(2)}) collective-permute-start(f32[3,256,512]{2,1,0:T(8,128)S(1)} %copy-done.2), channel_id=1, source_target_pairs={{0,16},{1,17},{2,18},{3,19},{4,20},{5,21},{6,22},{7,23},{8,24},{9,... | collective-permute-start | bytes 4718600 | tf_op jit(solution)/shard_map/ppermute | solution.py:511
  91.5 2.7 %collective-permute-start.9 = (f32[16,768]{1,0:T(8,128)S(1)}, f32[16,768]{1,0:T(8,128)S(1)}, u32[]{:S(2)}, u32[]{:S(2)}) collective-permute-start(f32[16,768]{1,0:T(8,128)S(1)} %get-tuple-element.29), channel_id=1, source_target_pairs={{0,8},{1,9},{2,10},{3,11},{4,12},{5,13},{6,14},{7,15},{8,0},{9,1},... | collective-permute-start | bytes 147464 | tf_op jit(solution)/shard_map/ppermute | solution.py:490
  94.3 2.3 %collective-permute-done.9 = f32[16,768]{1,0:T(8,128)S(1)} collective-permute-done((f32[16,768]{1,0:T(8,128)S(1)}, f32[16,768]{1,0:T(8,128)S(1)}, u32[]{:S(2)}, u32[]{:S(2)}) %collective-permute-start.9) | collective-permute-done | bytes 49184 | tf_op jit(solution)/shard_map/ppermute | solution.py:490
  96.6 2.0 %collective-permute-start.10 = (f32[32,768]{1,0:T(8,128)S(1)}, f32[32,768]{1,0:T(8,128)S(1)}, u32[]{:S(2)}, u32[]{:S(2)}) collective-permute-start(f32[32,768]{1,0:T(8,128)S(1)} %pad_maximum_fusion.3), channel_id=1, source_target_pairs={{0,4},{1,5},{2,6},{3,7},{4,0},{5,1},{6,2},{7,3},{8,12},{9,13},{10,... | collective-permute-start | bytes 294920 | tf_op jit(solution)/shard_map/ppermute | solution.py:490
  98.7 2.6 %collective-permute-done.10 = f32[32,768]{1,0:T(8,128)S(1)} collective-permute-done((f32[32,768]{1,0:T(8,128)S(1)}, f32[32,768]{1,0:T(8,128)S(1)}, u32[]{:S(2)}, u32[]{:S(2)}) %collective-permute-start.10) | collective-permute-done | bytes 98336 | tf_op jit(solution)/shard_map/ppermute | solution.py:490
  101.3 1.8 %collective-permute-start.11 = (f32[64,768]{1,0:T(8,128)S(1)}, f32[64,768]{1,0:T(8,128)S(1)}, u32[]{:S(2)}, u32[]{:S(2)}) collective-permute-start(f32[64,768]{1,0:T(8,128)S(1)} %pad_maximum_fusion.1), channel_id=1, source_target_pairs={{0,2},{1,3},{2,0},{3,1},{4,6},{5,7},{6,4},{7,5},{8,10},{9,11},{10,... | collective-permute-start | bytes 589832 | tf_op jit(solution)/shard_map/ppermute | solution.py:490
  103.2 3.9 %collective-permute-done.11 = f32[64,768]{1,0:T(8,128)S(1)} collective-permute-done((f32[64,768]{1,0:T(8,128)S(1)}, f32[64,768]{1,0:T(8,128)S(1)}, u32[]{:S(2)}, u32[]{:S(2)}) %collective-permute-start.11) | collective-permute-done | bytes 196640 | tf_op jit(solution)/shard_map/ppermute | solution.py:490
  107.2 1.7 %collective-permute-done.12 = f32[128,768]{1,0:T(8,128)S(1)} collective-permute-done((f32[128,768]{1,0:T(8,128)S(1)}, f32[128,768]{1,0:T(8,128)S(1)}, u32[]{:S(2)}, u32[]{:S(2)}) %collective-permute-start.12) | collective-permute-done | bytes 393248 | tf_op jit(solution)/shard_map/ppermute | solution.py:490
  108.9 31.2 %shard_map.71 = (f32[256,512]{1,0:T(8,128)}, f32[256,256]{1,0:T(8,128)S(1)}, f32[256,256]{1,0:T(8,128)S(1)}) custom-call(f32[256,768]{1,0:T(8,128)S(1)} %constant_dynamic-update-slice_fusion.g_ref), custom_call_target="tpu_custom_call" | custom-call | tf_op jit(solution)/shard_map/pallas_call | solution.py:436
  141.3 5.5 %shard_map.72 = f32[3,256,1024]{2,1,0:T(8,128)} custom-call(f32[256,256]{1,0:T(8,128)S(1)} %get-tuple-element.20.own_ref, f32[256,256]{1,0:T(8,128)S(1)} %get-tuple-element.21.other_ref, f32[3,256,512]{2,1,0:T(8,128)S(1)} %get-tuple-element.16.refs_5_.first_ref, f32[3,256,512]{2,1,0:T(8,128)S(1)} %copy-done.2, ...), custom_call_target="tpu_custom_call" | custom-call | tf_op jit(solution)/shard_map/pallas_call | solution.py:459
  (49 shorter events, 7.9 us)
Async XLA Ops:
  0.6 6.5 %copy-start.5 = (f32[4,3,3,1024]{3,0,2,1:T(4,128)S(1)}, f32[4,3,3,1024]{3,0,2,1:T(4,128)}, u32[]{:S(2)}) copy-start(f32[4,3,3,1024]{3,0,2,1:T(4,128)} %param.7) | copy-start | bytes 442372
  0.6 6.7 %copy-start.6 = (f32[3,1024]{1,0:T(4,128)S(1)}, f32[3,1024]{1,0:T(4,128)}, u32[]{:S(2)}) copy-start(f32[3,1024]{1,0:T(4,128)} %param.8) | copy-start | bytes 36868
  0.7 6.7 %copy-start.7 = (f32[1024]{0:T(1024)S(1)}, f32[1024]{0:T(1024)}, u32[]{:S(2)}) copy-start(f32[1024]{0:T(1024)} %param.6) | copy-start | bytes 12292
  0.7 6.7 %copy-start = (f32[3,256,1024]{2,1,0:T(8,128)S(1)}, f32[3,256,1024]{2,1,0:T(8,128)}, u32[]{:S(2)}) copy-start(f32[3,256,1024]{2,1,0:T(8,128)} %refs_1_.1) | copy-start | bytes 9437188
  4.2 40.4 %collective-permute-start = (f32[3,256,512]{2,1,0:T(8,128)}, f32[3,256,512]{2,1,0:T(8,128)}, u32[]{:S(2)}, u32[]{:S(2)}) collective-permute-start(f32[3,256,512]{2,1,0:T(8,128)} %slice_select_fusion), channel_id=1, source_target_pairs={{0,16},{16,0},{1,17},{17,1},{2,18},{18,2},{3,19},{19,3},{4,20},{20... | collective-permute-start | bytes 4718600 | tf_op jit(solution)/shard_map/ppermute | solution.py:495
  7.4 7.4 %copy-start.3 = (s32[4]{0:T(128)S(1)}, s32[4]{0:T(128)}, u32[]{:S(2)}) copy-start(s32[4]{0:T(128)} %refs_0_.3) | copy-start | bytes 52
  7.8 2.8 %collective-permute-start.1 = (f32[64,256]{1,0:T(8,128)S(1)}, f32[64,256]{1,0:T(8,128)S(1)}, u32[]{:S(2)}, u32[]{:S(2)}) collective-permute-start(f32[64,256]{1,0:T(8,128)S(1)} %get-tuple-element.13), channel_id=1, source_target_pairs={{0,1},{1,2},{2,3},{3,4},{4,5},{5,6},{6,7},{7,8},{8,9},{9,10},{10,1... | collective-permute-start | bytes 196616 | tf_op jit(solution)/shard_map/ppermute | solution.py:507
  9.3 4.7 %collective-permute-start.2 = (f32[64,256]{1,0:T(8,128)S(1)}, f32[64,256]{1,0:T(8,128)S(1)}, u32[]{:S(2)}, u32[]{:S(2)}) collective-permute-start(f32[64,256]{1,0:T(8,128)S(1)} %get-tuple-element.15), channel_id=1, source_target_pairs={{1,0},{2,1},{3,2},{4,3},{5,4},{6,5},{7,6},{8,7},{9,8},{10,9},{11,1... | collective-permute-start | bytes 196616 | tf_op jit(solution)/shard_map/ppermute | solution.py:508
  14.1 30.5 %collective-permute-start.3 = (f32[128,256]{1,0:T(8,128)S(1)}, f32[128,256]{1,0:T(8,128)S(1)}, u32[]{:S(2)}, u32[]{:S(2)}) collective-permute-start(f32[128,256]{1,0:T(8,128)S(1)} %maximum_select_fusion), channel_id=1, source_target_pairs={{0,16},{16,0},{1,17},{17,1},{2,18},{18,2},{3,19},{19,3},{4,20},{20... | collective-permute-start | bytes 393224 | tf_op jit(solution)/shard_map/ppermute | solution.py:495
  41.9 1.1 copy-start.1
  69.0 19.7 %copy-start.2 = (f32[3,256,512]{2,1,0:T(8,128)S(1)}, f32[3,256,512]{2,1,0:T(8,128)}, u32[]{:S(2)}) copy-start(f32[3,256,512]{2,1,0:T(8,128)} %copy-done.1) | copy-start | bytes 4718596
  69.0 2.8 %collective-permute-start.4 = (f32[128,512]{1,0:T(8,128)S(1)}, f32[128,512]{1,0:T(8,128)S(1)}, u32[]{:S(2)}, u32[]{:S(2)}) collective-permute-start(f32[128,512]{1,0:T(8,128)S(1)} %slice.63), channel_id=1, source_target_pairs={{0,1},{1,0},{2,3},{3,2},{4,5},{5,4},{6,7},{7,6},{8,9},{9,8},{10,11... | collective-permute-start | bytes 786440 | tf_op jit(solution)/shard_map/ppermute | solution.py:484
  71.9 6.1 %collective-permute-start.5 = (f32[64,512]{1,0:T(8,128)S(1)}, f32[64,512]{1,0:T(8,128)S(1)}, u32[]{:S(2)}, u32[]{:S(2)}) collective-permute-start(f32[64,512]{1,0:T(8,128)S(1)} %slice.79), channel_id=1, source_target_pairs={{0,2},{1,3},{2,0},{3,1},{4,6},{5,7},{6,4},{7,5},{8,10},{9,11},{10,... | collective-permute-start | bytes 393224 | tf_op jit(solution)/shard_map/ppermute | solution.py:484
  78.0 4.3 %collective-permute-start.6 = (f32[32,512]{1,0:T(8,128)S(1)}, f32[32,512]{1,0:T(8,128)S(1)}, u32[]{:S(2)}, u32[]{:S(2)}) collective-permute-start(f32[32,512]{1,0:T(8,128)S(1)} %slice.81), channel_id=1, source_target_pairs={{0,4},{1,5},{2,6},{3,7},{4,0},{5,1},{6,2},{7,3},{8,12},{9,13},{10,... | collective-permute-start | bytes 196616 | tf_op jit(solution)/shard_map/ppermute | solution.py:484
  82.4 4.9 %collective-permute-start.7 = (f32[16,512]{1,0:T(8,128)S(1)}, f32[16,512]{1,0:T(8,128)S(1)}, u32[]{:S(2)}, u32[]{:S(2)}) collective-permute-start(f32[16,512]{1,0:T(8,128)S(1)} %slice.83), channel_id=1, source_target_pairs={{0,8},{1,9},{2,10},{3,11},{4,12},{5,13},{6,14},{7,15},{8,0},{9,1},... | collective-permute-start | bytes 98312 | tf_op jit(solution)/shard_map/ppermute | solution.py:484
  87.3 4.2 %collective-permute-start.8 = (f32[16,512]{1,0:T(8,128)S(1)}, f32[16,512]{1,0:T(8,128)S(1)}, u32[]{:S(2)}, u32[]{:S(2)}) collective-permute-start(f32[16,512]{1,0:T(8,128)S(1)} %slice_add_fusion.3), channel_id=1, source_target_pairs={{0,16},{16,0},{1,17},{17,1},{2,18},{18,2},{3,19},{19,3},{4,20},{20... | collective-permute-start | bytes 98312 | tf_op jit(solution)/shard_map/ppermute | solution.py:495
  88.7 51.4 %collective-permute-start.13 = (f32[3,256,512]{2,1,0:T(8,128)S(1)}, f32[3,256,512]{2,1,0:T(8,128)S(1)}, u32[]{:S(2)}, u32[]{:S(2)}) collective-permute-start(f32[3,256,512]{2,1,0:T(8,128)S(1)} %copy-done.2), channel_id=1, source_target_pairs={{0,16},{1,17},{2,18},{3,19},{4,20},{5,21},{6,22},{7,23},{8,24},{9,... | collective-permute-start | bytes 4718600 | tf_op jit(solution)/shard_map/ppermute | solution.py:511
  91.5 5.1 %collective-permute-start.9 = (f32[16,768]{1,0:T(8,128)S(1)}, f32[16,768]{1,0:T(8,128)S(1)}, u32[]{:S(2)}, u32[]{:S(2)}) collective-permute-start(f32[16,768]{1,0:T(8,128)S(1)} %get-tuple-element.29), channel_id=1, source_target_pairs={{0,8},{1,9},{2,10},{3,11},{4,12},{5,13},{6,14},{7,15},{8,0},{9,1},... | collective-permute-start | bytes 147464 | tf_op jit(solution)/shard_map/ppermute | solution.py:490
  96.6 4.7 %collective-permute-start.10 = (f32[32,768]{1,0:T(8,128)S(1)}, f32[32,768]{1,0:T(8,128)S(1)}, u32[]{:S(2)}, u32[]{:S(2)}) collective-permute-start(f32[32,768]{1,0:T(8,128)S(1)} %pad_maximum_fusion.3), channel_id=1, source_target_pairs={{0,4},{1,5},{2,6},{3,7},{4,0},{5,1},{6,2},{7,3},{8,12},{9,13},{10,... | collective-permute-start | bytes 294920 | tf_op jit(solution)/shard_map/ppermute | solution.py:490
  101.3 5.7 %collective-permute-start.11 = (f32[64,768]{1,0:T(8,128)S(1)}, f32[64,768]{1,0:T(8,128)S(1)}, u32[]{:S(2)}, u32[]{:S(2)}) collective-permute-start(f32[64,768]{1,0:T(8,128)S(1)} %pad_maximum_fusion.1), channel_id=1, source_target_pairs={{0,2},{1,3},{2,0},{3,1},{4,6},{5,7},{6,4},{7,5},{8,10},{9,11},{10,... | collective-permute-start | bytes 589832 | tf_op jit(solution)/shard_map/ppermute | solution.py:490
  107.1 1.8 %collective-permute-start.12 = (f32[128,768]{1,0:T(8,128)S(1)}, f32[128,768]{1,0:T(8,128)S(1)}, u32[]{:S(2)}, u32[]{:S(2)}) collective-permute-start(f32[128,768]{1,0:T(8,128)S(1)} %pad_maximum_fusion), channel_id=1, source_target_pairs={{0,1},{1,0},{2,3},{3,2},{4,5},{5,4},{6,7},{7,6},{8,9},{9,8},{10,11... | collective-permute-start | bytes 1179656 | tf_op jit(solution)/shard_map/ppermute | solution.py:490
  140.1 1.2 copy-start.4

commit v3 on v2

--- a/solution.py
+++ b/solution.py
@@ -13,6 +13,8 @@
 TERMS = 9 * BANDS
 COEFS = TERMS + 4
 TILE = 128
+EARLY = 1
+AT_ONCE = 4
 EXACT = lax.Precision.HIGHEST
 CLOSE = lax.Precision.HIGH
 VMEM = pl.BlockSpec(memory_space=pltpu.VMEM)
@@ -135,55 +137,75 @@
 
     def apply(tiles, step, outs):
         sign = 1 if step % 2 == 0 else -1
-        result = [[], [], []]
+        result = [[[], [], []] for _ in range(AT_ONCE)]
 
         def turns_of(i):
             return [
-                [turned(tiles[m][i], REACH)]
-                + [turned(tiles[m][i], REACH + sign * offs[b]) for b in range(BANDS)]
-                for m in range(3)
+                [
+                    [turned(row[i], REACH)] + [turned(row[i], REACH + sign * offs[b]) for b in range(BANDS)]
+                    for row in tiles[at]
+                ]
+                for at in range(AT_ONCE)
             ]
 
         ahead = turns_of(0)
         for i in range(outs):
             here = ahead
-            ahead = turns_of(i + 1) if i + 1 < len(tiles[0]) else here
+            ahead = turns_of(i + 1) if i + 1 < len(tiles[0][0]) else here
+            spot = slice(TILE * i, TILE * i + TILE)
             shifted = [
-                [jnp.where(center, here[m][0], ahead[m][0])]
-                + [jnp.where(masks[sign, b], here[m][1 + b], ahead[m][1 + b]) for b in range(BANDS)]
-                for m in range(3)
+                [
+                    [jnp.where(center, here[at][m][0], ahead[at][m][0])]
+                    + [
+                        jnp.where(masks[sign, b], here[at][m][1 + b], ahead[at][m][1 + b])
+                        for b in range(BANDS)
+                    ]
+                    for m in range(3)
+                ]
+                for at in range(AT_ONCE)
             ]
-            for k in range(3):
-                total = shifted[k][0]
+
+            def sums(k):
+                total = [shifted[at][k][0] for at in range(AT_ONCE)]
                 for b in range(BANDS):
                     for m in range(3):
                         term = 9 * b + (3 * k + m if sign == 1 else 3 * m + k)
-                        total = total + tab_ref[step, term, :, TILE * i : TILE * i + TILE] * shifted[m][1 + b]
+                        table = tab_ref[step, term, :, spot]
+                        total = [total[at] + table * shifted[at][m][1 + b] for at in range(AT_ONCE)]
+                return total
+
+            for k in range(3):
+                total = sums(k)
                 if step % 2 == 0:
-                    total = total * mid_ref[step // 2, k, :, TILE * i : TILE * i + TILE]
-                if step == 1 and i == 0:
-                    total = total * in_ref[0]
-                if step == 1 and i == count:
-                    total = total * in_ref[1]
-                result[k].append(total)
+                    middle = mid_ref[step // 2, k, :, spot]
+                    total = [x * middle for x in total]
+                if step == 1 and i in (0, count):
+                    inside = in_ref[0 if i == 0 else 1]
+                    total = [x * inside for x in total]
+                for at in range(AT_ONCE):
+                    result[at][k].append(total[at])
         return result
 
     def group_step(g, carry):
-        spot = pl.ds(pl.multiple_of(8 * g, 8), 8)
+        spots = [pl.ds(pl.multiple_of(8 * (AT_ONCE * g + at), 8), 8) for at in range(AT_ONCE)]
         tiles = [
-            stretch(
-                [x_ref[m, spot, TILE * i : TILE * i + TILE] for i in range(count)], ends_ref[m, spot, :], lane
-            )
-            for m in range(3)
+            [
+                stretch(
+                    [x_ref[m, spot, TILE * i : TILE * i + TILE] for i in range(count)], ends_ref[m, spot, :], lane
+                )
+                for m in range(3)
+            ]
+            for spot in spots
         ]
         for step in range(4):
             tiles = apply(tiles, step, count + 1 if step < 3 else count)
-        for m in range(3):
-            for i in range(count):
-                out_refs[i // share][m, spot, pl.ds(TILE * (i % share), TILE)] = tiles[m][i]
+        for at, spot in enumerate(spots):
+            for m in range(3):
+                for i in range(count):
+                    out_refs[i // share][m, spot, pl.ds(TILE * (i % share), TILE)] = tiles[at][m][i]
         return carry
 
-    lax.fori_loop(0, rows // 8, group_step, 0)
+    lax.fori_loop(0, rows // (8 * AT_ONCE), group_step, 0)
 
 
 def panel_scratch(rows, cells):
@@ -211,6 +233,7 @@
 
 ALONG = ((1,), (1,))
 PLAIN = ((1,), (0,))
+ACROSS = ((0,), (0,))
 
 
 def own_kernel(scale, *refs):
@@ -308,79 +331,77 @@
     lanes = lax.broadcasted_iota(jnp.int32, (8, TILE), 1)
     a = [a_ref[8 * t : 8 * t + 8, :] for t in range(blocks)]
     e = [jnp.where(lanes == rows + 8 * t, 1.0, 0.0) for t in range(blocks)]
-    below = [rows >= i for i in range(8)]
+
+    def repeated(t, s):
+        return [over_lanes(a[t], 8 * s + j) for j in range(8)]
+
+    ready = {}
     for s in range(blocks):
-        columns = [over_lanes(a[s], 8 * s + j) for j in range(8)]
-        d = {(i, j): over_rows(columns[j], i) for j in range(8) for i in range(j, 8)}
-        inv, low = [], {}
-        for j in range(8):
-            inv.append(lax.rsqrt(d[j, j]))
-            for i in range(j + 1, 8):
-                low[i, j] = d[i, j] * inv[j]
-            for k in range(j + 1, 8):
-                for i in range(k, 8):
-                    d[i, k] = d[i, k] - low[i, j] * low[k, j]
-        w = {}
+        columns = {t: ready[t] if t in ready else repeated(t, s) for t in range(s, blocks)}
+        early = range(s + 1, min(s + 1 + EARLY, blocks))
+        ready = {t: repeated(t, s + 1) for t in early}
+        upper = [over_rows(a[s], k) for k in range(8)]
+        side = [over_rows(e[s], k) for k in range(8)]
         for k in range(8):
-            w[k, k] = inv[k]
-            for i in range(k + 1, 8):
-                total = low[i, k] * w[k, k]
-                for m in range(k + 1, i):
-                    total = total + low[i, m] * w[m, k]
-                w[i, k] = -inv[i] * total
-        upper = side = None
-        for k in range(8):
-            mix = jnp.where(below[k], w[k, k], 0.0)
-            for i in range(k + 1, 8):
-                mix = jnp.where(below[i], w[i, k], mix)
-            u, f = mix * over_rows(a[s], k), mix * over_rows(e[s], k)
-            upper, side = (u, f) if k == 0 else (upper + u, side + f)
-        a[s], e[s] = upper, side
-        upper_rows = [over_rows(upper, i) for i in range(8)]
-        side_rows = [over_rows(side, i) for i in range(8)]
+            pivot = lax.rsqrt(over_rows(columns[s][k], k))
+            for t in range(s, blocks):
+                columns[t][k] = columns[t][k] * pivot
+            upper[k] = upper[k] * pivot
+            side[k] = side[k] * pivot
+            for m in range(k + 1, 8):
+                factor = over_rows(columns[s][k], m)
+                for t in range(s, blocks):
+                    columns[t][m] = columns[t][m] - columns[t][k] * factor
+                upper[m] = upper[m] - upper[k] * factor
+                side[m] = side[m] - side[k] * factor
+            if s + 1 < blocks:
+                for j in range(8):
+                    factor = over_rows(columns[s + 1][k], j)
+                    for t in early:
+                        ready[t][j] = ready[t][j] - columns[t][k] * factor
         for t in range(s + 1, blocks):
-            columns = [over_lanes(a[t], 8 * s + j) for j in range(8)]
-            for i in range(8):
-                factor = w[i, 0] * columns[0]
-                for k in range(1, i + 1):
-                    factor = factor + w[i, k] * columns[k]
-                a[t] = a[t] - factor * upper_rows[i]
-                e[t] = e[t] - factor * side_rows[i]
-    for t in range(blocks):
-        a_ref[8 * t : 8 * t + 8, :] = jnp.where(lanes >= rows + 8 * t, a[t], 0.0)
-        e_ref[8 * t : 8 * t + 8, :] = e[t]
+            for k in range(8):
+                a[t] = a[t] - columns[t][k] * upper[k]
+                e[t] = e[t] - columns[t][k] * side[k]
+        for k in range(1, 8):
+            upper[0] = jnp.where(rows >= k, upper[k], upper[0])
+            side[0] = jnp.where(rows >= k, side[k], side[0])
+        a_ref[8 * s : 8 * s + 8, :] = jnp.where(lanes >= rows + 8 * s, upper[0], 0.0)
+        e_ref[8 * s : 8 * s + 8, :] = side[0]
 
 
 def factor_steps(work, r_ref, x_ref, tile_a, tile_e):
     size = work.shape[0]
-    dot = functools.partial(jnp.dot, precision=EXACT, preferred_element_type=jnp.float32)
-
-    def outer(left, right):
-        return lax.dot_general(
-            left, right, (((0,), (0,)), ((), ())), precision=EXACT, preferred_element_type=jnp.float32
-        )
-
-    rows = lax.broadcasted_iota(jnp.int32, (size, size), 0)
-    columns = lax.broadcasted_iota(jnp.int32, (size, size), 1)
-    x_ref[...] = jnp.where(rows == columns, 1.0, 0.0)
-    lanes = lax.broadcasted_iota(jnp.int32, (TILE, size), 1)
+    blocks = size // TILE
+    r_ref[...] = jnp.zeros((size, size), jnp.float32)
+    x_ref[...] = jnp.zeros((size, size), jnp.float32)
 
     def block_step(b, carry):
-        start = pl.multiple_of(b * TILE, TILE)
-        spot = pl.ds(start, TILE)
+        spot = pl.ds(pl.multiple_of(b * TILE, TILE), TILE)
         tile_a[...] = work[spot, spot]
         factor_tile(tile_a, tile_e)
-        inverse = tile_e[...]
-        right = jnp.where(lanes >= start + TILE, dot(inverse, work[spot, :]), 0.0)
-        side = dot(inverse, x_ref[spot, :])
-        r_ref[spot, :] = right
         r_ref[spot, spot] = tile_a[...]
-        x_ref[spot, :] = side
-        work[...] = work[...] - outer(right, right)
-        x_ref[...] = x_ref[...] - outer(right, side)
+        x_ref[spot, spot] = tile_e[...]
+        for at in range(blocks):
+            here, rest = slice(TILE * at, TILE * at + TILE), slice(TILE * at + TILE, size)
+
+            @pl.when(b == at)
+            def _():
+                inverse = pieces(tile_e[...])
+                if at > 0:
+                    done = slice(0, TILE * at)
+                    x_ref[here, done] = close_dot(inverse, pieces(x_ref[here, done]), PLAIN)
+                if at < blocks - 1:
+                    right = close_dot(inverse, pieces(work[here, rest]), PLAIN)
+                    r_ref[here, rest] = right
+                    right = pieces(right)
+                    work[rest, rest] = work[rest, rest] - close_dot(right, right, ACROSS)
+                    done = slice(0, TILE * at + TILE)
+                    x_ref[rest, done] = x_ref[rest, done] - close_dot(right, pieces(x_ref[here, done]), ACROSS)
+
         return carry
 
-    lax.fori_loop(0, size // TILE, block_step, 0)
+    lax.fori_loop(0, blocks, block_step, 0)
 
 
 def factor_scratch(size):
@@ -501,7 +522,8 @@
     scale = 1.0 / (3 * cells * slabs)
     is_first = lax.axis_index("probe") == 0
     half = cells // 2
-    theirs = swapped(jnp.where(is_first, probes[:, :, :half], probes[:, :, half:]))
+    start = lax.axis_index("probe") * half
+    theirs = swapped(lax.dynamic_slice_in_dim(probes, start, half, 2))
     first, mid, last = pack_edges(probes, coefs)
     forward = [(i, i + 1) for i in range(slabs - 1)]
     low = lax.ppermute(last, "slab", forward)

time: 147 us -> 119 us (0.81)
  Pallas kernels: 88.6 us -> 60.4 us
  local copies, waits for them, and re-layouts: 2.63 us -> 6.37 us
  other arithmetic: 3.71 us -> 0.18 us
    pallas_call x1, Pallas kernels: 31.2 us -> 14.9 us  [factorize_pair(): pl.pallas_call(functools.partial(pair_kernel, count), in_specs=[VMEM], ou...]
    pallas_call x1, Pallas kernels: 24.4 us -> 15 us  [cross_of(): pl.pallas_call(functools.partial(cross_kernel, scale, count), in_specs=[S...]
    select_n x1 -> x0, other arithmetic: 3.53 us -> none  [pair_body(): jnp.where(is_first, probes[:, :, :half], probes[:, :, half:])]
    dynamic_slice x0 -> x1, local copies, waits for them, and re-layouts: none -> 2.83 us  [pair_body(): theirs = swapped(lax.dynamic_slice_in_dim(probes, start, half, 2))]
    pallas_call x1, Pallas kernels: 27.1 us -> 24.6 us  [panel_of(): pl.pallas_call(functools.partial(own_kernel, scale), in_specs=[SMEM] + [V...]
    ppermute x3, waiting for transfers between devices: 1.51 us -> 3.15 us  [swapped(): return lax.ppermute(block, 'probe', [(0, 1), (1, 0)])]
    unnamed x20 -> x18, local copies, waits for them, and re-layouts: 2.48 us -> 3.39 us
  transfers between devices with their start and end apart: 14 -> 14, of which waited for: 10 -> 10; matrix products, arithmetic and copies ran while one was open for 0% -> 1% of each run, Pallas kernels for 40% -> 34%
where the time goes in v3:
time: 119 us
  Pallas kernels  60.4 us (51%)
  waiting for transfers between devices  27 us (23%)
  starting transfers between devices  24.1 us (20%)
  local copies, waits for them, and re-layouts  6.37 us (5%)
    pallas_call x1, Pallas kernels, panel_of(): pl.pallas_call(functools.partial(own_kernel, scale), in_specs=[SMEM] + [V...  24.6 us
    pallas_call x1, Pallas kernels, cross_of(): pl.pallas_call(functools.partial(cross_kernel, scale, count), in_specs=[S...  15 us
    pallas_call x1, Pallas kernels, factorize_pair(): pl.pallas_call(functools.partial(pair_kernel, count), in_specs=[VMEM], ou...  14.9 us
    ppermute x4, waiting for transfers between devices, gather_back(): lax.ppermute(block, axis, partners(axis, bit))  10.6 us
    ppermute x4, waiting for transfers between devices, scatter_sum(): block = block[:half] + lax.ppermute(block[half:], axis, partners(axis, bit))  9.86 us
    ppermute x4, starting transfers between devices, gather_back(): lax.ppermute(block, axis, partners(axis, bit))  6.92 us
    ppermute x4, starting transfers between devices, scatter_sum(): block = block[:half] + lax.ppermute(block[half:], axis, partners(axis, bit))  6.6 us
    pallas_call x1, Pallas kernels, basis_of(): pl.pallas_call(basis_kernel, grid=(3,), in_specs=[weights] * 2 + [panel]...  5.46 us
  transfers between devices with their start and end apart: 14, of which 10 were waited for; matrix products, arithmetic and copies ran while one was open for 1% of the time, Pallas kernels for 34%

profile of v3, /device:TPU:0, one launch (start us, length us, event | category | flops | bytes accessed | tf_op | source)
XLA Modules:
  0.0 119.0 jit_solution(9280616183016028246)
XLA Ops:
  0.7 2.8 %constant_dynamic-slice_fusion = f32[3,256,512]{2,1,0:T(8,128)} fusion(f32[3,256,1024]{2,1,0:T(8,128)} %refs_1_.1, s32[]{:T(128)S(6)} %select_n.32), kind=kLoop, calls=%fused_computation.19 | loop fusion | bytes 3145732 | tf_op jit(solution)/shard_map/dynamic_slice | solution.py:526
  3.5 2.9 %collective-permute-start = (f32[3,256,512]{2,1,0:T(8,128)}, f32[3,256,512]{2,1,0:T(8,128)}, u32[]{:S(2)}, u32[]{:S(2)}) collective-permute-start(f32[3,256,512]{2,1,0:T(8,128)} %constant_dynamic-slice_fusion), channel_id=1, source_target_pairs={{0,16},{16,0},{1,17},{17,1},{2,18},{18,2},{3,19},{19,3},{4,20},{20... | collective-permute-start | bytes 4718600 | tf_op jit(solution)/shard_map/ppermute | solution.py:516
  10.8 3.4 %collective-permute-done.2.refs_4_ = f32[64,256]{1,0:T(8,128)S(1)} collective-permute-done((f32[64,256]{1,0:T(8,128)S(1)}, f32[64,256]{1,0:T(8,128)S(1)}, u32[]{:S(2)}, u32[]{:S(2)}) %collective-permute-start.2) | collective-permute-done | bytes 65568 | tf_op jit(solution)/shard_map/ppermute | solution.py:530
  15.0 24.6 %shard_map.69 = (f32[3,256,512]{2,1,0:T(8,128)S(1)}, f32[3,256,512]{2,1,0:T(8,128)S(1)}, f32[256,256]{1,0:T(8,128)S(1)}) custom-call(s32[4]{0:T(128)S(1)} %copy-done.3, f32[3,256,1024]{2,1,0:T(8,128)} %refs_1_.1, f32[40,1024]{1,0:T(8,128)S(1)} %pad_maximum_fusion.2.coef_ref.refs_2_, f32[64,256]{1,0:T(8,128)S(1)} %collective-permute-done.1.refs_3_, ...), custom_call_target="tpu_custom_call" | custom-call | tf_op jit(solution)/shard_map/pallas_call | solution.py:254
  40.7 3.1 %collective-permute-done.3 = f32[128,256]{1,0:T(8,128)S(1)} collective-permute-done((f32[128,256]{1,0:T(8,128)S(1)}, f32[128,256]{1,0:T(8,128)S(1)}, u32[]{:S(2)}, u32[]{:S(2)}) %collective-permute-start.3) | collective-permute-done | bytes 131104 | tf_op jit(solution)/shard_map/ppermute | solution.py:516
  43.9 15.0 %shard_map.70 = (f32[3,256,512]{2,1,0:T(8,128)S(1)}, f32[256,512]{1,0:T(8,128)S(1)}) custom-call(s32[4]{0:T(128)S(1)} %copy-done.3, f32[3,256,512]{2,1,0:T(8,128)} %collective-permute-done.refs_1_, f32[40,512]{1,0:T(8,128)S(1)} %slice_select_fusion.refs_2_, f32[64,256]{1,0:T(8,128)S(1)} %get-tuple-element.25.refs_3_, ...), custom_call_target="tpu_custom_call" | custom-call | tf_op jit(solution)/shard_map/pallas_call | solution.py:307
  59.0 1.5 %collective-permute-done.4 = f32[128,512]{1,0:T(8,128)S(1)} collective-permute-done((f32[128,512]{1,0:T(8,128)S(1)}, f32[128,512]{1,0:T(8,128)S(1)}, u32[]{:S(2)}, u32[]{:S(2)}) %collective-permute-start.4) | collective-permute-done | bytes 262176 | tf_op jit(solution)/shard_map/ppermute | solution.py:505
  60.6 1.8 %collective-permute-start.5 = (f32[64,512]{1,0:T(8,128)S(1)}, f32[64,512]{1,0:T(8,128)S(1)}, u32[]{:S(2)}, u32[]{:S(2)}) collective-permute-start(f32[64,512]{1,0:T(8,128)S(1)} %slice.71), channel_id=1, source_target_pairs={{0,2},{1,3},{2,0},{3,1},{4,6},{5,7},{6,4},{7,5},{8,10},{9,11},{10,... | collective-permute-start | bytes 393224 | tf_op jit(solution)/shard_map/ppermute | solution.py:505
  62.4 3.8 %collective-permute-done.5 = f32[64,512]{1,0:T(8,128)S(1)} collective-permute-done((f32[64,512]{1,0:T(8,128)S(1)}, f32[64,512]{1,0:T(8,128)S(1)}, u32[]{:S(2)}, u32[]{:S(2)}) %collective-permute-start.5) | collective-permute-done | bytes 131104 | tf_op jit(solution)/shard_map/ppermute | solution.py:505
  66.3 1.8 %collective-permute-start.6 = (f32[32,512]{1,0:T(8,128)S(1)}, f32[32,512]{1,0:T(8,128)S(1)}, u32[]{:S(2)}, u32[]{:S(2)}) collective-permute-start(f32[32,512]{1,0:T(8,128)S(1)} %slice.73), channel_id=1, source_target_pairs={{0,4},{1,5},{2,6},{3,7},{4,0},{5,1},{6,2},{7,3},{8,12},{9,13},{10,... | collective-permute-start | bytes 196616 | tf_op jit(solution)/shard_map/ppermute | solution.py:505
  68.1 2.5 %collective-permute-done.6 = f32[32,512]{1,0:T(8,128)S(1)} collective-permute-done((f32[32,512]{1,0:T(8,128)S(1)}, f32[32,512]{1,0:T(8,128)S(1)}, u32[]{:S(2)}, u32[]{:S(2)}) %collective-permute-start.6) | collective-permute-done | bytes 65568 | tf_op jit(solution)/shard_map/ppermute | solution.py:505
  70.6 2.9 %collective-permute-start.7 = (f32[16,512]{1,0:T(8,128)S(1)}, f32[16,512]{1,0:T(8,128)S(1)}, u32[]{:S(2)}, u32[]{:S(2)}) collective-permute-start(f32[16,512]{1,0:T(8,128)S(1)} %slice.75), channel_id=1, source_target_pairs={{0,8},{1,9},{2,10},{3,11},{4,12},{5,13},{6,14},{7,15},{8,0},{9,1},... | collective-permute-start | bytes 98312 | tf_op jit(solution)/shard_map/ppermute | solution.py:505
  73.5 2.0 %collective-permute-done.7 = f32[16,512]{1,0:T(8,128)S(1)} collective-permute-done((f32[16,512]{1,0:T(8,128)S(1)}, f32[16,512]{1,0:T(8,128)S(1)}, u32[]{:S(2)}, u32[]{:S(2)}) %collective-permute-start.7) | collective-permute-done | bytes 32800 | tf_op jit(solution)/shard_map/ppermute | solution.py:505
  75.5 1.7 %collective-permute-start.8 = (f32[16,512]{1,0:T(8,128)S(1)}, f32[16,512]{1,0:T(8,128)S(1)}, u32[]{:S(2)}, u32[]{:S(2)}) collective-permute-start(f32[16,512]{1,0:T(8,128)S(1)} %slice_add_fusion.3), channel_id=1, source_target_pairs={{0,16},{16,0},{1,17},{17,1},{2,18},{18,2},{3,19},{19,3},{4,20},{20... | collective-permute-start | bytes 98312 | tf_op jit(solution)/shard_map/ppermute | solution.py:516
  77.2 2.5 %collective-permute-start.13 = (f32[3,256,512]{2,1,0:T(8,128)S(1)}, f32[3,256,512]{2,1,0:T(8,128)S(1)}, u32[]{:S(2)}, u32[]{:S(2)}) collective-permute-start(f32[3,256,512]{2,1,0:T(8,128)S(1)} %copy-done.2), channel_id=1, source_target_pairs={{0,16},{1,17},{2,18},{3,19},{4,20},{5,21},{6,22},{7,23},{8,24},{9,... | collective-permute-start | bytes 4718600 | tf_op jit(solution)/shard_map/ppermute | solution.py:533
  79.8 2.9 %collective-permute-start.9 = (f32[16,768]{1,0:T(8,128)S(1)}, f32[16,768]{1,0:T(8,128)S(1)}, u32[]{:S(2)}, u32[]{:S(2)}) collective-permute-start(f32[16,768]{1,0:T(8,128)S(1)} %get-tuple-element.29), channel_id=1, source_target_pairs={{0,8},{1,9},{2,10},{3,11},{4,12},{5,13},{6,14},{7,15},{8,0},{9,1},... | collective-permute-start | bytes 147464 | tf_op jit(solution)/shard_map/ppermute | solution.py:511
  82.7 2.2 %collective-permute-done.9 = f32[16,768]{1,0:T(8,128)S(1)} collective-permute-done((f32[16,768]{1,0:T(8,128)S(1)}, f32[16,768]{1,0:T(8,128)S(1)}, u32[]{:S(2)}, u32[]{:S(2)}) %collective-permute-start.9) | collective-permute-done | bytes 49184 | tf_op jit(solution)/shard_map/ppermute | solution.py:511
  84.9 2.4 %collective-permute-start.10 = (f32[32,768]{1,0:T(8,128)S(1)}, f32[32,768]{1,0:T(8,128)S(1)}, u32[]{:S(2)}, u32[]{:S(2)}) collective-permute-start(f32[32,768]{1,0:T(8,128)S(1)} %pad_maximum_fusion.3), channel_id=1, source_target_pairs={{0,4},{1,5},{2,6},{3,7},{4,0},{5,1},{6,2},{7,3},{8,12},{9,13},{10,... | collective-permute-start | bytes 294920 | tf_op jit(solution)/shard_map/ppermute | solution.py:511
  87.2 2.6 %collective-permute-done.10 = f32[32,768]{1,0:T(8,128)S(1)} collective-permute-done((f32[32,768]{1,0:T(8,128)S(1)}, f32[32,768]{1,0:T(8,128)S(1)}, u32[]{:S(2)}, u32[]{:S(2)}) %collective-permute-start.10) | collective-permute-done | bytes 98336 | tf_op jit(solution)/shard_map/ppermute | solution.py:511
  89.8 1.6 %collective-permute-start.11 = (f32[64,768]{1,0:T(8,128)S(1)}, f32[64,768]{1,0:T(8,128)S(1)}, u32[]{:S(2)}, u32[]{:S(2)}) collective-permute-start(f32[64,768]{1,0:T(8,128)S(1)} %pad_maximum_fusion.1), channel_id=1, source_target_pairs={{0,2},{1,3},{2,0},{3,1},{4,6},{5,7},{6,4},{7,5},{8,10},{9,11},{10,... | collective-permute-start | bytes 589832 | tf_op jit(solution)/shard_map/ppermute | solution.py:511
  91.4 4.1 %collective-permute-done.11 = f32[64,768]{1,0:T(8,128)S(1)} collective-permute-done((f32[64,768]{1,0:T(8,128)S(1)}, f32[64,768]{1,0:T(8,128)S(1)}, u32[]{:S(2)}, u32[]{:S(2)}) %collective-permute-start.11) | collective-permute-done | bytes 196640 | tf_op jit(solution)/shard_map/ppermute | solution.py:511
  95.7 1.7 %collective-permute-done.12 = f32[128,768]{1,0:T(8,128)S(1)} collective-permute-done((f32[128,768]{1,0:T(8,128)S(1)}, f32[128,768]{1,0:T(8,128)S(1)}, u32[]{:S(2)}, u32[]{:S(2)}) %collective-permute-start.12) | collective-permute-done | bytes 393248 | tf_op jit(solution)/shard_map/ppermute | solution.py:511
  97.4 14.9 %shard_map.71 = (f32[256,512]{1,0:T(8,128)}, f32[256,256]{1,0:T(8,128)S(1)}, f32[256,256]{1,0:T(8,128)S(1)}) custom-call(f32[256,768]{1,0:T(8,128)S(1)} %constant_dynamic-update-slice_fusion.g_ref), custom_call_target="tpu_custom_call" | custom-call | tf_op jit(solution)/shard_map/pallas_call | solution.py:457
  113.5 5.5 %shard_map.72 = f32[3,256,1024]{2,1,0:T(8,128)} custom-call(f32[256,256]{1,0:T(8,128)S(1)} %get-tuple-element.20.own_ref, f32[256,256]{1,0:T(8,128)S(1)} %get-tuple-element.21.other_ref, f32[3,256,512]{2,1,0:T(8,128)S(1)} %get-tuple-element.16.refs_5_.first_ref, f32[3,256,512]{2,1,0:T(8,128)S(1)} %copy-done.2, ...), custom_call_target="tpu_custom_call" | custom-call | tf_op jit(solution)/shard_map/pallas_call | solution.py:480
  (47 shorter events, 7.7 us)
Async XLA Ops:
  0.6 6.9 %copy-start.5 = (f32[3,1024]{1,0:T(4,128)S(1)}, f32[3,1024]{1,0:T(4,128)}, u32[]{:S(2)}) copy-start(f32[3,1024]{1,0:T(4,128)} %param.8) | copy-start | bytes 36868
  0.6 6.9 %copy-start.6 = (f32[1024]{0:T(1024)S(1)}, f32[1024]{0:T(1024)}, u32[]{:S(2)}) copy-start(f32[1024]{0:T(1024)} %param.6) | copy-start | bytes 12292
  0.7 6.9 %copy-start = (f32[3,256,1024]{2,1,0:T(8,128)S(1)}, f32[3,256,1024]{2,1,0:T(8,128)}, u32[]{:S(2)}) copy-start(f32[3,256,1024]{2,1,0:T(8,128)} %refs_1_.1) | copy-start | bytes 9437188
  3.5 40.4 %collective-permute-start = (f32[3,256,512]{2,1,0:T(8,128)}, f32[3,256,512]{2,1,0:T(8,128)}, u32[]{:S(2)}, u32[]{:S(2)}) collective-permute-start(f32[3,256,512]{2,1,0:T(8,128)} %constant_dynamic-slice_fusion), channel_id=1, source_target_pairs={{0,16},{16,0},{1,17},{17,1},{2,18},{18,2},{3,19},{19,3},{4,20},{20... | collective-permute-start | bytes 4718600 | tf_op jit(solution)/shard_map/ppermute | solution.py:516
  7.6 7.4 %copy-start.3 = (s32[4]{0:T(128)S(1)}, s32[4]{0:T(128)}, u32[]{:S(2)}) copy-start(s32[4]{0:T(128)} %refs_0_.3) | copy-start | bytes 52
  8.0 2.8 %collective-permute-start.1 = (f32[64,256]{1,0:T(8,128)S(1)}, f32[64,256]{1,0:T(8,128)S(1)}, u32[]{:S(2)}, u32[]{:S(2)}) collective-permute-start(f32[64,256]{1,0:T(8,128)S(1)} %get-tuple-element.13), channel_id=1, source_target_pairs={{0,1},{1,2},{2,3},{3,4},{4,5},{5,6},{6,7},{7,8},{8,9},{9,10},{10,1... | collective-permute-start | bytes 196616 | tf_op jit(solution)/shard_map/ppermute | solution.py:529
  9.5 4.7 %collective-permute-start.2 = (f32[64,256]{1,0:T(8,128)S(1)}, f32[64,256]{1,0:T(8,128)S(1)}, u32[]{:S(2)}, u32[]{:S(2)}) collective-permute-start(f32[64,256]{1,0:T(8,128)S(1)} %get-tuple-element.15), channel_id=1, source_target_pairs={{1,0},{2,1},{3,2},{4,3},{5,4},{6,5},{7,6},{8,7},{9,8},{10,9},{11,1... | collective-permute-start | bytes 196616 | tf_op jit(solution)/shard_map/ppermute | solution.py:530
  14.3 29.6 %collective-permute-start.3 = (f32[128,256]{1,0:T(8,128)S(1)}, f32[128,256]{1,0:T(8,128)S(1)}, u32[]{:S(2)}, u32[]{:S(2)}) collective-permute-start(f32[128,256]{1,0:T(8,128)S(1)} %maximum_select_fusion), channel_id=1, source_target_pairs={{0,16},{16,0},{1,17},{17,1},{2,18},{18,2},{3,19},{19,3},{4,20},{20... | collective-permute-start | bytes 393224 | tf_op jit(solution)/shard_map/ppermute | solution.py:516
  39.5 1.2 copy-start.1
  58.9 18.3 %copy-start.2 = (f32[3,256,512]{2,1,0:T(8,128)S(1)}, f32[3,256,512]{2,1,0:T(8,128)}, u32[]{:S(2)}) copy-start(f32[3,256,512]{2,1,0:T(8,128)} %copy-done.1) | copy-start | bytes 4718596
  58.9 1.6 %collective-permute-start.4 = (f32[128,512]{1,0:T(8,128)S(1)}, f32[128,512]{1,0:T(8,128)S(1)}, u32[]{:S(2)}, u32[]{:S(2)}) collective-permute-start(f32[128,512]{1,0:T(8,128)S(1)} %slice.55), channel_id=1, source_target_pairs={{0,1},{1,0},{2,3},{3,2},{4,5},{5,4},{6,7},{7,6},{8,9},{9,8},{10,11... | collective-permute-start | bytes 786440 | tf_op jit(solution)/shard_map/ppermute | solution.py:505
  60.6 5.7 %collective-permute-start.5 = (f32[64,512]{1,0:T(8,128)S(1)}, f32[64,512]{1,0:T(8,128)S(1)}, u32[]{:S(2)}, u32[]{:S(2)}) collective-permute-start(f32[64,512]{1,0:T(8,128)S(1)} %slice.71), channel_id=1, source_target_pairs={{0,2},{1,3},{2,0},{3,1},{4,6},{5,7},{6,4},{7,5},{8,10},{9,11},{10,... | collective-permute-start | bytes 393224 | tf_op jit(solution)/shard_map/ppermute | solution.py:505
  66.3 4.3 %collective-permute-start.6 = (f32[32,512]{1,0:T(8,128)S(1)}, f32[32,512]{1,0:T(8,128)S(1)}, u32[]{:S(2)}, u32[]{:S(2)}) collective-permute-start(f32[32,512]{1,0:T(8,128)S(1)} %slice.73), channel_id=1, source_target_pairs={{0,4},{1,5},{2,6},{3,7},{4,0},{5,1},{6,2},{7,3},{8,12},{9,13},{10,... | collective-permute-start | bytes 196616 | tf_op jit(solution)/shard_map/ppermute | solution.py:505
  70.6 4.9 %collective-permute-start.7 = (f32[16,512]{1,0:T(8,128)S(1)}, f32[16,512]{1,0:T(8,128)S(1)}, u32[]{:S(2)}, u32[]{:S(2)}) collective-permute-start(f32[16,512]{1,0:T(8,128)S(1)} %slice.75), channel_id=1, source_target_pairs={{0,8},{1,9},{2,10},{3,11},{4,12},{5,13},{6,14},{7,15},{8,0},{9,1},... | collective-permute-start | bytes 98312 | tf_op jit(solution)/shard_map/ppermute | solution.py:505
  75.5 4.2 %collective-permute-start.8 = (f32[16,512]{1,0:T(8,128)S(1)}, f32[16,512]{1,0:T(8,128)S(1)}, u32[]{:S(2)}, u32[]{:S(2)}) collective-permute-start(f32[16,512]{1,0:T(8,128)S(1)} %slice_add_fusion.3), channel_id=1, source_target_pairs={{0,16},{16,0},{1,17},{17,1},{2,18},{18,2},{3,19},{19,3},{4,20},{20... | collective-permute-start | bytes 98312 | tf_op jit(solution)/shard_map/ppermute | solution.py:516
  77.2 35.1 %collective-permute-start.13 = (f32[3,256,512]{2,1,0:T(8,128)S(1)}, f32[3,256,512]{2,1,0:T(8,128)S(1)}, u32[]{:S(2)}, u32[]{:S(2)}) collective-permute-start(f32[3,256,512]{2,1,0:T(8,128)S(1)} %copy-done.2), channel_id=1, source_target_pairs={{0,16},{1,17},{2,18},{3,19},{4,20},{5,21},{6,22},{7,23},{8,24},{9,... | collective-permute-start | bytes 4718600 | tf_op jit(solution)/shard_map/ppermute | solution.py:533
  79.8 5.1 %collective-permute-start.9 = (f32[16,768]{1,0:T(8,128)S(1)}, f32[16,768]{1,0:T(8,128)S(1)}, u32[]{:S(2)}, u32[]{:S(2)}) collective-permute-start(f32[16,768]{1,0:T(8,128)S(1)} %get-tuple-element.29), channel_id=1, source_target_pairs={{0,8},{1,9},{2,10},{3,11},{4,12},{5,13},{6,14},{7,15},{8,0},{9,1},... | collective-permute-start | bytes 147464 | tf_op jit(solution)/shard_map/ppermute | solution.py:511
  84.9 5.0 %collective-permute-start.10 = (f32[32,768]{1,0:T(8,128)S(1)}, f32[32,768]{1,0:T(8,128)S(1)}, u32[]{:S(2)}, u32[]{:S(2)}) collective-permute-start(f32[32,768]{1,0:T(8,128)S(1)} %pad_maximum_fusion.3), channel_id=1, source_target_pairs={{0,4},{1,5},{2,6},{3,7},{4,0},{5,1},{6,2},{7,3},{8,12},{9,13},{10,... | collective-permute-start | bytes 294920 | tf_op jit(solution)/shard_map/ppermute | solution.py:511
  89.8 5.7 %collective-permute-start.11 = (f32[64,768]{1,0:T(8,128)S(1)}, f32[64,768]{1,0:T(8,128)S(1)}, u32[]{:S(2)}, u32[]{:S(2)}) collective-permute-start(f32[64,768]{1,0:T(8,128)S(1)} %pad_maximum_fusion.1), channel_id=1, source_target_pairs={{0,2},{1,3},{2,0},{3,1},{4,6},{5,7},{6,4},{7,5},{8,10},{9,11},{10,... | collective-permute-start | bytes 589832 | tf_op jit(solution)/shard_map/ppermute | solution.py:511
  95.6 1.8 %collective-permute-start.12 = (f32[128,768]{1,0:T(8,128)S(1)}, f32[128,768]{1,0:T(8,128)S(1)}, u32[]{:S(2)}, u32[]{:S(2)}) collective-permute-start(f32[128,768]{1,0:T(8,128)S(1)} %pad_maximum_fusion), channel_id=1, source_target_pairs={{0,1},{1,0},{2,3},{3,2},{4,5},{5,4},{6,7},{7,6},{8,9},{9,8},{10,11... | collective-permute-start | bytes 1179656 | tf_op jit(solution)/shard_map/ppermute | solution.py:511
  112.3 1.2 copy-start.4

commit v4 on v3

--- a/solution.py
+++ b/solution.py
@@ -14,54 +14,64 @@
 COEFS = TERMS + 4
 TILE = 128
 EARLY = 1
-AT_ONCE = 4
+AT_ONCE = 8
 EXACT = lax.Precision.HIGHEST
 CLOSE = lax.Precision.HIGH
 VMEM = pl.BlockSpec(memory_space=pltpu.VMEM)
+
+
+def taking(micros):
+    return pl.CostEstimate(flops=0, transcendentals=0, bytes_accessed=int(micros * 3.5e6))
+
+
 PARAMS = pltpu.CompilerParams(vmem_limit_bytes=48 * 2**20)
 
 
-def pack_kernel(first_ref, before_ref, after_ref, last_ref, coef_ref, low_ref, mid_ref, high_ref):
-    rows, cells = first_ref.shape[1], coef_ref.shape[1]
+def pack_kernel(x_ref, coef_ref, low_ref, mid_ref, high_ref, tiles_ref, sems):
+    rows, cells = x_ref.shape[1], coef_ref.shape[1]
     blank = jnp.zeros((rows - COEFS, TILE), jnp.float32)
-
-    def pack(out_ref, x_ref, start, spot):
+    is_first = lax.axis_index("probe") == 0
+    middle = jnp.where(is_first, cells // 4, cells // 4 * 3 - TILE)
+    starts = (0, pl.multiple_of(middle, TILE), cells - TILE)
+    copies = [
+        pltpu.make_async_copy(x_ref.at[:, :, pl.ds(start, TILE)], tiles_ref.at[at], sems.at[at])
+        for at, start in enumerate(starts)
+    ]
+    for copy in copies:
+        copy.start()
+    for copy in copies:
+        copy.wait()
+
+    def pack(out_ref, at, spot):
         for comp in range(3):
-            out_ref[HALO * comp : HALO * comp + HALO, :] = x_ref[comp].T[spot]
-        coef = jnp.concatenate([coef_ref[:, start : start + TILE], blank], 0)
+            out_ref[HALO * comp : HALO * comp + HALO, :] = tiles_ref[at, comp].T[spot]
+        coef = jnp.concatenate([coef_ref[:, pl.ds(starts[at], TILE)], blank], 0)
         out_ref[3 * HALO : 4 * HALO, :] = coef.T[spot]
 
     head, tail = slice(0, HALO), slice(TILE - HALO, TILE)
-    pack(low_ref, first_ref, 0, head)
-    pack(high_ref, last_ref, cells - TILE, tail)
-    is_first = lax.axis_index("probe") == 0
+    pack(low_ref, 0, head)
+    pack(high_ref, 2, tail)
 
     @pl.when(is_first)
     def _():
-        pack(mid_ref, after_ref, cells // 2, head)
+        pack(mid_ref, 1, head)
 
     @pl.when(jnp.logical_not(is_first))
     def _():
-        pack(mid_ref, before_ref, cells // 2 - TILE, tail)
+        pack(mid_ref, 1, tail)
 
 
 def pack_edges(probes, coefs):
     _, rows, cells = probes.shape
     edge = jax.ShapeDtypeStruct((4 * HALO, rows), jnp.float32)
-    half = cells // TILE // 2
-
-    def tile(at):
-        return pl.BlockSpec((3, rows, TILE), lambda i: (0, 0, at))
-
     return pl.pallas_call(
         pack_kernel,
-        grid=(1,),
-        in_specs=[tile(0), tile(half - 1), tile(half), tile(2 * half - 1)]
-        + [pl.BlockSpec((COEFS, cells), lambda i: (0, 0))],
-        out_specs=[pl.BlockSpec((4 * HALO, rows), lambda i: (0, 0))] * 3,
+        in_specs=[pl.BlockSpec(memory_space=pltpu.HBM), VMEM],
+        out_specs=[VMEM] * 3,
         out_shape=[edge] * 3,
+        scratch_shapes=[pltpu.VMEM((3, 3, rows, TILE), jnp.float32), pltpu.SemaphoreType.DMA((3,))],
         compiler_params=PARAMS,
-    )(probes, probes, probes, probes, coefs)
+    )(probes, coefs)
 
 
 def turned(x, amount):
@@ -78,34 +88,65 @@
     ]
 
 
-def stretch(own, ends, lane):
-    turns = [turned(t, TILE - HALO) for t in own]
-    middle = [jnp.where(lane < HALO, turns[i], turns[i + 1]) for i in range(len(own) - 1)]
-    return [jnp.where(lane < HALO, ends, turns[0])] + middle + [jnp.where(lane < HALO, turns[-1], ends)]
-
-
-def panel_steps(off_ref, x_ref, coef_ref, low_ref, high_ref, out_refs, ends_ref, tab_ref, mid_ref, in_ref):
-    _, rows, cells = x_ref.shape
-    share = cells // TILE // len(out_refs)
-    count = cells // TILE
+def stretch(tiles, lane):
+    turns = [turned(t, TILE - HALO) for t in tiles]
+    return [jnp.where(lane < HALO, turns[i], turns[i + 1]) for i in range(len(tiles) - 1)]
+
+
+def segment_steps(x_at, coef_at, count, off_ref, x_ref, coef_ref, edges, out_refs, scratch):
+    rows = edges[0].shape[1]
+    tab_ref, mid_ref, in_ref, ends_ref, *fetched = scratch
+    if fetched:
+        here_ref, sem = fetched
+        fetch = pltpu.make_async_copy(x_ref, here_ref, sem)
+        fetch.start()
     lane = lax.broadcasted_iota(jnp.int32, (8, TILE), 1)
-    offs = [off_ref[b] for b in range(BANDS)]
-
-    blank = jnp.zeros((TILE - 2 * HALO, rows), jnp.float32)
+    given = [off_ref[b] for b in range(BANDS)]
+    slots = [sum((other < off).astype(jnp.int32) for other in given) for off in given]
+    offs = [sum(jnp.where(slot == r, off, 0) for slot, off in zip(slots, given)) for r in range(BANDS)]
+    offs[0], offs[-1] = -REACH, REACH
+    me = lax.axis_index("probe")
+    x_first, coef_first = x_at(me), coef_at(me)
+
+    coef_low_ref, coef_high_ref = edges
+    blank = jnp.zeros((TILE - HALO, rows), jnp.float32)
     for comp in range(4):
-        spot = slice(HALO * comp, HALO * comp + HALO)
-        ends_ref[comp] = jnp.concatenate([low_ref[spot, :], high_ref[spot, :], blank], 0).T
+        start = HALO * comp
+        low, high = coef_low_ref[start : start + HALO, :], coef_high_ref[start : start + HALO, :]
+        if comp < 3 and not fetched:
+            start += 3 * rows
+            low, high = x_ref[start : start + HALO, :], x_ref[start + 3 * HALO : start + 4 * HALO, :]
+        ends_ref[comp] = jnp.concatenate([blank, low], 0).T
+        ends_ref[4 + comp] = jnp.concatenate([high, blank], 0).T
+
+    def tiles_of(load, first, total, comp, spot):
+        def at(i):
+            start = i * TILE
+            return load(pl.ds(start if isinstance(i, int) else pl.multiple_of(start, TILE), TILE))
+
+        def edge(is_end, which, i):
+            halo = ends_ref[which + comp, spot, :]
+            if isinstance(first, int):
+                return halo if is_end else at(i)
+            return jnp.where(is_end, halo, at(jnp.clip(i, 0, total - 1)))
+
+        return (
+            [edge(first == 0, 0, first - 1)]
+            + [at(first + i) for i in range(count)]
+            + [edge(first + count == total, 4, first + count)]
+        )
 
     for group in range(COEFS // 8):
         spot = slice(8 * group, 8 * group + 8)
+        coef_total = coef_ref.shape[1] // TILE
         ext = stretch(
-            [coef_ref[spot, TILE * i : TILE * i + TILE] for i in range(count)], ends_ref[3, spot, :], lane
+            tiles_of(lambda where: coef_ref[spot, where], coef_first, coef_total, 3, spot), lane
         )
         by_step = {(0, b): moved(ext, REACH, lane) for b in range(BANDS)}
         by_step.update({(2, b): moved(ext, 3 * REACH, lane) for b in range(BANDS)})
         for b in range(BANDS):
-            by_step[1, b] = moved(ext, 2 * REACH - offs[b], lane)
-            by_step[3, b] = moved(ext, 4 * REACH - offs[b], lane)
+            by_step[1, b] = moved(ext, 2 * REACH - given[b], lane)
+            by_step[3, b] = moved(ext, 4 * REACH - given[b], lane)
         for j in range(8):
             row = 8 * group + j
             if row >= TERMS:
@@ -113,7 +154,7 @@
             for step in range(4):
                 for i in range(count + 1):
                     tile = by_step[step, row // 9][i]
-                    tab_ref[step, row, :, TILE * i : TILE * i + TILE] = jnp.broadcast_to(
+                    tab_ref[step, 9 * slots[row // 9] + row % 9, :, TILE * i : TILE * i + TILE] = jnp.broadcast_to(
                         tile[j : j + 1, :], (8, TILE)
                     )
         if group == COEFS // 8 - 1:
@@ -129,20 +170,16 @@
                 inside = jnp.broadcast_to(between[i][4:5, :], (8, TILE)) != 0.0
                 in_ref[at] = jnp.where(inside, 1.0, 0.0)
 
-    masks = {}
-    for sign in (1, -1):
-        for b in range(BANDS):
-            masks[sign, b] = lane < TILE - (REACH + sign * offs[b])
-    center = lane < TILE - REACH
-
     def apply(tiles, step, outs):
         sign = 1 if step % 2 == 0 else -1
         result = [[[], [], []] for _ in range(AT_ONCE)]
+        amounts = [REACH] + [REACH + sign * off for off in offs]
+        masks = [lane < TILE - amount for amount in amounts]
 
         def turns_of(i):
             return [
                 [
-                    [turned(row[i], REACH)] + [turned(row[i], REACH + sign * offs[b]) for b in range(BANDS)]
+                    [row[i] if isinstance(amount, int) and amount == 0 else turned(row[i], amount) for amount in amounts]
                     for row in tiles[at]
                 ]
                 for at in range(AT_ONCE)
@@ -155,10 +192,11 @@
             spot = slice(TILE * i, TILE * i + TILE)
             shifted = [
                 [
-                    [jnp.where(center, here[at][m][0], ahead[at][m][0])]
-                    + [
-                        jnp.where(masks[sign, b], here[at][m][1 + b], ahead[at][m][1 + b])
-                        for b in range(BANDS)
+                    [
+                        here[at][m][j]
+                        if isinstance(amounts[j], int) and amounts[j] == 0
+                        else jnp.where(masks[j], here[at][m][j], ahead[at][m][j])
+                        for j in range(1 + BANDS)
                     ]
                     for m in range(3)
                 ]
@@ -188,33 +226,48 @@
 
     def group_step(g, carry):
         spots = [pl.ds(pl.multiple_of(8 * (AT_ONCE * g + at), 8), 8) for at in range(AT_ONCE)]
+        total = x_ref.shape[-1] // TILE
+
+        def load(m, at, where):
+            if fetched:
+                return here_ref[m, spots[at], where]
+            return x_ref[pl.ds(pl.multiple_of(m * rows + 8 * (AT_ONCE * g + at), 8), 8), where]
+
         tiles = [
             [
                 stretch(
-                    [x_ref[m, spot, TILE * i : TILE * i + TILE] for i in range(count)], ends_ref[m, spot, :], lane
+                    tiles_of(functools.partial(load, m, at), x_first, total, m, spot), lane
                 )
                 for m in range(3)
             ]
-            for spot in spots
+            for at, spot in enumerate(spots)
         ]
         for step in range(4):
             tiles = apply(tiles, step, count + 1 if step < 3 else count)
         for at, spot in enumerate(spots):
             for m in range(3):
-                for i in range(count):
-                    out_refs[i // share][m, spot, pl.ds(TILE * (i % share), TILE)] = tiles[at][m][i]
+                for i in range(count // len(out_refs)):
+                    here = slice(TILE * i, TILE * i + TILE)
+                    if len(out_refs) == 1:
+                        out_refs[0][m, spot, here] = tiles[at][m][i]
+                    else:
+                        one, two = tiles[at][m][i], tiles[at][m][count // 2 + i]
+                        out_refs[0][m, spot, here] = jnp.where(me == 0, one, two)
+                        out_refs[1][m, spot, here] = jnp.where(me == 0, two, one)
         return carry
 
+    if fetched:
+        fetch.wait()
     lax.fori_loop(0, rows // (8 * AT_ONCE), group_step, 0)
 
 
-def panel_scratch(rows, cells):
-    wide = cells + TILE
+def segment_scratch(rows, count):
+    wide = (count + 1) * TILE
     return [
-        pltpu.VMEM((4, rows, TILE), jnp.float32),
         pltpu.VMEM((4, TERMS, 8, wide), jnp.float32),
         pltpu.VMEM((2, 3, 8, wide), jnp.float32),
         pltpu.VMEM((2, 8, TILE), jnp.float32),
+        pltpu.VMEM((8, rows, TILE), jnp.float32),
     ]
 
 
@@ -236,29 +289,54 @@
 ACROSS = ((0,), (0,))
 
 
-def own_kernel(scale, *refs):
-    *ins, first_ref, second_ref, gram_ref = refs[:8]
-    panel_steps(*ins, (first_ref, second_ref), *refs[8:])
+def products(left, right):
     total = None
-    for ref in (first_ref, second_ref):
+    for k in range(3):
+        part = close_dot(pieces(left[k]), pieces(right[k]), ALONG)
+        total = part if total is None else total + part
+    return total
+
+
+def own_products(refs):
+    dot = functools.partial(lax.dot_general, dimension_numbers=(ALONG, ((), ())), preferred_element_type=jnp.float32)
+    main = mixed = None
+    for ref in refs:
         for k in range(3):
-            x = pieces(ref[k])
-            part = close_dot(x, x, ALONG)
-            total = part if total is None else total + part
-    gram_ref[...] = total * scale
-
-
-def panel_of(probes, coefs, low, high, offsets, scale):
-    _, rows, cells = probes.shape
-    half = jax.ShapeDtypeStruct((3, rows, cells // 2), jnp.float32)
-    return pl.pallas_call(
-        functools.partial(own_kernel, scale),
-        in_specs=[SMEM] + [VMEM] * 4,
-        out_specs=[VMEM] * 3,
-        out_shape=[half, half, jax.ShapeDtypeStruct((rows, rows), jnp.float32)],
-        scratch_shapes=panel_scratch(rows, cells),
+            high, low = pieces(ref[k])
+            one, two = dot(high, high), dot(high, low)
+            main, mixed = (one, two) if main is None else (main + one, mixed + two)
+    return main + (mixed + mixed.T)
+
+
+def segment_kernel(x_at, coef_at, count, parts, scale, off_ref, x_ref, coef_ref, *refs):
+    edges, refs = refs[:2], refs[2:]
+    rest, refs = (refs[:2], refs[2:]) if scale else ((), refs)
+    out_refs, refs = refs[:parts], refs[parts:]
+    gram_ref, refs = (refs[0], refs[1:]) if scale else (None, refs)
+    segment_steps(x_at, coef_at, count, off_ref, x_ref, coef_ref, edges, out_refs, refs)
+    if scale:
+        gram_ref[...] = own_products((*out_refs, *rest)) * scale
+
+
+def segment(x_at, coef_at, count, offsets, x, coefs, edges, parts=1, rest=(), scale=None):
+    rows = edges[0].shape[1]
+    scratch, place = segment_scratch(rows, count), VMEM
+    if x.ndim == 3:
+        place = pl.BlockSpec(memory_space=pltpu.HBM)
+        scratch += [pltpu.VMEM(x.shape, jnp.float32), pltpu.SemaphoreType.DMA(())]
+    shapes = [jax.ShapeDtypeStruct((3, rows, count * TILE // parts), jnp.float32)] * parts
+    if scale:
+        shapes.append(jax.ShapeDtypeStruct((rows, rows), jnp.float32))
+    result = pl.pallas_call(
+        functools.partial(segment_kernel, x_at, coef_at, count, parts, scale),
+        in_specs=[SMEM, place] + [VMEM] * (1 + len(edges) + len(rest)),
+        out_specs=[VMEM] * len(shapes),
+        out_shape=shapes,
+        scratch_shapes=scratch,
         compiler_params=PARAMS,
-    )(offsets, probes, coefs, low, high)
+        cost_estimate=taking(2 + 2 * (count + 1) * rows / 256),
+    )(offsets, x, coefs, *edges, *rest)
+    return result if len(shapes) > 1 else result[0]
 
 
 def reversed_bits(place, count):
@@ -270,30 +348,23 @@
 
 
 def block_at(place, count):
-    return lax.bitwise_xor(lax.axis_index("slab"), jnp.int32(reversed_bits(place, count)))
-
-
-def cross_kernel(scale, count, *refs):
-    *ins, first_ref, second_ref, gram_ref, other_ref, out_ref = refs[:10]
-    panel_steps(*ins, (other_ref,), *refs[10:-1])
-    work = refs[-1]
+    return lax.bitwise_xor(lax.rem(lax.axis_index("slab"), count), jnp.int32(reversed_bits(place, count)))
+
+
+def cross_kernel(scale, count, own_ref, raw_ref, ready_ref, gram_ref, out_ref, work):
     rows = gram_ref.shape[0]
+    quarter = raw_ref.shape[2]
     is_first = lax.axis_index("probe") == 0
-
-    def product(left, right):
-        total = None
-        for k in range(3):
-            part = close_dot(pieces(left[k]), pieces(right[k]), ALONG)
-            total = part if total is None else total + part
-        work[...] = total * scale
 
     @pl.when(is_first)
     def _():
-        product(second_ref, other_ref)
+        near, far = own_ref.at[:, :, :quarter], own_ref.at[:, :, quarter:]
+        work[...] = (products(near, ready_ref) + products(far, raw_ref)) * scale
 
     @pl.when(jnp.logical_not(is_first))
     def _():
-        product(other_ref, first_ref)
+        near, far = own_ref.at[:, :, :quarter], own_ref.at[:, :, quarter:]
+        work[...] = (products(raw_ref, near) + products(ready_ref, far)) * scale
 
     share = rows // count
     for place in range(count):
@@ -302,19 +373,16 @@
         out_ref[share * place : share * place + share, rows:] = work[spot, :]
 
 
-def cross_of(half, coefs, low, high, offsets, first, second, gram, scale, count):
-    _, rows, cells = half.shape
+def cross_of(own, raw, ready, gram, scale, count):
+    _, rows, _ = own.shape
     return pl.pallas_call(
         functools.partial(cross_kernel, scale, count),
-        in_specs=[SMEM] + [VMEM] * 7,
-        out_specs=[VMEM] * 2,
-        out_shape=[
-            jax.ShapeDtypeStruct(half.shape, jnp.float32),
-            jax.ShapeDtypeStruct((rows, 2 * rows), jnp.float32),
-        ],
-        scratch_shapes=panel_scratch(rows, cells) + [pltpu.VMEM((rows, rows), jnp.float32)],
+        in_specs=[VMEM] * 4,
+        out_specs=VMEM,
+        out_shape=jax.ShapeDtypeStruct((rows, 2 * rows), jnp.float32),
+        scratch_shapes=[pltpu.VMEM((rows, rows), jnp.float32)],
         compiler_params=PARAMS,
-    )(offsets, half, coefs, low, high, first, second, gram)
+    )(own, raw, ready, gram)
 
 
 def over_lanes(x, j):
@@ -461,30 +529,40 @@
         out_shape=[jax.ShapeDtypeStruct((rows, 2 * rows), jnp.float32), square, square],
         scratch_shapes=factor_scratch(2 * rows) + [pltpu.VMEM((2 * rows, 2 * rows), jnp.float32)] * 2,
         compiler_params=PARAMS,
+        cost_estimate=taking(15),
     )(travelled)
 
 
-def basis_kernel(own_ref, other_ref, first_ref, second_ref, front_ref, back_ref, out_ref):
-    half = first_ref.shape[2]
-    own, other = pieces(own_ref[...]), pieces(other_ref[...])
-    for at, (mine, theirs) in enumerate(((first_ref, front_ref), (second_ref, back_ref))):
-        out_ref[0, :, half * at : half * at + half] = close_dot(own, pieces(mine[0]), PLAIN) + close_dot(
-            other, pieces(theirs[0]), PLAIN
-        )
-
-
-def basis_of(own, other, first, second, front, back):
-    _, rows, half = first.shape
+def basis_kernel(own_ref, other_ref, outer_ref, inner_ref, half_ref, raw_ref, ready_ref, early_ref, late_ref, out_ref):
+    me = lax.axis_index("probe")
+    quarter = outer_ref.shape[2]
+    own = pieces(own_ref[...])
+    starts = (me * 3 * quarter, (1 + me) * quarter, (1 - me) * 2 * quarter)
+    for start, ref in zip(starts, (outer_ref, inner_ref, half_ref)):
+        spot = pl.ds(pl.multiple_of(start, TILE), ref.shape[2])
+        out_ref[0, :, spot] = close_dot(own, pieces(ref[0]), PLAIN)
+
+    @pl.when(me == 1)
+    def _():
+        other = pieces(other_ref[...])
+        for at, ref in enumerate((raw_ref, ready_ref, early_ref, late_ref)):
+            spot = slice(quarter * at, quarter * at + quarter)
+            out_ref[0, :, spot] = out_ref[0, :, spot] + close_dot(other, pieces(ref[0]), PLAIN)
+
+
+def basis_of(own, other, outer, inner, half, raw, ready, early, late):
+    _, rows, quarter = outer.shape
     weights = pl.BlockSpec((rows, rows), lambda k: (0, 0))
-    panel = pl.BlockSpec((1, rows, half), lambda k: (k, 0, 0))
+    short = pl.BlockSpec((1, rows, quarter), lambda k: (k, 0, 0))
+    wide = pl.BlockSpec((1, rows, 2 * quarter), lambda k: (k, 0, 0))
     return pl.pallas_call(
         basis_kernel,
         grid=(3,),
-        in_specs=[weights] * 2 + [panel] * 4,
-        out_specs=pl.BlockSpec((1, rows, 2 * half), lambda k: (k, 0, 0)),
-        out_shape=jax.ShapeDtypeStruct((3, rows, 2 * half), jnp.float32),
+        in_specs=[weights, weights, short, short, wide, short, short, short, short],
+        out_specs=pl.BlockSpec((1, rows, 4 * quarter), lambda k: (k, 0, 0)),
+        out_shape=jax.ShapeDtypeStruct((3, rows, 4 * quarter), jnp.float32),
         compiler_params=PARAMS,
-    )(own, other, first, second, front, back)
+    )(own, other, outer, inner, half, raw, ready, early, late)
 
 
 def partners(axis, bit):
@@ -499,44 +577,83 @@
     return bits
 
 
+def split_bits(axis):
+    bits = bits_of(axis)
+    return bits[: max(len(bits) - 2, 0)], bits[max(len(bits) - 2, 0) :]
+
+
 def scatter_sum(block, axis):
-    for bit in bits_of(axis):
+    halved, whole = split_bits(axis)
+    for bit in halved:
         half = block.shape[0] // 2
         block = block[:half] + lax.ppermute(block[half:], axis, partners(axis, bit))
+    for bit in whole:
+        block = block + lax.ppermute(block, axis, partners(axis, bit))
     return block
 
 
 def gather_back(block, axis):
-    for bit in reversed(bits_of(axis)):
+    for bit in reversed(split_bits(axis)[0]):
         block = jnp.concatenate([block, lax.ppermute(block, axis, partners(axis, bit))], 0)
     return block
 
 
 def swapped(block):
     return lax.ppermute(block, "probe", [(0, 1), (1, 0)])
+
+
+def halo_of(first, last):
+    slabs = lax.axis_size("slab")
+    forward = [(i, i + 1) for i in range(slabs - 1)]
+    return lax.ppermute(last, "slab", forward), lax.ppermute(first, "slab", [(b, a) for a, b in forward])
 
 
 def pair_body(probes, coefs, offsets):
     _, columns, cells = probes.shape
     slabs = lax.axis_size("slab")
     scale = 1.0 / (3 * cells * slabs)
-    is_first = lax.axis_index("probe") == 0
-    half = cells // 2
-    start = lax.axis_index("probe") * half
-    theirs = swapped(lax.dynamic_slice_in_dim(probes, start, half, 2))
+    me = lax.axis_index("probe")
+    is_first = me == 0
+    quarter = cells // 4
+    tiles = quarter // TILE
+
     first, mid, last = pack_edges(probes, coefs)
-    forward = [(i, i + 1) for i in range(slabs - 1)]
-    low = lax.ppermute(last, "slab", forward)
-    high = lax.ppermute(first, "slab", [(b, a) for a, b in forward])
-    ends = swapped(jnp.where(is_first, jnp.concatenate([low, mid], 0), jnp.concatenate([mid, high], 0)))
-    front, back, gram = panel_of(probes, coefs, low, high, offsets, scale)
-    their_back = lax.ppermute(back, "probe", [(0, 1)])
-    half_coefs = jnp.where(is_first, coefs[:, half:], coefs[:, :half])
-    their_front, sums = cross_of(
-        theirs, half_coefs, ends[: 4 * HALO], ends[4 * HALO :], offsets, front, back, gram, scale, slabs
+    low, high = halo_of(first, last)
+    pack = 3 * HALO
+    ends = jnp.where(
+        is_first,
+        jnp.concatenate([low[:pack], mid[:pack]], 0),
+        jnp.concatenate([mid[:pack], high[:pack]], 0),
     )
+    sent = lax.dynamic_slice_in_dim(probes, me * 3 * quarter, quarter, 2).reshape(3 * columns, quarter)
+    theirs = swapped(jnp.concatenate([sent, ends], 0))
+    run = functools.partial(segment, offsets=offsets, coefs=coefs)
+
+    def at_half(me):
+        return me * 2 * tiles
+
+    def at_other_half(me):
+        return (1 - me) * 2 * tiles
+
+    def at_raw(me):
+        return (1 - me) * 3 * tiles
+
+    edges = (low, high)
+    outer, inner = run(at_half, at_half, 2 * tiles, x=probes, edges=edges, parts=2)
+    ready = swapped(inner)
+    half, gram = run(
+        at_other_half, at_other_half, 2 * tiles, x=probes, edges=edges, rest=(inner, outer), scale=scale
+    )
+    rest = (half[:, :, :quarter], half[:, :, quarter:])
+    early = lax.ppermute(rest[0], "probe", [(0, 1)])
+    raw = run(lambda me: 0, at_raw, tiles, x=theirs, edges=edges)
+    count = 1 << len(split_bits("slab")[0])
+    sums = cross_of(half, raw, ready, gram, scale, count)
     share = scatter_sum(sums, "slab")
+    share, early = lax.optimization_barrier((share, early))
     other = swapped(share)
+    other, late = lax.optimization_barrier((other, rest[1]))
+    late = lax.ppermute(late, "probe", [(0, 1)])
     share = jnp.concatenate(
         [
             jnp.where(is_first, share[:, :columns], other[:, :columns]),
@@ -545,21 +662,18 @@
         ],
         1,
     )
-    r_rows, own, other = factorize_pair(gather_back(share, "slab"), slabs)
-    return basis_of(own, other, front, back, their_front, their_back), r_rows
+    r_rows, own, other = factorize_pair(gather_back(share, "slab"), count)
+    return basis_of(own, other, outer, inner, half, raw, ready, early, late), r_rows
 
 
 def whole_body(probes, coefs, offsets):
     _, columns, cells = probes.shape
-    slabs, groups = lax.axis_size("slab"), lax.axis_size("probe")
+    slabs = lax.axis_size("slab")
     me = lax.axis_index("probe")
     scale = 1.0 / (3 * cells * slabs)
     first, _, last = pack_edges(probes, coefs)
-    forward = [(i, i + 1) for i in range(slabs - 1)]
-    low = lax.ppermute(last, "slab", forward)
-    high = lax.ppermute(first, "slab", [(b, a) for a, b in forward])
-    front, back, _ = panel_of(probes, coefs, low, high, offsets, scale)
-    panel = jnp.concatenate([front, back], 2)
+    low, high = halo_of(first, last)
+    panel = segment(lambda me: 0, lambda me: 0, cells // TILE, offsets, probes, coefs, (low, high))
     everyone = lax.all_gather(panel, "probe", axis=1, tiled=True)
     part = scale * jnp.einsum("kpc,kqc->pq", panel, everyone, precision=CLOSE)
     gram = lax.all_gather(lax.psum(part, "slab"), "probe", axis=0, tiled=True)

time: 119 us -> 112 us (0.941)
  Pallas kernels: 60.4 us -> 55.9 us
  waiting for transfers between devices: 27 us -> 24.4 us
  local copies, waits for them, and re-layouts: 6.37 us -> 4.14 us
  other arithmetic: 0.18 us -> 2.15 us
    ppermute x3 -> x6, starting transfers between devices: 5.26 us -> 16.3 us  [the longest x2 6.12 us: scatter_sum(): block = block + lax.ppermute(block, axis, partners(axis, bit))]
    ppermute x3 -> x6, waiting for transfers between devices: 3.42 us -> 11.2 us  [the longest x2 7.99 us: scatter_sum(): block = block + lax.ppermute(block, axis, partners(axis, bit))]
    ppermute x4 -> x2, waiting for transfers between devices: 10.6 us -> 3.83 us  [gather_back(): lax.ppermute(block, axis, partners(axis, bit))]
    ppermute x4 -> x2, waiting for transfers between devices: 9.86 us -> 3.41 us  [scatter_sum(): block = block[:half] + lax.ppermute(block[half:], axis, partners(axis, bit))]
    ppermute x4 -> x2, starting transfers between devices: 6.92 us -> 0.52 us  [gather_back(): lax.ppermute(block, axis, partners(axis, bit))]
    pallas_call x4 -> x6, Pallas kernels: 45.5 us -> 41 us  [the longest x3 34.1 us: segment(): pl.pallas_call(functools.partial(segment_kernel, x_at, coef_at, count, pa...]
    ppermute x3, starting transfers between devices: 5.3 us -> 2.41 us  [swapped(): return lax.ppermute(block, 'probe', [(0, 1), (1, 0)])]
    ppermute x3, waiting for transfers between devices: 3.15 us -> 5.93 us  [swapped(): return lax.ppermute(block, 'probe', [(0, 1), (1, 0)])]
  transfers between devices with their start and end apart: 14 -> 13, of which waited for: 10 -> 8; matrix products, arithmetic and copies ran while one was open for 1% -> 1% of each run, Pallas kernels for 34% -> 44%
where the time goes in v4:
time: 112 us
  Pallas kernels  55.9 us (50%)
  waiting for transfers between devices  24.4 us (22%)
  starting transfers between devices  24.1 us (22%)
  local copies, waits for them, and re-layouts  4.14 us (4%)
  other arithmetic  2.15 us (2%)
    pallas_call x3, Pallas kernels, segment(): pl.pallas_call(functools.partial(segment_kernel, x_at, coef_at, count, pa...  34.1 us
    pallas_call x1, Pallas kernels, factorize_pair(): pl.pallas_call(functools.partial(pair_kernel, count), in_specs=[VMEM], ou...  14.9 us
    ppermute x2, waiting for transfers between devices, scatter_sum(): block = block + lax.ppermute(block, axis, partners(axis, bit))  7.99 us
    ppermute x2, starting transfers between devices, scatter_sum(): block = block + lax.ppermute(block, axis, partners(axis, bit))  6.12 us
    ppermute x3, waiting for transfers between devices, swapped(): return lax.ppermute(block, 'probe', [(0, 1), (1, 0)])  5.93 us
    ppermute x2, starting transfers between devices, scatter_sum(): block = block[:half] + lax.ppermute(block[half:], axis, partners(axis, bit))  4.87 us
    pallas_call x1, Pallas kernels, basis_of(): pl.pallas_call(basis_kernel, grid=(3,), in_specs=[weights, weights, short...  4.63 us
    ppermute x2, waiting for transfers between devices, gather_back(): lax.ppermute(block, axis, partners(axis, bit))  3.83 us
  transfers between devices with their start and end apart: 13, of which 8 were waited for; matrix products, arithmetic and copies ran while one was open for 1% of the time, Pallas kernels for 44%

profile of v4, /device:TPU:0, one launch (start us, length us, event | category | flops | bytes accessed | tf_op | source)
XLA Modules:
  0.0 111.5 jit_solution(7400791395359348476)
XLA Ops:
  2.5 1.9 %copy-done = f32[3,256,1024]{2,1,0:T(8,128)S(1)} copy-done((f32[3,256,1024]{2,1,0:T(8,128)S(1)}, f32[3,256,1024]{2,1,0:T(8,128)}, u32[]{:S(2)}) %copy-start) | copy-done | bytes 3145752
  4.4 1.3 %shard_map.68 = (f32[64,256]{1,0:T(8,128)}, f32[64,256]{1,0:T(8,128)S(1)}, f32[64,256]{1,0:T(8,128)}) custom-call(f32[3,256,1024]{2,1,0:T(8,128)S(1)} %copy-done, f32[40,1024]{1,0:T(8,128)S(1)} %pad_maximum_fusion.4.coef_ref), custom_call_target="tpu_custom_call" | custom-call | tf_op jit(solution)/shard_map/pallas_call | solution.py:67
  5.6 2.4 %collective-permute-start = (f32[64,256]{1,0:T(8,128)}, f32[64,256]{1,0:T(8,128)S(1)}, u32[]{:S(2)}, u32[]{:S(2)}) collective-permute-start(f32[64,256]{1,0:T(8,128)} %get-tuple-element.16), channel_id=1, source_target_pairs={{0,1},{1,2},{2,3},{3,4},{4,5},{5,6},{6,7},{7,8},{8,9},{9,10},{10,1... | collective-permute-start | bytes 196616 | tf_op jit(solution)/shard_map/ppermute | solution.py:608
  8.0 1.3 %collective-permute-start.1 = (f32[64,256]{1,0:T(8,128)}, f32[64,256]{1,0:T(8,128)S(1)}, u32[]{:S(2)}, u32[]{:S(2)}) collective-permute-start(f32[64,256]{1,0:T(8,128)} %get-tuple-element.17), channel_id=1, source_target_pairs={{1,0},{2,1},{3,2},{4,3},{5,4},{6,5},{7,6},{8,7},{9,8},{10,9},{11,1... | collective-permute-start | bytes 196616 | tf_op jit(solution)/shard_map/ppermute | solution.py:608
  10.3 3.2 %collective-permute-done.1.refs_1_ = f32[64,256]{1,0:T(8,128)S(1)} collective-permute-done((f32[64,256]{1,0:T(8,128)}, f32[64,256]{1,0:T(8,128)S(1)}, u32[]{:S(2)}, u32[]{:S(2)}) %collective-permute-start.1) | collective-permute-done | bytes 65568 | tf_op jit(solution)/shard_map/ppermute | solution.py:608
  13.5 1.2 %pad_maximum_fusion = f32[864,256]{1,0:T(8,128)S(1)} fusion(f32[96,256]{1,0:T(8,128)S(1)} %maximum_select_fusion, f32[768,256]{1,0:T(8,128)} %bitcast.2), kind=kLoop, calls=%fused_computation | loop fusion | flops 221184 | bytes 1769472 | tf_op jit(solution)/shard_map/concatenate | solution.py:629
  14.7 1.7 %collective-permute-start.2 = (f32[864,256]{1,0:T(8,128)S(1)}, f32[864,256]{1,0:T(8,128)S(1)}, u32[]{:S(2)}, u32[]{:S(2)}) collective-permute-start(f32[864,256]{1,0:T(8,128)S(1)} %pad_maximum_fusion), channel_id=1, source_target_pairs={{0,16},{16,0},{1,17},{17,1},{2,18},{18,2},{3,19},{19,3},{4,20},{20... | collective-permute-start | bytes 2654216 | tf_op jit(solution)/shard_map/ppermute | solution.py:602
  16.4 12.0 %shard_map.69 = (f32[3,256,256]{2,1,0:T(8,128)S(1)}, f32[3,256,256]{2,1,0:T(8,128)S(1)}) custom-call(s32[4]{0:T(128)S(1)} %copy-done.3, f32[3,256,1024]{2,1,0:T(8,128)S(1)} %copy-done.1, f32[40,1024]{1,0:T(8,128)S(1)} %pad_maximum_fusion.4.coef_ref, f32[64,256]{1,0:T(8,128)S(1)} %collective-permute-done.refs_0_, f32[64,256]{1,0:T(8,128)S(1)} %collective-permute-done.1.refs_1_), custom_call_target="tpu_custom_call" | custom-call | bytes 42000000 | tf_op jit(solution)/shard_map/pallas_call | solution.py:330
  28.9 14.7 %shard_map.70 = (f32[3,256,512]{2,1,0:T(8,128)S(1)}, f32[256,256]{1,0:T(8,128)S(1)}) custom-call(s32[4]{0:T(128)S(1)} %copy-done.3, f32[3,256,1024]{2,1,0:T(8,128)} %x_ref.5, f32[40,1024]{1,0:T(8,128)S(1)} %pad_maximum_fusion.4.coef_ref, f32[64,256]{1,0:T(8,128)S(1)} %collective-permute-done.refs_0_, f32[64,256]{1,0:T(8,128)S(1)} %collective-permute-done.1.refs_1_, ...), custom_call_target="tpu_custom_call" | custom-call | bytes 42000000 | tf_op jit(solution)/shard_map/pallas_call | solution.py:330
  43.6 7.3 %shard_map.71.raw_ref = f32[3,256,256]{2,1,0:T(8,128)S(1)} custom-call(s32[4]{0:T(128)S(1)} %copy-done.3, f32[864,256]{1,0:T(8,128)S(1)} %collective-permute-done.2.x_ref, f32[40,1024]{1,0:T(8,128)S(1)} %pad_maximum_fusion.4.coef_ref, f32[64,256]{1,0:T(8,128)S(1)} %collective-permute-done.refs_0_, f32[64,256]{1,0:T(8,128)S(1)} %collective-permute-done.1.refs_1_), custom_call_target="tpu_custom_call" | custom-call | bytes 28000000 | tf_op jit(solution)/shard_map/pallas_call | solution.py:330
  53.2 1.9 %collective-permute-start.4 = (f32[128,512]{1,0:T(8,128)S(1)}, f32[128,512]{1,0:T(8,128)S(1)}, u32[]{:S(2)}, u32[]{:S(2)}) collective-permute-start(f32[128,512]{1,0:T(8,128)S(1)} %slice.58), channel_id=1, source_target_pairs={{0,1},{1,0},{2,3},{3,2},{4,5},{5,4},{6,7},{7,6},{8,9},{9,8},{10,11... | collective-permute-start | bytes 786440 | tf_op jit(solution)/shard_map/ppermute | solution.py:589
  55.3 3.3 %collective-permute-start.8 = (f32[3,256,256]{2,1,0:T(8,128)S(1)}, f32[3,256,256]{2,1,0:T(8,128)S(1)}, u32[]{:S(2)}, u32[]{:S(2)}) collective-permute-start(f32[3,256,256]{2,1,0:T(8,128)S(1)} %get-tuple-element.31), channel_id=1, source_target_pairs={{0,16},{1,17},{2,18},{3,19},{4,20},{5,21},{6,22},{7,23},{8,24},{9,... | collective-permute-start | bytes 2359304 | tf_op jit(solution)/shard_map/ppermute | solution.py:648
  58.7 3.0 %collective-permute-start.5 = (f32[64,512]{1,0:T(8,128)S(1)}, f32[64,512]{1,0:T(8,128)S(1)}, u32[]{:S(2)}, u32[]{:S(2)}) collective-permute-start(f32[64,512]{1,0:T(8,128)S(1)} %slice.60), channel_id=1, source_target_pairs={{0,2},{1,3},{2,0},{3,1},{4,6},{5,7},{6,4},{7,5},{8,10},{9,11},{10,... | collective-permute-start | bytes 393224 | tf_op jit(solution)/shard_map/ppermute | solution.py:589
  61.7 3.4 %collective-permute-done.5 = f32[64,512]{1,0:T(8,128)S(1)} collective-permute-done((f32[64,512]{1,0:T(8,128)S(1)}, f32[64,512]{1,0:T(8,128)S(1)}, u32[]{:S(2)}, u32[]{:S(2)}) %collective-permute-start.5) | collective-permute-done | bytes 131104 | tf_op jit(solution)/shard_map/ppermute | solution.py:589
  65.1 3.1 %collective-permute-start.6 = (f32[64,512]{1,0:T(8,128)S(1)}, f32[64,512]{1,0:T(8,128)S(1)}, u32[]{:S(2)}, u32[]{:S(2)}) collective-permute-start(f32[64,512]{1,0:T(8,128)S(1)} %slice_add_fusion.1), channel_id=1, source_target_pairs={{0,4},{1,5},{2,6},{3,7},{4,0},{5,1},{6,2},{7,3},{8,12},{9,13},{10,... | collective-permute-start | bytes 393224 | tf_op jit(solution)/shard_map/ppermute | solution.py:591
  68.2 3.0 %collective-permute-done.6 = f32[64,512]{1,0:T(8,128)S(1)} collective-permute-done((f32[64,512]{1,0:T(8,128)S(1)}, f32[64,512]{1,0:T(8,128)S(1)}, u32[]{:S(2)}, u32[]{:S(2)}) %collective-permute-start.6) | collective-permute-done | bytes 131104 | tf_op jit(solution)/shard_map/ppermute | solution.py:591
  71.3 3.0 %collective-permute-start.7 = (f32[64,512]{1,0:T(8,128)S(1)}, f32[64,512]{1,0:T(8,128)S(1)}, u32[]{:S(2)}, u32[]{:S(2)}) collective-permute-start(f32[64,512]{1,0:T(8,128)S(1)} %add.21), channel_id=1, source_target_pairs={{0,8},{1,9},{2,10},{3,11},{4,12},{5,13},{6,14},{7,15},{8,0},{9,1},... | collective-permute-start | bytes 393224 | tf_op jit(solution)/shard_map/ppermute | solution.py:591
  74.3 4.9 %collective-permute-done.7 = f32[64,512]{1,0:T(8,128)S(1)} collective-permute-done((f32[64,512]{1,0:T(8,128)S(1)}, f32[64,512]{1,0:T(8,128)S(1)}, u32[]{:S(2)}, u32[]{:S(2)}) %collective-permute-start.7) | collective-permute-done | bytes 131104 | tf_op jit(solution)/shard_map/ppermute | solution.py:591
  79.5 4.8 %collective-permute-done.9 = f32[64,512]{1,0:T(8,128)S(1)} collective-permute-done((f32[64,512]{1,0:T(8,128)S(1)}, f32[64,512]{1,0:T(8,128)S(1)}, u32[]{:S(2)}, u32[]{:S(2)}) %collective-permute-start.9) | collective-permute-done | bytes 131104 | tf_op jit(solution)/shard_map/ppermute | solution.py:602
  84.8 3.2 %collective-permute-start.12 = (f32[3,256,256]{2,1,0:T(8,128)S(1)}, f32[3,256,256]{2,1,0:T(8,128)S(1)}, u32[]{:S(2)}, u32[]{:S(2)}) collective-permute-start(f32[3,256,256]{2,1,0:T(8,128)S(1)} %get-tuple-element.28), channel_id=1, source_target_pairs={{0,16},{1,17},{2,18},{3,19},{4,20},{5,21},{6,22},{7,23},{8,24},{9,... | collective-permute-start | bytes 2359304 | tf_op jit(solution)/shard_map/ppermute | solution.py:656
  88.0 2.1 %collective-permute-done.10 = f32[64,768]{1,0:T(8,128)S(1)} collective-permute-done((f32[64,768]{1,0:T(8,128)S(1)}, f32[64,768]{1,0:T(8,128)S(1)}, u32[]{:S(2)}, u32[]{:S(2)}) %collective-permute-start.10) | collective-permute-done | bytes 196640 | tf_op jit(solution)/shard_map/ppermute | solution.py:597
  90.2 1.7 %collective-permute-done.11 = f32[128,768]{1,0:T(8,128)S(1)} collective-permute-done((f32[128,768]{1,0:T(8,128)S(1)}, f32[128,768]{1,0:T(8,128)S(1)}, u32[]{:S(2)}, u32[]{:S(2)}) %collective-permute-start.11) | collective-permute-done | bytes 393248 | tf_op jit(solution)/shard_map/ppermute | solution.py:597
  92.0 14.9 %shard_map.73 = (f32[256,512]{1,0:T(8,128)}, f32[256,256]{1,0:T(8,128)S(1)}, f32[256,256]{1,0:T(8,128)S(1)}) custom-call(f32[256,768]{1,0:T(8,128)S(1)} %pad_maximum_fusion.1.g_ref), custom_call_target="tpu_custom_call" | custom-call | bytes 52500000 | tf_op jit(solution)/shard_map/pallas_call | solution.py:525
  106.9 4.6 %shard_map.74 = f32[3,256,1024]{2,1,0:T(8,128)} custom-call(f32[256,256]{1,0:T(8,128)S(1)} %get-tuple-element.25.own_ref, f32[256,256]{1,0:T(8,128)S(1)} %get-tuple-element.26.other_ref, f32[3,256,256]{2,1,0:T(8,128)S(1)} %get-tuple-element.19.refs_3_.outer_ref, f32[3,256,256]{2,1,0:T(8,128)S(1)} %get-tuple-element.18.refs_2_.inner_ref, ...), custom_call_target="tpu_custom_call" | custom-call | tf_op jit(solution)/shard_map/pallas_call | solution.py:558
  (37 shorter events, 6.7 us)
Async XLA Ops:
  2.5 1.9 %copy-start = (f32[3,256,1024]{2,1,0:T(8,128)S(1)}, f32[3,256,1024]{2,1,0:T(8,128)}, u32[]{:S(2)}) copy-start(f32[3,256,1024]{2,1,0:T(8,128)} %x_ref.5) | copy-start | bytes 9437188
  4.4 4.9 %copy-start.1 = (f32[3,256,1024]{2,1,0:T(8,128)S(1)}, f32[3,256,1024]{2,1,0:T(8,128)}, u32[]{:S(2)}) copy-start(f32[3,256,1024]{2,1,0:T(8,128)} %x_ref.5) | copy-start | bytes 9437188
  4.4 12.0 %copy-start.3 = (s32[4]{0:T(128)S(1)}, s32[4]{0:T(128)}, u32[]{:S(2)}) copy-start(s32[4]{0:T(128)} %off_ref.5) | copy-start | bytes 52
  5.6 4.7 %collective-permute-start = (f32[64,256]{1,0:T(8,128)}, f32[64,256]{1,0:T(8,128)S(1)}, u32[]{:S(2)}, u32[]{:S(2)}) collective-permute-start(f32[64,256]{1,0:T(8,128)} %get-tuple-element.16), channel_id=1, source_target_pairs={{0,1},{1,2},{2,3},{3,4},{4,5},{5,6},{6,7},{7,8},{8,9},{9,10},{10,1... | collective-permute-start | bytes 196616 | tf_op jit(solution)/shard_map/ppermute | solution.py:608
  8.0 5.5 %collective-permute-start.1 = (f32[64,256]{1,0:T(8,128)}, f32[64,256]{1,0:T(8,128)S(1)}, u32[]{:S(2)}, u32[]{:S(2)}) collective-permute-start(f32[64,256]{1,0:T(8,128)} %get-tuple-element.17), channel_id=1, source_target_pairs={{1,0},{2,1},{3,2},{4,3},{5,4},{6,5},{7,6},{8,7},{9,8},{10,9},{11,1... | collective-permute-start | bytes 196616 | tf_op jit(solution)/shard_map/ppermute | solution.py:608
  14.7 28.9 %collective-permute-start.2 = (f32[864,256]{1,0:T(8,128)S(1)}, f32[864,256]{1,0:T(8,128)S(1)}, u32[]{:S(2)}, u32[]{:S(2)}) collective-permute-start(f32[864,256]{1,0:T(8,128)S(1)} %pad_maximum_fusion), channel_id=1, source_target_pairs={{0,16},{16,0},{1,17},{17,1},{2,18},{18,2},{3,19},{19,3},{4,20},{20... | collective-permute-start | bytes 2654216 | tf_op jit(solution)/shard_map/ppermute | solution.py:602
  28.4 23.7 %collective-permute-start.3 = (f32[3,256,256]{2,1,0:T(8,128)S(1)}, f32[3,256,256]{2,1,0:T(8,128)S(1)}, u32[]{:S(2)}, u32[]{:S(2)}) collective-permute-start(f32[3,256,256]{2,1,0:T(8,128)S(1)} %get-tuple-element.18.refs_2_.inner_ref), channel_id=1, source_target_pairs={{0,16},{16,0},{1,17},{17,1},{2,18},{18,2},{3,19},{19,3},{4,20},{20... | collective-permute-start | bytes 2359304 | tf_op jit(solution)/shard_map/ppermute | solution.py:602
  43.6 11.5 %copy-start.2 = (f32[3,256,512]{2,1,0:T(8,128)}, f32[3,256,512]{2,1,0:T(8,128)S(1)}, u32[]{:S(2)}) copy-start(f32[3,256,512]{2,1,0:T(8,128)S(1)} %get-tuple-element.20.own_ref.half_ref) | copy-start | bytes 4718596
  53.2 5.4 %collective-permute-start.4 = (f32[128,512]{1,0:T(8,128)S(1)}, f32[128,512]{1,0:T(8,128)S(1)}, u32[]{:S(2)}, u32[]{:S(2)}) collective-permute-start(f32[128,512]{1,0:T(8,128)S(1)} %slice.58), channel_id=1, source_target_pairs={{0,1},{1,0},{2,3},{3,2},{4,5},{5,4},{6,7},{7,6},{8,9},{9,8},{10,11... | collective-permute-start | bytes 786440 | tf_op jit(solution)/shard_map/ppermute | solution.py:589
  55.3 24.0 %collective-permute-start.8 = (f32[3,256,256]{2,1,0:T(8,128)S(1)}, f32[3,256,256]{2,1,0:T(8,128)S(1)}, u32[]{:S(2)}, u32[]{:S(2)}) collective-permute-start(f32[3,256,256]{2,1,0:T(8,128)S(1)} %get-tuple-element.31), channel_id=1, source_target_pairs={{0,16},{1,17},{2,18},{3,19},{4,20},{5,21},{6,22},{7,23},{8,24},{9,... | collective-permute-start | bytes 2359304 | tf_op jit(solution)/shard_map/ppermute | solution.py:648
  58.7 6.4 %collective-permute-start.5 = (f32[64,512]{1,0:T(8,128)S(1)}, f32[64,512]{1,0:T(8,128)S(1)}, u32[]{:S(2)}, u32[]{:S(2)}) collective-permute-start(f32[64,512]{1,0:T(8,128)S(1)} %slice.60), channel_id=1, source_target_pairs={{0,2},{1,3},{2,0},{3,1},{4,6},{5,7},{6,4},{7,5},{8,10},{9,11},{10,... | collective-permute-start | bytes 393224 | tf_op jit(solution)/shard_map/ppermute | solution.py:589
  65.1 6.2 %collective-permute-start.6 = (f32[64,512]{1,0:T(8,128)S(1)}, f32[64,512]{1,0:T(8,128)S(1)}, u32[]{:S(2)}, u32[]{:S(2)}) collective-permute-start(f32[64,512]{1,0:T(8,128)S(1)} %slice_add_fusion.1), channel_id=1, source_target_pairs={{0,4},{1,5},{2,6},{3,7},{4,0},{5,1},{6,2},{7,3},{8,12},{9,13},{10,... | collective-permute-start | bytes 393224 | tf_op jit(solution)/shard_map/ppermute | solution.py:591
  71.3 7.9 %collective-permute-start.7 = (f32[64,512]{1,0:T(8,128)S(1)}, f32[64,512]{1,0:T(8,128)S(1)}, u32[]{:S(2)}, u32[]{:S(2)}) collective-permute-start(f32[64,512]{1,0:T(8,128)S(1)} %add.21), channel_id=1, source_target_pairs={{0,8},{1,9},{2,10},{3,11},{4,12},{5,13},{6,14},{7,15},{8,0},{9,1},... | collective-permute-start | bytes 393224 | tf_op jit(solution)/shard_map/ppermute | solution.py:591
  79.3 5.0 %collective-permute-start.9 = (f32[64,512]{1,0:T(8,128)S(1)}, f32[64,512]{1,0:T(8,128)S(1)}, u32[]{:S(2)}, u32[]{:S(2)}) collective-permute-start(f32[64,512]{1,0:T(8,128)S(1)} %add.22), channel_id=1, source_target_pairs={{0,16},{16,0},{1,17},{17,1},{2,18},{18,2},{3,19},{19,3},{4,20},{20... | collective-permute-start | bytes 393224 | tf_op jit(solution)/shard_map/ppermute | solution.py:602
  84.4 5.7 %collective-permute-start.10 = (f32[64,768]{1,0:T(8,128)S(1)}, f32[64,768]{1,0:T(8,128)S(1)}, u32[]{:S(2)}, u32[]{:S(2)}) collective-permute-start(f32[64,768]{1,0:T(8,128)S(1)} %pad_maximum_fusion.3), channel_id=1, source_target_pairs={{0,2},{1,3},{2,0},{3,1},{4,6},{5,7},{6,4},{7,5},{8,10},{9,11},{10,... | collective-permute-start | bytes 589832 | tf_op jit(solution)/shard_map/ppermute | solution.py:597
  84.8 22.1 %collective-permute-start.12 = (f32[3,256,256]{2,1,0:T(8,128)S(1)}, f32[3,256,256]{2,1,0:T(8,128)S(1)}, u32[]{:S(2)}, u32[]{:S(2)}) collective-permute-start(f32[3,256,256]{2,1,0:T(8,128)S(1)} %get-tuple-element.28), channel_id=1, source_target_pairs={{0,16},{1,17},{2,18},{3,19},{4,20},{5,21},{6,22},{7,23},{8,24},{9,... | collective-permute-start | bytes 2359304 | tf_op jit(solution)/shard_map/ppermute | solution.py:656
  90.1 1.8 %collective-permute-start.11 = (f32[128,768]{1,0:T(8,128)S(1)}, f32[128,768]{1,0:T(8,128)S(1)}, u32[]{:S(2)}, u32[]{:S(2)}) collective-permute-start(f32[128,768]{1,0:T(8,128)S(1)} %pad_maximum_fusion.2), channel_id=1, source_target_pairs={{0,1},{1,0},{2,3},{3,2},{4,5},{5,4},{6,7},{7,6},{8,9},{9,8},{10,11... | collective-permute-start | bytes 1179656 | tf_op jit(solution)/shard_map/ppermute | solution.py:597

commit v5 on v4

--- a/solution.py
+++ b/solution.py
@@ -27,7 +27,8 @@
 PARAMS = pltpu.CompilerParams(vmem_limit_bytes=48 * 2**20)
 
 
-def pack_kernel(x_ref, coef_ref, low_ref, mid_ref, high_ref, tiles_ref, sems):
+def pack_kernel(x_ref, *refs):
+    given, (low_ref, mid_ref, high_ref, coef_ref, tiles_ref), held, sems = refs[:3], refs[3:8], refs[8:11], refs[11]
     rows, cells = x_ref.shape[1], coef_ref.shape[1]
     blank = jnp.zeros((rows - COEFS, TILE), jnp.float32)
     is_first = lax.axis_index("probe") == 0
@@ -37,10 +38,18 @@
         pltpu.make_async_copy(x_ref.at[:, :, pl.ds(start, TILE)], tiles_ref.at[at], sems.at[at])
         for at, start in enumerate(starts)
     ]
+    copies += [pltpu.make_async_copy(one, two, sems.at[3 + at]) for at, (one, two) in enumerate(zip(given, held))]
     for copy in copies:
         copy.start()
     for copy in copies:
         copy.wait()
+    coup_ref, visc_ref, weight_ref = held
+    for k in range(3):
+        for m in range(3):
+            start = BANDS * (3 * k + m)
+            coef_ref[start : start + BANDS, :] = coup_ref[k, m]
+    coef_ref[TERMS : TERMS + 1, :] = visc_ref[...]
+    coef_ref[TERMS + 1 :, :] = weight_ref[...]
 
     def pack(out_ref, at, spot):
         for comp in range(3):
@@ -61,17 +70,23 @@
         pack(mid_ref, 1, tail)
 
 
-def pack_edges(probes, coefs):
+def pack_edges(probes, coupling, viscosity, misfit_weight):
     _, rows, cells = probes.shape
     edge = jax.ShapeDtypeStruct((4 * HALO, rows), jnp.float32)
     return pl.pallas_call(
         pack_kernel,
-        in_specs=[pl.BlockSpec(memory_space=pltpu.HBM), VMEM],
-        out_specs=[VMEM] * 3,
-        out_shape=[edge] * 3,
-        scratch_shapes=[pltpu.VMEM((3, 3, rows, TILE), jnp.float32), pltpu.SemaphoreType.DMA((3,))],
-        compiler_params=PARAMS,
-    )(probes, coefs)
+        in_specs=[pl.BlockSpec(memory_space=pltpu.HBM)] * 4,
+        out_specs=[VMEM] * 4,
+        out_shape=[edge] * 3 + [jax.ShapeDtypeStruct((COEFS, cells), jnp.float32)],
+        scratch_shapes=[
+            pltpu.VMEM((3, 3, rows, TILE), jnp.float32),
+            pltpu.VMEM((3, 3, BANDS, cells), jnp.float32),
+            pltpu.VMEM((1, cells), jnp.float32),
+            pltpu.VMEM((3, cells), jnp.float32),
+            pltpu.SemaphoreType.DMA((6,)),
+        ],
+        compiler_params=pltpu.CompilerParams(vmem_limit_bytes=60 * 2**20),
+    )(probes, coupling.transpose(1, 2, 0, 3), viscosity[None, :], misfit_weight)
 
 
 def turned(x, amount):
@@ -93,13 +108,11 @@
     return [jnp.where(lane < HALO, turns[i], turns[i + 1]) for i in range(len(tiles) - 1)]
 
 
-def segment_steps(x_at, coef_at, count, off_ref, x_ref, coef_ref, edges, out_refs, scratch):
+def segment_steps(x_at, coef_at, count, inward, off_ref, x_ref, coef_ref, edges, out_refs, scratch):
     rows = edges[0].shape[1]
-    tab_ref, mid_ref, in_ref, ends_ref, *fetched = scratch
-    if fetched:
-        here_ref, sem = fetched
-        fetch = pltpu.make_async_copy(x_ref, here_ref, sem)
-        fetch.start()
+    tab_ref, mid_ref, in_ref, ends_ref, here_ref, sem = scratch
+    fetch = pltpu.make_async_copy(x_ref, here_ref, sem)
+    fetch.start()
     lane = lax.broadcasted_iota(jnp.int32, (8, TILE), 1)
     given = [off_ref[b] for b in range(BANDS)]
     slots = [sum((other < off).astype(jnp.int32) for other in given) for off in given]
@@ -108,14 +121,14 @@
     me = lax.axis_index("probe")
     x_first, coef_first = x_at(me), coef_at(me)
 
-    coef_low_ref, coef_high_ref = edges
+    coef_low_ref, coef_high_ref, *x_ends = edges
     blank = jnp.zeros((TILE - HALO, rows), jnp.float32)
     for comp in range(4):
         start = HALO * comp
         low, high = coef_low_ref[start : start + HALO, :], coef_high_ref[start : start + HALO, :]
-        if comp < 3 and not fetched:
-            start += 3 * rows
-            low, high = x_ref[start : start + HALO, :], x_ref[start + 3 * HALO : start + 4 * HALO, :]
+        if comp < 3 and x_ends:
+            low = x_ends[0][start : start + HALO, :]
+            high = x_ends[0][start + 3 * HALO : start + 4 * HALO, :]
         ends_ref[comp] = jnp.concatenate([blank, low], 0).T
         ends_ref[4 + comp] = jnp.concatenate([high, blank], 0).T
 
@@ -153,8 +166,8 @@
                 continue
             for step in range(4):
                 for i in range(count + 1):
-                    tile = by_step[step, row // 9][i]
-                    tab_ref[step, 9 * slots[row // 9] + row % 9, :, TILE * i : TILE * i + TILE] = jnp.broadcast_to(
+                    tile = by_step[step, row % BANDS][i]
+                    tab_ref[step, 9 * slots[row % BANDS] + row // BANDS, :, TILE * i : TILE * i + TILE] = jnp.broadcast_to(
                         tile[j : j + 1, :], (8, TILE)
                     )
         if group == COEFS // 8 - 1:
@@ -229,9 +242,7 @@
         total = x_ref.shape[-1] // TILE
 
         def load(m, at, where):
-            if fetched:
-                return here_ref[m, spots[at], where]
-            return x_ref[pl.ds(pl.multiple_of(m * rows + 8 * (AT_ONCE * g + at), 8), 8), where]
+            return here_ref[m, spots[at], where]
 
         tiles = [
             [
@@ -252,12 +263,13 @@
                         out_refs[0][m, spot, here] = tiles[at][m][i]
                     else:
                         one, two = tiles[at][m][i], tiles[at][m][count // 2 + i]
-                        out_refs[0][m, spot, here] = jnp.where(me == 0, one, two)
-                        out_refs[1][m, spot, here] = jnp.where(me == 0, two, one)
+                        if inward:
+                            one, two = jnp.where(me == 0, one, two), jnp.where(me == 0, two, one)
+                        out_refs[0][m, spot, here] = one
+                        out_refs[1][m, spot, here] = two
         return carry
 
-    if fetched:
-        fetch.wait()
+    fetch.wait()
     lax.fori_loop(0, rows // (8 * AT_ONCE), group_step, 0)
 
 
@@ -308,28 +320,27 @@
     return main + (mixed + mixed.T)
 
 
-def segment_kernel(x_at, coef_at, count, parts, scale, off_ref, x_ref, coef_ref, *refs):
-    edges, refs = refs[:2], refs[2:]
+def segment_kernel(x_at, coef_at, count, parts, inward, scale, bounds, off_ref, x_ref, coef_ref, *refs):
+    edges, refs = refs[:bounds], refs[bounds:]
     rest, refs = (refs[:2], refs[2:]) if scale else ((), refs)
     out_refs, refs = refs[:parts], refs[parts:]
     gram_ref, refs = (refs[0], refs[1:]) if scale else (None, refs)
-    segment_steps(x_at, coef_at, count, off_ref, x_ref, coef_ref, edges, out_refs, refs)
+    segment_steps(x_at, coef_at, count, inward, off_ref, x_ref, coef_ref, edges, out_refs, refs)
     if scale:
         gram_ref[...] = own_products((*out_refs, *rest)) * scale
 
 
-def segment(x_at, coef_at, count, offsets, x, coefs, edges, parts=1, rest=(), scale=None):
+def segment(x_at, coef_at, count, offsets, x, coefs, edges, ends=None, parts=1, inward=False, rest=(), scale=None):
     rows = edges[0].shape[1]
-    scratch, place = segment_scratch(rows, count), VMEM
-    if x.ndim == 3:
-        place = pl.BlockSpec(memory_space=pltpu.HBM)
-        scratch += [pltpu.VMEM(x.shape, jnp.float32), pltpu.SemaphoreType.DMA(())]
+    scratch = segment_scratch(rows, count) + [pltpu.VMEM(x.shape, jnp.float32), pltpu.SemaphoreType.DMA(())]
+    if ends is not None:
+        edges = (*edges, ends)
     shapes = [jax.ShapeDtypeStruct((3, rows, count * TILE // parts), jnp.float32)] * parts
     if scale:
         shapes.append(jax.ShapeDtypeStruct((rows, rows), jnp.float32))
     result = pl.pallas_call(
-        functools.partial(segment_kernel, x_at, coef_at, count, parts, scale),
-        in_specs=[SMEM, place] + [VMEM] * (1 + len(edges) + len(rest)),
+        functools.partial(segment_kernel, x_at, coef_at, count, parts, inward, scale, len(edges)),
+        in_specs=[SMEM, pl.BlockSpec(memory_space=pltpu.HBM)] + [VMEM] * (1 + len(edges) + len(rest)),
         out_specs=[VMEM] * len(shapes),
         out_shape=shapes,
         scratch_shapes=scratch,
@@ -351,38 +362,35 @@
     return lax.bitwise_xor(lax.rem(lax.axis_index("slab"), count), jnp.int32(reversed_bits(place, count)))
 
 
-def cross_kernel(scale, count, own_ref, raw_ref, ready_ref, gram_ref, out_ref, work):
+def cross_kernel(scale, count, front_ref, back_ref, raw_ref, ready_ref, gram_ref, own_ref, out_ref, work):
     rows = gram_ref.shape[0]
-    quarter = raw_ref.shape[2]
     is_first = lax.axis_index("probe") == 0
 
     @pl.when(is_first)
     def _():
-        near, far = own_ref.at[:, :, :quarter], own_ref.at[:, :, quarter:]
-        work[...] = (products(near, ready_ref) + products(far, raw_ref)) * scale
+        work[...] = (products(front_ref, ready_ref) + products(back_ref, raw_ref)) * scale
 
     @pl.when(jnp.logical_not(is_first))
     def _():
-        near, far = own_ref.at[:, :, :quarter], own_ref.at[:, :, quarter:]
-        work[...] = (products(raw_ref, near) + products(ready_ref, far)) * scale
+        work[...] = (products(raw_ref, front_ref) + products(ready_ref, back_ref)) * scale
 
     share = rows // count
     for place in range(count):
         spot = pl.ds(pl.multiple_of(block_at(place, count) * share, share), share)
-        out_ref[share * place : share * place + share, :rows] = gram_ref[spot, :]
-        out_ref[share * place : share * place + share, rows:] = work[spot, :]
-
-
-def cross_of(own, raw, ready, gram, scale, count):
-    _, rows, _ = own.shape
+        own_ref[share * place : share * place + share, :] = gram_ref[spot, :]
+        out_ref[share * place : share * place + share, :] = work[spot, :]
+
+
+def cross_of(front, back, raw, ready, gram, scale, count):
+    rows = gram.shape[0]
     return pl.pallas_call(
         functools.partial(cross_kernel, scale, count),
-        in_specs=[VMEM] * 4,
-        out_specs=VMEM,
-        out_shape=jax.ShapeDtypeStruct((rows, 2 * rows), jnp.float32),
+        in_specs=[VMEM] * 5,
+        out_specs=[VMEM] * 2,
+        out_shape=[jax.ShapeDtypeStruct((rows, rows), jnp.float32)] * 2,
         scratch_shapes=[pltpu.VMEM((rows, rows), jnp.float32)],
         compiler_params=PARAMS,
-    )(own, raw, ready, gram)
+    )(front, back, raw, ready, gram)
 
 
 def over_lanes(x, j):
@@ -398,7 +406,6 @@
     rows = lax.broadcasted_iota(jnp.int32, (8, TILE), 0)
     lanes = lax.broadcasted_iota(jnp.int32, (8, TILE), 1)
     a = [a_ref[8 * t : 8 * t + 8, :] for t in range(blocks)]
-    e = [jnp.where(lanes == rows + 8 * t, 1.0, 0.0) for t in range(blocks)]
 
     def repeated(t, s):
         return [over_lanes(a[t], 8 * s + j) for j in range(8)]
@@ -409,7 +416,7 @@
         early = range(s + 1, min(s + 1 + EARLY, blocks))
         ready = {t: repeated(t, s + 1) for t in early}
         upper = [over_rows(a[s], k) for k in range(8)]
-        side = [over_rows(e[s], k) for k in range(8)]
+        side = [jnp.where(lanes < 8 * s, upper[k], jnp.where(lanes == 8 * s + k, 1.0, 0.0)) for k in range(8)]
         for k in range(8):
             pivot = lax.rsqrt(over_rows(columns[s][k], k))
             for t in range(s, blocks):
@@ -427,10 +434,12 @@
                     factor = over_rows(columns[s + 1][k], j)
                     for t in early:
                         ready[t][j] = ready[t][j] - columns[t][k] * factor
+        done = lanes < 8 * s + 8
+        both = [jnp.where(done, side[k], upper[k]) for k in range(8)]
         for t in range(s + 1, blocks):
+            a[t] = jnp.where((lanes < 8 * s) | (lanes >= 8 * s + 8), a[t], 0.0)
             for k in range(8):
-                a[t] = a[t] - columns[t][k] * upper[k]
-                e[t] = e[t] - columns[t][k] * side[k]
+                a[t] = a[t] - columns[t][k] * both[k]
         for k in range(1, 8):
             upper[0] = jnp.where(rows >= k, upper[k], upper[0])
             side[0] = jnp.where(rows >= k, side[k], side[0])
@@ -533,13 +542,13 @@
     )(travelled)
 
 
-def basis_kernel(own_ref, other_ref, outer_ref, inner_ref, half_ref, raw_ref, ready_ref, early_ref, late_ref, out_ref):
+def basis_kernel(own_ref, other_ref, outer_ref, inner_ref, front_ref, back_ref, raw_ref, ready_ref, early_ref, late_ref, out_ref):
     me = lax.axis_index("probe")
     quarter = outer_ref.shape[2]
     own = pieces(own_ref[...])
-    starts = (me * 3 * quarter, (1 + me) * quarter, (1 - me) * 2 * quarter)
-    for start, ref in zip(starts, (outer_ref, inner_ref, half_ref)):
-        spot = pl.ds(pl.multiple_of(start, TILE), ref.shape[2])
+    places = (me * 3, 1 + me, (1 - me) * 2, (1 - me) * 2 + 1)
+    for place, ref in zip(places, (outer_ref, inner_ref, front_ref, back_ref)):
+        spot = pl.ds(pl.multiple_of(place * quarter, TILE), quarter)
         out_ref[0, :, spot] = close_dot(own, pieces(ref[0]), PLAIN)
 
     @pl.when(me == 1)
@@ -550,19 +559,18 @@
             out_ref[0, :, spot] = out_ref[0, :, spot] + close_dot(other, pieces(ref[0]), PLAIN)
 
 
-def basis_of(own, other, outer, inner, half, raw, ready, early, late):
-    _, rows, quarter = outer.shape
+def basis_of(own, other, *panels):
+    _, rows, quarter = panels[0].shape
     weights = pl.BlockSpec((rows, rows), lambda k: (0, 0))
-    short = pl.BlockSpec((1, rows, quarter), lambda k: (k, 0, 0))
-    wide = pl.BlockSpec((1, rows, 2 * quarter), lambda k: (k, 0, 0))
+    panel = pl.BlockSpec((1, rows, quarter), lambda k: (k, 0, 0))
     return pl.pallas_call(
         basis_kernel,
         grid=(3,),
-        in_specs=[weights, weights, short, short, wide, short, short, short, short],
+        in_specs=[weights] * 2 + [panel] * len(panels),
         out_specs=pl.BlockSpec((1, rows, 4 * quarter), lambda k: (k, 0, 0)),
         out_shape=jax.ShapeDtypeStruct((3, rows, 4 * quarter), jnp.float32),
         compiler_params=PARAMS,
-    )(own, other, outer, inner, half, raw, ready, early, late)
+    )(own, other, *panels)
 
 
 def partners(axis, bit):
@@ -608,7 +616,7 @@
     return lax.ppermute(last, "slab", forward), lax.ppermute(first, "slab", [(b, a) for a, b in forward])
 
 
-def pair_body(probes, coefs, offsets):
+def pair_body(probes, coefs, first, mid, last, offsets):
     _, columns, cells = probes.shape
     slabs = lax.axis_size("slab")
     scale = 1.0 / (3 * cells * slabs)
@@ -617,16 +625,16 @@
     quarter = cells // 4
     tiles = quarter // TILE
 
-    first, mid, last = pack_edges(probes, coefs)
     low, high = halo_of(first, last)
     pack = 3 * HALO
-    ends = jnp.where(
-        is_first,
-        jnp.concatenate([low[:pack], mid[:pack]], 0),
-        jnp.concatenate([mid[:pack], high[:pack]], 0),
+    ends = swapped(
+        jnp.where(
+            is_first,
+            jnp.concatenate([low[:pack], mid[:pack]], 0),
+            jnp.concatenate([mid[:pack], high[:pack]], 0),
+        )
     )
-    sent = lax.dynamic_slice_in_dim(probes, me * 3 * quarter, quarter, 2).reshape(3 * columns, quarter)
-    theirs = swapped(jnp.concatenate([sent, ends], 0))
+    theirs = swapped(lax.dynamic_slice_in_dim(probes, me * 3 * quarter, quarter, 2))
     run = functools.partial(segment, offsets=offsets, coefs=coefs)
 
     def at_half(me):
@@ -639,39 +647,33 @@
         return (1 - me) * 3 * tiles
 
     edges = (low, high)
-    outer, inner = run(at_half, at_half, 2 * tiles, x=probes, edges=edges, parts=2)
+    outer, inner = run(at_half, at_half, 2 * tiles, x=probes, edges=edges, parts=2, inward=True)
+    inner, ends = lax.optimization_barrier((inner, ends))
     ready = swapped(inner)
-    half, gram = run(
-        at_other_half, at_other_half, 2 * tiles, x=probes, edges=edges, rest=(inner, outer), scale=scale
+    front, back, gram = run(
+        at_other_half, at_other_half, 2 * tiles, x=probes, edges=edges, parts=2, rest=(inner, outer), scale=scale
     )
-    rest = (half[:, :, :quarter], half[:, :, quarter:])
-    early = lax.ppermute(rest[0], "probe", [(0, 1)])
-    raw = run(lambda me: 0, at_raw, tiles, x=theirs, edges=edges)
+    early = swapped(front)
+    raw = run(lambda me: 0, at_raw, tiles, x=theirs, edges=edges, ends=ends)
     count = 1 << len(split_bits("slab")[0])
-    sums = cross_of(half, raw, ready, gram, scale, count)
-    share = scatter_sum(sums, "slab")
-    share, early = lax.optimization_barrier((share, early))
-    other = swapped(share)
-    other, late = lax.optimization_barrier((other, rest[1]))
-    late = lax.ppermute(late, "probe", [(0, 1)])
+    own, cross = cross_of(front, back, raw, ready, gram, scale, count)
+    own, cross = scatter_sum(own, "slab"), scatter_sum(cross, "slab")
+    own, cross, early = lax.optimization_barrier((own, cross, early))
+    their_own, their_cross = swapped(own), swapped(cross)
+    their_own, their_cross, late = lax.optimization_barrier((their_own, their_cross, back))
+    late = swapped(late)
     share = jnp.concatenate(
-        [
-            jnp.where(is_first, share[:, :columns], other[:, :columns]),
-            share[:, columns:] + other[:, columns:],
-            jnp.where(is_first, other[:, :columns], share[:, :columns]),
-        ],
-        1,
+        [jnp.where(is_first, own, their_own), cross + their_cross, jnp.where(is_first, their_own, own)], 1
     )
     r_rows, own, other = factorize_pair(gather_back(share, "slab"), count)
-    return basis_of(own, other, outer, inner, half, raw, ready, early, late), r_rows
-
-
-def whole_body(probes, coefs, offsets):
+    return basis_of(own, other, outer, inner, front, back, raw, ready, early, late), r_rows
+
+
+def whole_body(probes, coefs, first, mid, last, offsets):
     _, columns, cells = probes.shape
     slabs = lax.axis_size("slab")
     me = lax.axis_index("probe")
     scale = 1.0 / (3 * cells * slabs)
-    first, _, last = pack_edges(probes, coefs)
     low, high = halo_of(first, last)
     panel = segment(lambda me: 0, lambda me: 0, cells // TILE, offsets, probes, coefs, (low, high))
     everyone = lax.all_gather(panel, "probe", axis=1, tiled=True)
@@ -684,9 +686,9 @@
 
 
 def body(probes, viscosity, coupling, misfit_weight, band_offsets):
-    coefs = jnp.concatenate([coupling.reshape(TERMS, -1), viscosity[None, :], misfit_weight], 0)
+    first, mid, last, coefs = pack_edges(probes, coupling, viscosity, misfit_weight)
     run = pair_body if lax.axis_size("probe") == 2 else whole_body
-    return run(probes, coefs, band_offsets)
+    return run(probes, coefs, first, mid, last, band_offsets)
 
 
 def solution(mesh):

time: 112 us -> 107 us (0.955)
  waiting for transfers between devices: 24.4 us -> 18.2 us
  starting transfers between devices: 24.1 us -> 27 us
  other arithmetic: 2.15 us -> 0.22 us
  local copies, waits for them, and re-layouts: 4.14 us -> 2.74 us
    ppermute x2 -> x0, starting transfers between devices: 6.5 us -> none  [the longest x1 3.35 us: pair_body(): early = lax.ppermute(rest[0], 'probe', [(0, 1)])]
    ppermute x3 -> x7, starting transfers between devices: 2.41 us -> 7.59 us  [swapped(): return lax.ppermute(block, 'probe', [(0, 1), (1, 0)])]
    ppermute x2 -> x4, waiting for transfers between devices: 7.99 us -> 4.86 us  [scatter_sum(): block = block + lax.ppermute(block, axis, partners(axis, bit))]
    ppermute x3 -> x7, waiting for transfers between devices: 5.93 us -> 3.59 us  [swapped(): return lax.ppermute(block, 'probe', [(0, 1), (1, 0)])]
    concatenate x3 -> x1, other arithmetic: 1.95 us -> 0.02 us  [pair_body(): jnp.concatenate([jnp.where(is_first, own, their_own), cross + their_cross...]
    ppermute x2, starting transfers between devices: 0.52 us -> 2.35 us  [gather_back(): lax.ppermute(block, axis, partners(axis, bit))]
    ppermute x2 -> x4, starting transfers between devices: 6.12 us -> 7.92 us  [scatter_sum(): block = block + lax.ppermute(block, axis, partners(axis, bit))]
    pallas_call x1, Pallas kernels: 1.25 us -> 2.64 us  [pack_edges(): pl.pallas_call(pack_kernel, in_specs=[pl.BlockSpec(memory_space=pltpu.HBM...]
  transfers between devices with their start and end apart: 13 -> 19, of which waited for: 8 -> 12; matrix products, arithmetic and copies ran while one was open for 1% -> 1% of each run, Pallas kernels for 44% -> 46%
where the time goes in v5:
time: 107 us; the launch traced here: 106 us
  Pallas kernels  57 us (53%)
  starting transfers between devices  27 us (25%)
  waiting for transfers between devices  18.2 us (17%)
  local copies, waits for them, and re-layouts  2.74 us (3%)
    pallas_call x3, Pallas kernels, segment(): pl.pallas_call(functools.partial(segment_kernel, x_at, coef_at, count, pa...  34.5 us
    pallas_call x1, Pallas kernels, factorize_pair(): pl.pallas_call(functools.partial(pair_kernel, count), in_specs=[VMEM], ou...  14.4 us
    ppermute x4, starting transfers between devices, scatter_sum(): block = block + lax.ppermute(block, axis, partners(axis, bit))  7.92 us
    ppermute x7, starting transfers between devices, swapped(): return lax.ppermute(block, 'probe', [(0, 1), (1, 0)])  7.59 us
    ppermute x4, starting transfers between devices, scatter_sum(): block = block[:half] + lax.ppermute(block[half:], axis, partners(axis, bit))  5.54 us
    ppermute x4, waiting for transfers between devices, scatter_sum(): block = block + lax.ppermute(block, axis, partners(axis, bit))  4.86 us
    pallas_call x1, Pallas kernels, basis_of(): pl.pallas_call(basis_kernel, grid=(3,), in_specs=[weights] * 2 + [panel]...  4.27 us
    ppermute x2, waiting for transfers between devices, gather_back(): lax.ppermute(block, axis, partners(axis, bit))  4.03 us
  transfers between devices with their start and end apart: 19, of which 12 were waited for; matrix products, arithmetic and copies ran while one was open for 1% of the time, Pallas kernels for 46%

profile of v5, /device:TPU:0, one launch (start us, length us, event | category | flops | bytes accessed | tf_op | source)
XLA Modules:
  0.0 106.0 jit_solution(1277201940081161813)
XLA Ops:
  0.7 2.6 %shard_map.68 = (f32[64,256]{1,0:T(8,128)}, f32[64,256]{1,0:T(8,128)}, f32[64,256]{1,0:T(8,128)}, f32[40,1024]{1,0:T(8,128)}) custom-call(f32[3,256,1024]{2,1,0:T(8,128)} %x_ref.5, f32[3,3,4,1024]{3,2,1,0:T(4,128)} %bitcast.2, f32[1,1024]{1,0:T(1,128)} %bitcast.3, f32[3,1024]{1,0:T(4,128)} %refs_2_.1), custom_call_target="tpu_custom_call" | custom-call | tf_op jit(solution)/shard_map/pallas_call | solution.py:76
  3.3 2.4 %collective-permute-start = (f32[64,256]{1,0:T(8,128)}, f32[64,256]{1,0:T(8,128)S(1)}, u32[]{:S(2)}, u32[]{:S(2)}) collective-permute-start(f32[64,256]{1,0:T(8,128)} %get-tuple-element.25), channel_id=1, source_target_pairs={{0,1},{1,2},{2,3},{3,4},{4,5},{5,6},{6,7},{7,8},{8,9},{9,10},{10,1... | collective-permute-start | bytes 196616 | tf_op jit(solution)/shard_map/ppermute | solution.py:616
  7.8 3.4 %collective-permute-done.1.refs_1_ = f32[64,256]{1,0:T(8,128)S(1)} collective-permute-done((f32[64,256]{1,0:T(8,128)}, f32[64,256]{1,0:T(8,128)S(1)}, u32[]{:S(2)}, u32[]{:S(2)}) %collective-permute-start.1) | collective-permute-done | bytes 65568 | tf_op jit(solution)/shard_map/ppermute | solution.py:616
  11.2 1.7 %collective-permute-start.2 = (f32[96,256]{1,0:T(8,128)S(1)}, f32[96,256]{1,0:T(8,128)S(1)}, u32[]{:S(2)}, u32[]{:S(2)}) collective-permute-start(f32[96,256]{1,0:T(8,128)S(1)} %maximum_select_fusion), channel_id=1, source_target_pairs={{0,16},{16,0},{1,17},{17,1},{2,18},{18,2},{3,19},{19,3},{4,20},{20... | collective-permute-start | bytes 294920 | tf_op jit(solution)/shard_map/ppermute | solution.py:610
  14.3 12.2 %shard_map.69 = (f32[3,256,256]{2,1,0:T(8,128)S(1)}, f32[3,256,256]{2,1,0:T(8,128)S(1)}) custom-call(s32[4]{0:T(128)S(1)} %copy-done.2, f32[3,256,1024]{2,1,0:T(8,128)S(1)} %copy-done, f32[40,1024]{1,0:T(8,128)S(1)} %copy-done.1, f32[64,256]{1,0:T(8,128)S(1)} %collective-permute-done.refs_0_, f32[64,256]{1,0:T(8,128)S(1)} %collective-permute-done.1.refs_1_), custom_call_target="tpu_custom_call" | custom-call | bytes 42000000 | tf_op jit(solution)/shard_map/pallas_call | solution.py:341
  26.6 1.7 %collective-permute-start.4 = (f32[3,256,256]{2,1,0:T(8,128)S(1)}, f32[3,256,256]{2,1,0:T(8,128)S(1)}, u32[]{:S(2)}, u32[]{:S(2)}) collective-permute-start(f32[3,256,256]{2,1,0:T(8,128)S(1)} %get-tuple-element.29.refs_2_.inner_ref), channel_id=1, source_target_pairs={{0,16},{16,0},{1,17},{17,1},{2,18},{18,2},{3,19},{19,3},{4,20},{20... | collective-permute-start | bytes 2359304 | tf_op jit(solution)/shard_map/ppermute | solution.py:610
  28.2 14.8 %shard_map.70 = (f32[3,256,256]{2,1,0:T(8,128)S(1)}, f32[3,256,256]{2,1,0:T(8,128)S(1)}, f32[256,256]{1,0:T(8,128)S(1)}) custom-call(s32[4]{0:T(128)S(1)} %copy-done.2, f32[3,256,1024]{2,1,0:T(8,128)} %x_ref.5, f32[40,1024]{1,0:T(8,128)S(1)} %copy-done.1, f32[64,256]{1,0:T(8,128)S(1)} %collective-permute-done.refs_0_, ...), custom_call_target="tpu_custom_call" | custom-call | bytes 42000000 | tf_op jit(solution)/shard_map/pallas_call | solution.py:341
  43.0 7.5 %shard_map.71.raw_ref = f32[3,256,256]{2,1,0:T(8,128)S(1)} custom-call(s32[4]{0:T(128)S(1)} %copy-done.2, f32[3,256,256]{2,1,0:T(8,128)S(1)} %collective-permute-done.3.x_ref, f32[40,1024]{1,0:T(8,128)S(1)} %copy-done.1, f32[64,256]{1,0:T(8,128)S(1)} %collective-permute-done.refs_0_, f32[64,256]{1,0:T(8,128)S(1)} %collective-permute-done.1.refs_1_, ...), custom_call_target="tpu_custom_call" | custom-call | bytes 28000000 | tf_op jit(solution)/shard_map/pallas_call | solution.py:341
  51.7 2.2 %collective-permute-start.9 = (f32[128,256]{1,0:T(8,128)S(1)}, f32[128,256]{1,0:T(8,128)S(1)}, u32[]{:S(2)}, u32[]{:S(2)}) collective-permute-start(f32[128,256]{1,0:T(8,128)S(1)} %slice.42), channel_id=1, source_target_pairs={{0,1},{1,0},{2,3},{3,2},{4,5},{5,4},{6,7},{7,6},{8,9},{9,8},{10,11... | collective-permute-start | bytes 393224 | tf_op jit(solution)/shard_map/ppermute | solution.py:597
  54.9 2.5 %collective-permute-start.10 = (f32[64,256]{1,0:T(8,128)S(1)}, f32[64,256]{1,0:T(8,128)S(1)}, u32[]{:S(2)}, u32[]{:S(2)}) collective-permute-start(f32[64,256]{1,0:T(8,128)S(1)} %slice.50), channel_id=1, source_target_pairs={{0,2},{1,3},{2,0},{3,1},{4,6},{5,7},{6,4},{7,5},{8,10},{9,11},{10,... | collective-permute-start | bytes 196616 | tf_op jit(solution)/shard_map/ppermute | solution.py:597
  58.2 1.8 %collective-permute-done.10 = f32[64,256]{1,0:T(8,128)S(1)} collective-permute-done((f32[64,256]{1,0:T(8,128)S(1)}, f32[64,256]{1,0:T(8,128)S(1)}, u32[]{:S(2)}, u32[]{:S(2)}) %collective-permute-start.10) | collective-permute-done | bytes 65568 | tf_op jit(solution)/shard_map/ppermute | solution.py:597
  60.0 1.6 %collective-permute-start.11 = (f32[64,256]{1,0:T(8,128)S(1)}, f32[64,256]{1,0:T(8,128)S(1)}, u32[]{:S(2)}, u32[]{:S(2)}) collective-permute-start(f32[64,256]{1,0:T(8,128)S(1)} %slice_add_fusion.2), channel_id=1, source_target_pairs={{0,4},{1,5},{2,6},{3,7},{4,0},{5,1},{6,2},{7,3},{8,12},{9,13},{10,... | collective-permute-start | bytes 196616 | tf_op jit(solution)/shard_map/ppermute | solution.py:599
  61.7 1.6 %collective-permute-start.7 = (f32[64,256]{1,0:T(8,128)S(1)}, f32[64,256]{1,0:T(8,128)S(1)}, u32[]{:S(2)}, u32[]{:S(2)}) collective-permute-start(f32[64,256]{1,0:T(8,128)S(1)} %slice_add_fusion.3), channel_id=1, source_target_pairs={{0,4},{1,5},{2,6},{3,7},{4,0},{5,1},{6,2},{7,3},{8,12},{9,13},{10,... | collective-permute-start | bytes 196616 | tf_op jit(solution)/shard_map/ppermute | solution.py:599
  63.4 1.6 %collective-permute-done.11 = f32[64,256]{1,0:T(8,128)S(1)} collective-permute-done((f32[64,256]{1,0:T(8,128)S(1)}, f32[64,256]{1,0:T(8,128)S(1)}, u32[]{:S(2)}, u32[]{:S(2)}) %collective-permute-start.11) | collective-permute-done | bytes 65568 | tf_op jit(solution)/shard_map/ppermute | solution.py:599
  65.0 2.7 %collective-permute-start.12 = (f32[64,256]{1,0:T(8,128)S(1)}, f32[64,256]{1,0:T(8,128)S(1)}, u32[]{:S(2)}, u32[]{:S(2)}) collective-permute-start(f32[64,256]{1,0:T(8,128)S(1)} %add.37), channel_id=1, source_target_pairs={{0,8},{1,9},{2,10},{3,11},{4,12},{5,13},{6,14},{7,15},{8,0},{9,1},... | collective-permute-start | bytes 196616 | tf_op jit(solution)/shard_map/ppermute | solution.py:599
  67.7 2.0 %collective-permute-start.8 = (f32[64,256]{1,0:T(8,128)S(1)}, f32[64,256]{1,0:T(8,128)S(1)}, u32[]{:S(2)}, u32[]{:S(2)}) collective-permute-start(f32[64,256]{1,0:T(8,128)S(1)} %add.33), channel_id=1, source_target_pairs={{0,8},{1,9},{2,10},{3,11},{4,12},{5,13},{6,14},{7,15},{8,0},{9,1},... | collective-permute-start | bytes 196616 | tf_op jit(solution)/shard_map/ppermute | solution.py:599
  69.7 2.2 %collective-permute-done.12 = f32[64,256]{1,0:T(8,128)S(1)} collective-permute-done((f32[64,256]{1,0:T(8,128)S(1)}, f32[64,256]{1,0:T(8,128)S(1)}, u32[]{:S(2)}, u32[]{:S(2)}) %collective-permute-start.12) | collective-permute-done | bytes 65568 | tf_op jit(solution)/shard_map/ppermute | solution.py:599
  75.4 2.2 %collective-permute-done.14 = f32[64,256]{1,0:T(8,128)S(1)} collective-permute-done((f32[64,256]{1,0:T(8,128)S(1)}, f32[64,256]{1,0:T(8,128)S(1)}, u32[]{:S(2)}, u32[]{:S(2)}) %collective-permute-start.14) | collective-permute-done | bytes 65568 | tf_op jit(solution)/shard_map/ppermute | solution.py:610
  78.6 2.3 %collective-permute-start.16 = (f32[64,768]{1,0:T(8,128)S(1)}, f32[64,768]{1,0:T(8,128)S(1)}, u32[]{:S(2)}, u32[]{:S(2)}) collective-permute-start(f32[64,768]{1,0:T(8,128)S(1)} %pad_maximum_fusion.2), channel_id=1, source_target_pairs={{0,2},{1,3},{2,0},{3,1},{4,6},{5,7},{6,4},{7,5},{8,10},{9,11},{10,... | collective-permute-start | bytes 589832 | tf_op jit(solution)/shard_map/ppermute | solution.py:605
  80.9 1.3 %collective-permute-start.18 = (f32[3,256,256]{2,1,0:T(8,128)S(1)}, f32[3,256,256]{2,1,0:T(8,128)S(1)}, u32[]{:S(2)}, u32[]{:S(2)}) collective-permute-start(f32[3,256,256]{2,1,0:T(8,128)S(1)} %get-tuple-element.44.back_ref), channel_id=1, source_target_pairs={{0,16},{16,0},{1,17},{17,1},{2,18},{18,2},{3,19},{19,3},{4,20},{20... | collective-permute-start | bytes 2359304 | tf_op jit(solution)/shard_map/ppermute | solution.py:610
  82.2 2.3 %collective-permute-done.16 = f32[64,768]{1,0:T(8,128)S(1)} collective-permute-done((f32[64,768]{1,0:T(8,128)S(1)}, f32[64,768]{1,0:T(8,128)S(1)}, u32[]{:S(2)}, u32[]{:S(2)}) %collective-permute-start.16) | collective-permute-done | bytes 196640 | tf_op jit(solution)/shard_map/ppermute | solution.py:605
  84.6 1.7 %collective-permute-done.17 = f32[128,768]{1,0:T(8,128)S(1)} collective-permute-done((f32[128,768]{1,0:T(8,128)S(1)}, f32[128,768]{1,0:T(8,128)S(1)}, u32[]{:S(2)}, u32[]{:S(2)}) %collective-permute-start.17) | collective-permute-done | bytes 393248 | tf_op jit(solution)/shard_map/ppermute | solution.py:605
  86.4 14.4 %shard_map.73 = (f32[256,512]{1,0:T(8,128)}, f32[256,256]{1,0:T(8,128)S(1)}, f32[256,256]{1,0:T(8,128)S(1)}) custom-call(f32[256,768]{1,0:T(8,128)S(1)} %pad_maximum_fusion.g_ref), custom_call_target="tpu_custom_call" | custom-call | bytes 52500000 | tf_op jit(solution)/shard_map/pallas_call | solution.py:534
  101.7 4.3 %shard_map.74 = f32[3,256,1024]{2,1,0:T(8,128)} custom-call(f32[256,256]{1,0:T(8,128)S(1)} %get-tuple-element.41.own_ref, f32[256,256]{1,0:T(8,128)S(1)} %get-tuple-element.42.other_ref, f32[3,256,256]{2,1,0:T(8,128)S(1)} %get-tuple-element.30.refs_3_.outer_ref, f32[3,256,256]{2,1,0:T(8,128)S(1)} %get-tuple-element.29.refs_2_.inner_ref, ...), custom_call_target="tpu_custom_call" | custom-call | tf_op jit(solution)/shard_map/pallas_call | solution.py:566
  (51 shorter events, 12.2 us)
Async XLA Ops:
  0.6 12.2 %copy-start = (f32[3,256,1024]{2,1,0:T(8,128)S(1)}, f32[3,256,1024]{2,1,0:T(8,128)}, u32[]{:S(2)}) copy-start(f32[3,256,1024]{2,1,0:T(8,128)} %x_ref.5) | copy-start | bytes 9437188
  0.6 12.8 %copy-start.2 = (s32[4]{0:T(128)S(1)}, s32[4]{0:T(128)}, u32[]{:S(2)}) copy-start(s32[4]{0:T(128)} %off_ref.5) | copy-start | bytes 52
  3.3 4.5 %collective-permute-start = (f32[64,256]{1,0:T(8,128)}, f32[64,256]{1,0:T(8,128)S(1)}, u32[]{:S(2)}, u32[]{:S(2)}) collective-permute-start(f32[64,256]{1,0:T(8,128)} %get-tuple-element.25), channel_id=1, source_target_pairs={{0,1},{1,2},{2,3},{3,4},{4,5},{5,6},{6,7},{7,8},{8,9},{9,10},{10,1... | collective-permute-start | bytes 196616 | tf_op jit(solution)/shard_map/ppermute | solution.py:616
  5.7 5.5 %collective-permute-start.1 = (f32[64,256]{1,0:T(8,128)}, f32[64,256]{1,0:T(8,128)S(1)}, u32[]{:S(2)}, u32[]{:S(2)}) collective-permute-start(f32[64,256]{1,0:T(8,128)} %get-tuple-element.26), channel_id=1, source_target_pairs={{1,0},{2,1},{3,2},{4,3},{5,4},{6,5},{7,6},{8,7},{9,8},{10,9},{11,1... | collective-permute-start | bytes 196616 | tf_op jit(solution)/shard_map/ppermute | solution.py:616
  11.2 15.4 %collective-permute-start.2 = (f32[96,256]{1,0:T(8,128)S(1)}, f32[96,256]{1,0:T(8,128)S(1)}, u32[]{:S(2)}, u32[]{:S(2)}) collective-permute-start(f32[96,256]{1,0:T(8,128)S(1)} %maximum_select_fusion), channel_id=1, source_target_pairs={{0,16},{16,0},{1,17},{17,1},{2,18},{18,2},{3,19},{19,3},{4,20},{20... | collective-permute-start | bytes 294920 | tf_op jit(solution)/shard_map/ppermute | solution.py:610
  12.9 30.1 %collective-permute-start.3 = (f32[3,256,256]{2,1,0:T(8,128)S(1)}, f32[3,256,256]{2,1,0:T(8,128)S(1)}, u32[]{:S(2)}, u32[]{:S(2)}) collective-permute-start(f32[3,256,256]{2,1,0:T(8,128)S(1)} %constant_dynamic-slice_fusion), channel_id=1, source_target_pairs={{0,16},{16,0},{1,17},{17,1},{2,18},{18,2},{3,19},{19,3},{4,20},{20... | collective-permute-start | bytes 2359304 | tf_op jit(solution)/shard_map/ppermute | solution.py:610
  13.4 0.9 copy-start.1
  26.6 24.0 %collective-permute-start.4 = (f32[3,256,256]{2,1,0:T(8,128)S(1)}, f32[3,256,256]{2,1,0:T(8,128)S(1)}, u32[]{:S(2)}, u32[]{:S(2)}) collective-permute-start(f32[3,256,256]{2,1,0:T(8,128)S(1)} %get-tuple-element.29.refs_2_.inner_ref), channel_id=1, source_target_pairs={{0,16},{16,0},{1,17},{17,1},{2,18},{18,2},{3,19},{19,3},{4,20},{20... | collective-permute-start | bytes 2359304 | tf_op jit(solution)/shard_map/ppermute | solution.py:610
  51.7 3.1 %collective-permute-start.9 = (f32[128,256]{1,0:T(8,128)S(1)}, f32[128,256]{1,0:T(8,128)S(1)}, u32[]{:S(2)}, u32[]{:S(2)}) collective-permute-start(f32[128,256]{1,0:T(8,128)S(1)} %slice.42), channel_id=1, source_target_pairs={{0,1},{1,0},{2,3},{3,2},{4,5},{5,4},{6,7},{7,6},{8,9},{9,8},{10,11... | collective-permute-start | bytes 393224 | tf_op jit(solution)/shard_map/ppermute | solution.py:597
  53.8 19.5 %collective-permute-start.13 = (f32[3,256,256]{2,1,0:T(8,128)S(1)}, f32[3,256,256]{2,1,0:T(8,128)S(1)}, u32[]{:S(2)}, u32[]{:S(2)}) collective-permute-start(f32[3,256,256]{2,1,0:T(8,128)S(1)} %get-tuple-element.31.front_ref), channel_id=1, source_target_pairs={{0,16},{16,0},{1,17},{17,1},{2,18},{18,2},{3,19},{19,3},{4,20},{20... | collective-permute-start | bytes 2359304 | tf_op jit(solution)/shard_map/ppermute | solution.py:610
  54.3 3.1 %collective-permute-start.5 = (f32[128,256]{1,0:T(8,128)S(1)}, f32[128,256]{1,0:T(8,128)S(1)}, u32[]{:S(2)}, u32[]{:S(2)}) collective-permute-start(f32[128,256]{1,0:T(8,128)S(1)} %slice.38), channel_id=1, source_target_pairs={{0,1},{1,0},{2,3},{3,2},{4,5},{5,4},{6,7},{7,6},{8,9},{9,8},{10,11... | collective-permute-start | bytes 393224 | tf_op jit(solution)/shard_map/ppermute | solution.py:597
  54.9 5.1 %collective-permute-start.10 = (f32[64,256]{1,0:T(8,128)S(1)}, f32[64,256]{1,0:T(8,128)S(1)}, u32[]{:S(2)}, u32[]{:S(2)}) collective-permute-start(f32[64,256]{1,0:T(8,128)S(1)} %slice.50), channel_id=1, source_target_pairs={{0,2},{1,3},{2,0},{3,1},{4,6},{5,7},{6,4},{7,5},{8,10},{9,11},{10,... | collective-permute-start | bytes 196616 | tf_op jit(solution)/shard_map/ppermute | solution.py:597
  57.4 4.3 %collective-permute-start.6 = (f32[64,256]{1,0:T(8,128)S(1)}, f32[64,256]{1,0:T(8,128)S(1)}, u32[]{:S(2)}, u32[]{:S(2)}) collective-permute-start(f32[64,256]{1,0:T(8,128)S(1)} %slice.48), channel_id=1, source_target_pairs={{0,2},{1,3},{2,0},{3,1},{4,6},{5,7},{6,4},{7,5},{8,10},{9,11},{10,... | collective-permute-start | bytes 196616 | tf_op jit(solution)/shard_map/ppermute | solution.py:597
  60.0 5.0 %collective-permute-start.11 = (f32[64,256]{1,0:T(8,128)S(1)}, f32[64,256]{1,0:T(8,128)S(1)}, u32[]{:S(2)}, u32[]{:S(2)}) collective-permute-start(f32[64,256]{1,0:T(8,128)S(1)} %slice_add_fusion.2), channel_id=1, source_target_pairs={{0,4},{1,5},{2,6},{3,7},{4,0},{5,1},{6,2},{7,3},{8,12},{9,13},{10,... | collective-permute-start | bytes 196616 | tf_op jit(solution)/shard_map/ppermute | solution.py:599
  61.7 5.9 %collective-permute-start.7 = (f32[64,256]{1,0:T(8,128)S(1)}, f32[64,256]{1,0:T(8,128)S(1)}, u32[]{:S(2)}, u32[]{:S(2)}) collective-permute-start(f32[64,256]{1,0:T(8,128)S(1)} %slice_add_fusion.3), channel_id=1, source_target_pairs={{0,4},{1,5},{2,6},{3,7},{4,0},{5,1},{6,2},{7,3},{8,12},{9,13},{10,... | collective-permute-start | bytes 196616 | tf_op jit(solution)/shard_map/ppermute | solution.py:599
  65.0 6.8 %collective-permute-start.12 = (f32[64,256]{1,0:T(8,128)S(1)}, f32[64,256]{1,0:T(8,128)S(1)}, u32[]{:S(2)}, u32[]{:S(2)}) collective-permute-start(f32[64,256]{1,0:T(8,128)S(1)} %add.37), channel_id=1, source_target_pairs={{0,8},{1,9},{2,10},{3,11},{4,12},{5,13},{6,14},{7,15},{8,0},{9,1},... | collective-permute-start | bytes 196616 | tf_op jit(solution)/shard_map/ppermute | solution.py:599
  67.7 5.2 %collective-permute-start.8 = (f32[64,256]{1,0:T(8,128)S(1)}, f32[64,256]{1,0:T(8,128)S(1)}, u32[]{:S(2)}, u32[]{:S(2)}) collective-permute-start(f32[64,256]{1,0:T(8,128)S(1)} %add.33), channel_id=1, source_target_pairs={{0,8},{1,9},{2,10},{3,11},{4,12},{5,13},{6,14},{7,15},{8,0},{9,1},... | collective-permute-start | bytes 196616 | tf_op jit(solution)/shard_map/ppermute | solution.py:599
  73.4 4.3 %collective-permute-start.14 = (f32[64,256]{1,0:T(8,128)S(1)}, f32[64,256]{1,0:T(8,128)S(1)}, u32[]{:S(2)}, u32[]{:S(2)}) collective-permute-start(f32[64,256]{1,0:T(8,128)S(1)} %add.34), channel_id=1, source_target_pairs={{0,16},{16,0},{1,17},{17,1},{2,18},{18,2},{3,19},{19,3},{4,20},{20... | collective-permute-start | bytes 196616 | tf_op jit(solution)/shard_map/ppermute | solution.py:610
  74.3 4.3 %collective-permute-start.15 = (f32[64,256]{1,0:T(8,128)S(1)}, f32[64,256]{1,0:T(8,128)S(1)}, u32[]{:S(2)}, u32[]{:S(2)}) collective-permute-start(f32[64,256]{1,0:T(8,128)S(1)} %add.38), channel_id=1, source_target_pairs={{0,16},{16,0},{1,17},{17,1},{2,18},{18,2},{3,19},{19,3},{4,20},{20... | collective-permute-start | bytes 196616 | tf_op jit(solution)/shard_map/ppermute | solution.py:610
  78.6 5.9 %collective-permute-start.16 = (f32[64,768]{1,0:T(8,128)S(1)}, f32[64,768]{1,0:T(8,128)S(1)}, u32[]{:S(2)}, u32[]{:S(2)}) collective-permute-start(f32[64,768]{1,0:T(8,128)S(1)} %pad_maximum_fusion.2), channel_id=1, source_target_pairs={{0,2},{1,3},{2,0},{3,1},{4,6},{5,7},{6,4},{7,5},{8,10},{9,11},{10,... | collective-permute-start | bytes 589832 | tf_op jit(solution)/shard_map/ppermute | solution.py:605
  80.9 20.0 %collective-permute-start.18 = (f32[3,256,256]{2,1,0:T(8,128)S(1)}, f32[3,256,256]{2,1,0:T(8,128)S(1)}, u32[]{:S(2)}, u32[]{:S(2)}) collective-permute-start(f32[3,256,256]{2,1,0:T(8,128)S(1)} %get-tuple-element.44.back_ref), channel_id=1, source_target_pairs={{0,16},{16,0},{1,17},{17,1},{2,18},{18,2},{3,19},{19,3},{4,20},{20... | collective-permute-start | bytes 2359304 | tf_op jit(solution)/shard_map/ppermute | solution.py:610
  84.6 1.8 %collective-permute-start.17 = (f32[128,768]{1,0:T(8,128)S(1)}, f32[128,768]{1,0:T(8,128)S(1)}, u32[]{:S(2)}, u32[]{:S(2)}) collective-permute-start(f32[128,768]{1,0:T(8,128)S(1)} %pad_maximum_fusion.1), channel_id=1, source_target_pairs={{0,1},{1,0},{2,3},{3,2},{4,5},{5,4},{6,7},{7,6},{8,9},{9,8},{10,11... | collective-permute-start | bytes 1179656 | tf_op jit(solution)/shard_map/ppermute | solution.py:605
  100.8 0.9 copy-start.3

commit v6 on v5

--- a/solution.py
+++ b/solution.py
@@ -24,7 +24,7 @@
     return pl.CostEstimate(flops=0, transcendentals=0, bytes_accessed=int(micros * 3.5e6))
 
 
-PARAMS = pltpu.CompilerParams(vmem_limit_bytes=48 * 2**20)
+PARAMS = pltpu.CompilerParams(vmem_limit_bytes=32 * 2**20)
 
 
 def pack_kernel(x_ref, *refs):
@@ -292,8 +292,9 @@
 
 
 def close_dot(left, right, over):
-    dot = functools.partial(lax.dot_general, dimension_numbers=((over, ((), ()))), preferred_element_type=jnp.float32)
-    return dot(left[0], right[0]) + (dot(left[0], right[1]) + dot(left[1], right[0]))
+    left = jnp.concatenate([left[0], left[0], left[1]], over[0][0])
+    right = jnp.concatenate([right[0], right[1], right[0]], over[1][0])
+    return lax.dot_general(left, right, (over, ((), ())), preferred_element_type=jnp.float32)
 
 
 ALONG = ((1,), (1,))
@@ -301,10 +302,14 @@
 ACROSS = ((0,), (0,))
 
 
+def joined(refs, k):
+    return pieces(jnp.concatenate([ref[k] for ref in refs], 1))
+
+
 def products(left, right):
     total = None
     for k in range(3):
-        part = close_dot(pieces(left[k]), pieces(right[k]), ALONG)
+        part = close_dot(joined(left, k), joined(right, k), ALONG)
         total = part if total is None else total + part
     return total
 
@@ -312,11 +317,10 @@
 def own_products(refs):
     dot = functools.partial(lax.dot_general, dimension_numbers=(ALONG, ((), ())), preferred_element_type=jnp.float32)
     main = mixed = None
-    for ref in refs:
-        for k in range(3):
-            high, low = pieces(ref[k])
-            one, two = dot(high, high), dot(high, low)
-            main, mixed = (one, two) if main is None else (main + one, mixed + two)
+    for k in range(3):
+        high, low = joined(refs, k)
+        one, two = dot(high, high), dot(high, low)
+        main, mixed = (one, two) if main is None else (main + one, mixed + two)
     return main + (mixed + mixed.T)
 
 
@@ -368,11 +372,11 @@
 
     @pl.when(is_first)
     def _():
-        work[...] = (products(front_ref, ready_ref) + products(back_ref, raw_ref)) * scale
+        work[...] = products((front_ref, back_ref), (ready_ref, raw_ref)) * scale
 
     @pl.when(jnp.logical_not(is_first))
     def _():
-        work[...] = (products(raw_ref, front_ref) + products(ready_ref, back_ref)) * scale
+        work[...] = products((raw_ref, ready_ref), (front_ref, back_ref)) * scale
 
     share = rows // count
     for place in range(count):
@@ -542,34 +546,39 @@
     )(travelled)
 
 
-def basis_kernel(own_ref, other_ref, outer_ref, inner_ref, front_ref, back_ref, raw_ref, ready_ref, early_ref, late_ref, out_ref):
+def basis_kernel(own_ref, other_ref, *refs):
+    own_panels, their_panels, (out_ref, held_ref, sems) = refs[:4], refs[4:8], refs[8:]
     me = lax.axis_index("probe")
-    quarter = outer_ref.shape[2]
-    own = pieces(own_ref[...])
+    quarter = own_panels[0].shape[2]
+    own, other = pieces(own_ref[...]), pieces(other_ref[...])
     places = (me * 3, 1 + me, (1 - me) * 2, (1 - me) * 2 + 1)
-    for place, ref in zip(places, (outer_ref, inner_ref, front_ref, back_ref)):
-        spot = pl.ds(pl.multiple_of(place * quarter, TILE), quarter)
-        out_ref[0, :, spot] = close_dot(own, pieces(ref[0]), PLAIN)
-
-    @pl.when(me == 1)
-    def _():
-        other = pieces(other_ref[...])
-        for at, ref in enumerate((raw_ref, ready_ref, early_ref, late_ref)):
-            spot = slice(quarter * at, quarter * at + quarter)
-            out_ref[0, :, spot] = out_ref[0, :, spot] + close_dot(other, pieces(ref[0]), PLAIN)
+    copies = [pltpu.make_async_copy(held_ref.at[k], out_ref.at[k], sems.at[k]) for k in range(3)]
+    for k in range(3):
+        for place, ref in zip(places, own_panels):
+            spot = pl.ds(pl.multiple_of(place * quarter, TILE), quarter)
+            held_ref[k, :, spot] = close_dot(own, pieces(ref[k]), PLAIN)
+
+        @pl.when(me == 1)
+        def _():
+            for at, ref in enumerate(their_panels):
+                spot = slice(quarter * at, quarter * at + quarter)
+                held_ref[k, :, spot] = held_ref[k, :, spot] + close_dot(other, pieces(ref[k]), PLAIN)
+
+        copies[k].start()
+    for copy in copies:
+        copy.wait()
 
 
 def basis_of(own, other, *panels):
     _, rows, quarter = panels[0].shape
-    weights = pl.BlockSpec((rows, rows), lambda k: (0, 0))
-    panel = pl.BlockSpec((1, rows, quarter), lambda k: (k, 0, 0))
+    shape = (3, rows, 4 * quarter)
     return pl.pallas_call(
         basis_kernel,
-        grid=(3,),
-        in_specs=[weights] * 2 + [panel] * len(panels),
-        out_specs=pl.BlockSpec((1, rows, 4 * quarter), lambda k: (k, 0, 0)),
-        out_shape=jax.ShapeDtypeStruct((3, rows, 4 * quarter), jnp.float32),
-        compiler_params=PARAMS,
+        in_specs=[VMEM] * (2 + len(panels)),
+        out_specs=pl.BlockSpec(memory_space=pltpu.HBM),
+        out_shape=jax.ShapeDtypeStruct(shape, jnp.float32),
+        scratch_shapes=[pltpu.VMEM(shape, jnp.float32), pltpu.SemaphoreType.DMA((3,))],
+        compiler_params=pltpu.CompilerParams(vmem_limit_bytes=24 * 2**20),
     )(own, other, *panels)
 
 

time: 107 us -> 104 us (0.972)
  Pallas kernels: 57 us -> 53.6 us
    pallas_call x3, Pallas kernels: 34.5 us -> 33 us  [segment(): pl.pallas_call(functools.partial(segment_kernel, x_at, coef_at, count, pa...]
    pallas_call x1, Pallas kernels: 4.27 us -> 2.84 us  [basis_of(): pl.pallas_call(basis_kernel, in_specs=[VMEM] * (2 + len(panels)), out_spe...]
  transfers between devices with their start and end apart: 19 -> 19, of which waited for: 12 -> 11; matrix products, arithmetic and copies ran while one was open for 1% -> 1% of each run, Pallas kernels for 46% -> 46%
where the time goes in v6:
time: 104 us; the launch traced here: 103 us
  Pallas kernels  53.6 us (52%)
  starting transfers between devices  27.1 us (26%)
  waiting for transfers between devices  19.2 us (18%)
  local copies, waits for them, and re-layouts  1.84 us (2%)
    pallas_call x3, Pallas kernels, segment(): pl.pallas_call(functools.partial(segment_kernel, x_at, coef_at, count, pa...  33 us
    pallas_call x1, Pallas kernels, factorize_pair(): pl.pallas_call(functools.partial(pair_kernel, count), in_specs=[VMEM], ou...  14.2 us
    ppermute x4, starting transfers between devices, scatter_sum(): block = block + lax.ppermute(block, axis, partners(axis, bit))  8.76 us
    ppermute x7, starting transfers between devices, swapped(): return lax.ppermute(block, 'probe', [(0, 1), (1, 0)])  7.68 us
    ppermute x4, waiting for transfers between devices, scatter_sum(): block = block + lax.ppermute(block, axis, partners(axis, bit))  5.35 us
    ppermute x4, starting transfers between devices, scatter_sum(): block = block[:half] + lax.ppermute(block[half:], axis, partners(axis, bit))  5.31 us
    ppermute x2, waiting for transfers between devices, gather_back(): lax.ppermute(block, axis, partners(axis, bit))  4.79 us
    ppermute x7, waiting for transfers between devices, swapped(): return lax.ppermute(block, 'probe', [(0, 1), (1, 0)])  4.04 us
  transfers between devices with their start and end apart: 19, of which 11 were waited for; matrix products, arithmetic and copies ran while one was open for 1% of the time, Pallas kernels for 46%

profile of v6, /device:TPU:0, one launch (start us, length us, event | category | flops | bytes accessed | tf_op | source)
XLA Modules:
  0.0 103.0 jit_solution(17077723584915569616)
XLA Ops:
  0.7 2.6 %shard_map.68 = (f32[64,256]{1,0:T(8,128)}, f32[64,256]{1,0:T(8,128)}, f32[64,256]{1,0:T(8,128)}, f32[40,1024]{1,0:T(8,128)}) custom-call(f32[3,256,1024]{2,1,0:T(8,128)} %x_ref.5, f32[3,3,4,1024]{3,2,1,0:T(4,128)} %bitcast.2, f32[1,1024]{1,0:T(1,128)} %bitcast.3, f32[3,1024]{1,0:T(4,128)} %refs_2_.1), custom_call_target="tpu_custom_call" | custom-call | tf_op jit(solution)/shard_map/pallas_call | solution.py:76
  3.3 2.4 %collective-permute-start = (f32[64,256]{1,0:T(8,128)}, f32[64,256]{1,0:T(8,128)S(1)}, u32[]{:S(2)}, u32[]{:S(2)}) collective-permute-start(f32[64,256]{1,0:T(8,128)} %get-tuple-element.25), channel_id=1, source_target_pairs={{0,1},{1,2},{2,3},{3,4},{4,5},{5,6},{6,7},{7,8},{8,9},{9,10},{10,1... | collective-permute-start | bytes 196616 | tf_op jit(solution)/shard_map/ppermute | solution.py:625
  5.7 1.3 %collective-permute-start.1 = (f32[64,256]{1,0:T(8,128)}, f32[64,256]{1,0:T(8,128)S(1)}, u32[]{:S(2)}, u32[]{:S(2)}) collective-permute-start(f32[64,256]{1,0:T(8,128)} %get-tuple-element.26), channel_id=1, source_target_pairs={{1,0},{2,1},{3,2},{4,3},{5,4},{6,5},{7,6},{8,7},{9,8},{10,9},{11,1... | collective-permute-start | bytes 196616 | tf_op jit(solution)/shard_map/ppermute | solution.py:625
  7.8 3.4 %collective-permute-done.1.refs_1_ = f32[64,256]{1,0:T(8,128)S(1)} collective-permute-done((f32[64,256]{1,0:T(8,128)}, f32[64,256]{1,0:T(8,128)S(1)}, u32[]{:S(2)}, u32[]{:S(2)}) %collective-permute-start.1) | collective-permute-done | bytes 65568 | tf_op jit(solution)/shard_map/ppermute | solution.py:625
  11.2 1.7 %collective-permute-start.2 = (f32[96,256]{1,0:T(8,128)S(1)}, f32[96,256]{1,0:T(8,128)S(1)}, u32[]{:S(2)}, u32[]{:S(2)}) collective-permute-start(f32[96,256]{1,0:T(8,128)S(1)} %maximum_select_fusion), channel_id=1, source_target_pairs={{0,16},{16,0},{1,17},{17,1},{2,18},{18,2},{3,19},{19,3},{4,20},{20... | collective-permute-start | bytes 294920 | tf_op jit(solution)/shard_map/ppermute | solution.py:619
  14.3 12.2 %shard_map.69 = (f32[3,256,256]{2,1,0:T(8,128)S(1)}, f32[3,256,256]{2,1,0:T(8,128)S(1)}) custom-call(s32[4]{0:T(128)S(1)} %copy-done.2, f32[3,256,1024]{2,1,0:T(8,128)S(1)} %copy-done, f32[40,1024]{1,0:T(8,128)S(1)} %copy-done.1, f32[64,256]{1,0:T(8,128)S(1)} %collective-permute-done.refs_0_, f32[64,256]{1,0:T(8,128)S(1)} %collective-permute-done.1.refs_1_), custom_call_target="tpu_custom_call" | custom-call | bytes 42000000 | tf_op jit(solution)/shard_map/pallas_call | solution.py:345
  26.6 1.7 %collective-permute-start.4 = (f32[3,256,256]{2,1,0:T(8,128)S(1)}, f32[3,256,256]{2,1,0:T(8,128)S(1)}, u32[]{:S(2)}, u32[]{:S(2)}) collective-permute-start(f32[3,256,256]{2,1,0:T(8,128)S(1)} %get-tuple-element.29.refs_2_.refs_1_), channel_id=1, source_target_pairs={{0,16},{16,0},{1,17},{17,1},{2,18},{18,2},{3,19},{19,3},{4,20},{20... | collective-permute-start | bytes 2359304 | tf_op jit(solution)/shard_map/ppermute | solution.py:619
  28.2 13.2 %shard_map.70 = (f32[3,256,256]{2,1,0:T(8,128)S(1)}, f32[3,256,256]{2,1,0:T(8,128)S(1)}, f32[256,256]{1,0:T(8,128)S(1)}) custom-call(s32[4]{0:T(128)S(1)} %copy-done.2, f32[3,256,1024]{2,1,0:T(8,128)S(1)} %copy-done, f32[40,1024]{1,0:T(8,128)S(1)} %copy-done.1, f32[64,256]{1,0:T(8,128)S(1)} %collective-permute-done.refs_0_, ...), custom_call_target="tpu_custom_call" | custom-call | bytes 42000000 | tf_op jit(solution)/shard_map/pallas_call | solution.py:345
  41.5 7.5 %shard_map.71.raw_ref.refs_4_ = f32[3,256,256]{2,1,0:T(8,128)S(1)} custom-call(s32[4]{0:T(128)S(1)} %copy-done.2, f32[3,256,256]{2,1,0:T(8,128)S(1)} %collective-permute-done.3.x_ref, f32[40,1024]{1,0:T(8,128)S(1)} %copy-done.1, f32[64,256]{1,0:T(8,128)S(1)} %collective-permute-done.refs_0_, f32[64,256]{1,0:T(8,128)S(1)} %collective-permute-done.1.refs_1_, ...), custom_call_target="tpu_custom_call" | custom-call | bytes 28000000 | tf_op jit(solution)/shard_map/pallas_call | solution.py:345
  53.3 2.8 %collective-permute-start.10 = (f32[64,256]{1,0:T(8,128)S(1)}, f32[64,256]{1,0:T(8,128)S(1)}, u32[]{:S(2)}, u32[]{:S(2)}) collective-permute-start(f32[64,256]{1,0:T(8,128)S(1)} %slice.50), channel_id=1, source_target_pairs={{0,2},{1,3},{2,0},{3,1},{4,6},{5,7},{6,4},{7,5},{8,10},{9,11},{10,... | collective-permute-start | bytes 196616 | tf_op jit(solution)/shard_map/ppermute | solution.py:606
  56.1 1.3 %collective-permute-start.6 = (f32[64,256]{1,0:T(8,128)S(1)}, f32[64,256]{1,0:T(8,128)S(1)}, u32[]{:S(2)}, u32[]{:S(2)}) collective-permute-start(f32[64,256]{1,0:T(8,128)S(1)} %slice.48), channel_id=1, source_target_pairs={{0,2},{1,3},{2,0},{3,1},{4,6},{5,7},{6,4},{7,5},{8,10},{9,11},{10,... | collective-permute-start | bytes 196616 | tf_op jit(solution)/shard_map/ppermute | solution.py:606
  57.4 1.4 %collective-permute-done.10 = f32[64,256]{1,0:T(8,128)S(1)} collective-permute-done((f32[64,256]{1,0:T(8,128)S(1)}, f32[64,256]{1,0:T(8,128)S(1)}, u32[]{:S(2)}, u32[]{:S(2)}) %collective-permute-start.10) | collective-permute-done | bytes 65568 | tf_op jit(solution)/shard_map/ppermute | solution.py:606
  58.8 3.1 %collective-permute-start.11 = (f32[64,256]{1,0:T(8,128)S(1)}, f32[64,256]{1,0:T(8,128)S(1)}, u32[]{:S(2)}, u32[]{:S(2)}) collective-permute-start(f32[64,256]{1,0:T(8,128)S(1)} %slice_add_fusion.2), channel_id=1, source_target_pairs={{0,4},{1,5},{2,6},{3,7},{4,0},{5,1},{6,2},{7,3},{8,12},{9,13},{10,... | collective-permute-start | bytes 196616 | tf_op jit(solution)/shard_map/ppermute | solution.py:608
  62.9 1.9 %collective-permute-done.11 = f32[64,256]{1,0:T(8,128)S(1)} collective-permute-done((f32[64,256]{1,0:T(8,128)S(1)}, f32[64,256]{1,0:T(8,128)S(1)}, u32[]{:S(2)}, u32[]{:S(2)}) %collective-permute-start.11) | collective-permute-done | bytes 65568 | tf_op jit(solution)/shard_map/ppermute | solution.py:608
  64.9 2.9 %collective-permute-start.12 = (f32[64,256]{1,0:T(8,128)S(1)}, f32[64,256]{1,0:T(8,128)S(1)}, u32[]{:S(2)}, u32[]{:S(2)}) collective-permute-start(f32[64,256]{1,0:T(8,128)S(1)} %add.37), channel_id=1, source_target_pairs={{0,8},{1,9},{2,10},{3,11},{4,12},{5,13},{6,14},{7,15},{8,0},{9,1},... | collective-permute-start | bytes 196616 | tf_op jit(solution)/shard_map/ppermute | solution.py:608
  67.8 1.8 %collective-permute-start.8 = (f32[64,256]{1,0:T(8,128)S(1)}, f32[64,256]{1,0:T(8,128)S(1)}, u32[]{:S(2)}, u32[]{:S(2)}) collective-permute-start(f32[64,256]{1,0:T(8,128)S(1)} %add.33), channel_id=1, source_target_pairs={{0,8},{1,9},{2,10},{3,11},{4,12},{5,13},{6,14},{7,15},{8,0},{9,1},... | collective-permute-start | bytes 196616 | tf_op jit(solution)/shard_map/ppermute | solution.py:608
  69.5 2.1 %collective-permute-done.12 = f32[64,256]{1,0:T(8,128)S(1)} collective-permute-done((f32[64,256]{1,0:T(8,128)S(1)}, f32[64,256]{1,0:T(8,128)S(1)}, u32[]{:S(2)}, u32[]{:S(2)}) %collective-permute-start.12) | collective-permute-done | bytes 65568 | tf_op jit(solution)/shard_map/ppermute | solution.py:608
  71.7 1.3 %collective-permute-done.8 = f32[64,256]{1,0:T(8,128)S(1)} collective-permute-done((f32[64,256]{1,0:T(8,128)S(1)}, f32[64,256]{1,0:T(8,128)S(1)}, u32[]{:S(2)}, u32[]{:S(2)}) %collective-permute-start.8) | collective-permute-done | bytes 65568 | tf_op jit(solution)/shard_map/ppermute | solution.py:608
  75.1 2.2 %collective-permute-done.14 = f32[64,256]{1,0:T(8,128)S(1)} collective-permute-done((f32[64,256]{1,0:T(8,128)S(1)}, f32[64,256]{1,0:T(8,128)S(1)}, u32[]{:S(2)}, u32[]{:S(2)}) %collective-permute-start.14) | collective-permute-done | bytes 65568 | tf_op jit(solution)/shard_map/ppermute | solution.py:619
  78.2 1.6 %collective-permute-start.16 = (f32[64,768]{1,0:T(8,128)S(1)}, f32[64,768]{1,0:T(8,128)S(1)}, u32[]{:S(2)}, u32[]{:S(2)}) collective-permute-start(f32[64,768]{1,0:T(8,128)S(1)} %pad_maximum_fusion.2), channel_id=1, source_target_pairs={{0,2},{1,3},{2,0},{3,1},{4,6},{5,7},{6,4},{7,5},{8,10},{9,11},{10,... | collective-permute-start | bytes 589832 | tf_op jit(solution)/shard_map/ppermute | solution.py:614
  80.8 3.1 %collective-permute-done.16 = f32[64,768]{1,0:T(8,128)S(1)} collective-permute-done((f32[64,768]{1,0:T(8,128)S(1)}, f32[64,768]{1,0:T(8,128)S(1)}, u32[]{:S(2)}, u32[]{:S(2)}) %collective-permute-start.16) | collective-permute-done | bytes 196640 | tf_op jit(solution)/shard_map/ppermute | solution.py:614
  84.0 1.7 %collective-permute-done.17 = f32[128,768]{1,0:T(8,128)S(1)} collective-permute-done((f32[128,768]{1,0:T(8,128)S(1)}, f32[128,768]{1,0:T(8,128)S(1)}, u32[]{:S(2)}, u32[]{:S(2)}) %collective-permute-start.17) | collective-permute-done | bytes 393248 | tf_op jit(solution)/shard_map/ppermute | solution.py:614
  85.8 14.2 %shard_map.73 = (f32[256,512]{1,0:T(8,128)}, f32[256,256]{1,0:T(8,128)S(1)}, f32[256,256]{1,0:T(8,128)S(1)}) custom-call(f32[256,768]{1,0:T(8,128)S(1)} %pad_maximum_fusion.g_ref), custom_call_target="tpu_custom_call" | custom-call | bytes 52500000 | tf_op jit(solution)/shard_map/pallas_call | solution.py:538
  99.9 2.8 %shard_map.74 = f32[3,256,1024]{2,1,0:T(8,128)} custom-call(f32[256,256]{1,0:T(8,128)S(1)} %get-tuple-element.41.own_ref, f32[256,256]{1,0:T(8,128)S(1)} %get-tuple-element.42.other_ref, f32[3,256,256]{2,1,0:T(8,128)S(1)} %get-tuple-element.30.refs_3_.refs_0_, f32[3,256,256]{2,1,0:T(8,128)S(1)} %get-tuple-element.29.refs_2_.refs_1_, ...), custom_call_target="tpu_custom_call" | custom-call | tf_op jit(solution)/shard_map/pallas_call | solution.py:575
  (49 shorter events, 11.8 us)
Async XLA Ops:
  0.6 12.2 %copy-start = (f32[3,256,1024]{2,1,0:T(8,128)S(1)}, f32[3,256,1024]{2,1,0:T(8,128)}, u32[]{:S(2)}) copy-start(f32[3,256,1024]{2,1,0:T(8,128)} %x_ref.5) | copy-start | bytes 9437188
  0.6 12.8 %copy-start.2 = (s32[4]{0:T(128)S(1)}, s32[4]{0:T(128)}, u32[]{:S(2)}) copy-start(s32[4]{0:T(128)} %off_ref.5) | copy-start | bytes 52
  3.3 4.5 %collective-permute-start = (f32[64,256]{1,0:T(8,128)}, f32[64,256]{1,0:T(8,128)S(1)}, u32[]{:S(2)}, u32[]{:S(2)}) collective-permute-start(f32[64,256]{1,0:T(8,128)} %get-tuple-element.25), channel_id=1, source_target_pairs={{0,1},{1,2},{2,3},{3,4},{4,5},{5,6},{6,7},{7,8},{8,9},{9,10},{10,1... | collective-permute-start | bytes 196616 | tf_op jit(solution)/shard_map/ppermute | solution.py:625
  5.7 5.5 %collective-permute-start.1 = (f32[64,256]{1,0:T(8,128)}, f32[64,256]{1,0:T(8,128)S(1)}, u32[]{:S(2)}, u32[]{:S(2)}) collective-permute-start(f32[64,256]{1,0:T(8,128)} %get-tuple-element.26), channel_id=1, source_target_pairs={{1,0},{2,1},{3,2},{4,3},{5,4},{6,5},{7,6},{8,7},{9,8},{10,9},{11,1... | collective-permute-start | bytes 196616 | tf_op jit(solution)/shard_map/ppermute | solution.py:625
  11.2 15.4 %collective-permute-start.2 = (f32[96,256]{1,0:T(8,128)S(1)}, f32[96,256]{1,0:T(8,128)S(1)}, u32[]{:S(2)}, u32[]{:S(2)}) collective-permute-start(f32[96,256]{1,0:T(8,128)S(1)} %maximum_select_fusion), channel_id=1, source_target_pairs={{0,16},{16,0},{1,17},{17,1},{2,18},{18,2},{3,19},{19,3},{4,20},{20... | collective-permute-start | bytes 294920 | tf_op jit(solution)/shard_map/ppermute | solution.py:619
  12.9 28.5 %collective-permute-start.3 = (f32[3,256,256]{2,1,0:T(8,128)S(1)}, f32[3,256,256]{2,1,0:T(8,128)S(1)}, u32[]{:S(2)}, u32[]{:S(2)}) collective-permute-start(f32[3,256,256]{2,1,0:T(8,128)S(1)} %constant_dynamic-slice_fusion), channel_id=1, source_target_pairs={{0,16},{16,0},{1,17},{17,1},{2,18},{18,2},{3,19},{19,3},{4,20},{20... | collective-permute-start | bytes 2359304 | tf_op jit(solution)/shard_map/ppermute | solution.py:619
  13.4 0.9 copy-start.1
  26.6 23.5 %collective-permute-start.4 = (f32[3,256,256]{2,1,0:T(8,128)S(1)}, f32[3,256,256]{2,1,0:T(8,128)S(1)}, u32[]{:S(2)}, u32[]{:S(2)}) collective-permute-start(f32[3,256,256]{2,1,0:T(8,128)S(1)} %get-tuple-element.29.refs_2_.refs_1_), channel_id=1, source_target_pairs={{0,16},{16,0},{1,17},{17,1},{2,18},{18,2},{3,19},{19,3},{4,20},{20... | collective-permute-start | bytes 2359304 | tf_op jit(solution)/shard_map/ppermute | solution.py:619
  51.1 2.2 %collective-permute-start.9 = (f32[128,256]{1,0:T(8,128)S(1)}, f32[128,256]{1,0:T(8,128)S(1)}, u32[]{:S(2)}, u32[]{:S(2)}) collective-permute-start(f32[128,256]{1,0:T(8,128)S(1)} %slice.42), channel_id=1, source_target_pairs={{0,1},{1,0},{2,3},{3,2},{4,5},{5,4},{6,7},{7,6},{8,9},{9,8},{10,11... | collective-permute-start | bytes 393224 | tf_op jit(solution)/shard_map/ppermute | solution.py:606
  52.3 20.7 %collective-permute-start.13 = (f32[3,256,256]{2,1,0:T(8,128)S(1)}, f32[3,256,256]{2,1,0:T(8,128)S(1)}, u32[]{:S(2)}, u32[]{:S(2)}) collective-permute-start(f32[3,256,256]{2,1,0:T(8,128)S(1)} %get-tuple-element.31.front_ref.refs_2_), channel_id=1, source_target_pairs={{0,16},{16,0},{1,17},{17,1},{2,18},{18,2},{3,19},{19,3},{4,20},{20... | collective-permute-start | bytes 2359304 | tf_op jit(solution)/shard_map/ppermute | solution.py:619
  53.0 3.1 %collective-permute-start.5 = (f32[128,256]{1,0:T(8,128)S(1)}, f32[128,256]{1,0:T(8,128)S(1)}, u32[]{:S(2)}, u32[]{:S(2)}) collective-permute-start(f32[128,256]{1,0:T(8,128)S(1)} %slice.38), channel_id=1, source_target_pairs={{0,1},{1,0},{2,3},{3,2},{4,5},{5,4},{6,7},{7,6},{8,9},{9,8},{10,11... | collective-permute-start | bytes 393224 | tf_op jit(solution)/shard_map/ppermute | solution.py:606
  53.3 5.5 %collective-permute-start.10 = (f32[64,256]{1,0:T(8,128)S(1)}, f32[64,256]{1,0:T(8,128)S(1)}, u32[]{:S(2)}, u32[]{:S(2)}) collective-permute-start(f32[64,256]{1,0:T(8,128)S(1)} %slice.50), channel_id=1, source_target_pairs={{0,2},{1,3},{2,0},{3,1},{4,6},{5,7},{6,4},{7,5},{8,10},{9,11},{10,... | collective-permute-start | bytes 196616 | tf_op jit(solution)/shard_map/ppermute | solution.py:606
  56.1 5.8 %collective-permute-start.6 = (f32[64,256]{1,0:T(8,128)S(1)}, f32[64,256]{1,0:T(8,128)S(1)}, u32[]{:S(2)}, u32[]{:S(2)}) collective-permute-start(f32[64,256]{1,0:T(8,128)S(1)} %slice.48), channel_id=1, source_target_pairs={{0,2},{1,3},{2,0},{3,1},{4,6},{5,7},{6,4},{7,5},{8,10},{9,11},{10,... | collective-permute-start | bytes 196616 | tf_op jit(solution)/shard_map/ppermute | solution.py:606
  58.8 6.0 %collective-permute-start.11 = (f32[64,256]{1,0:T(8,128)S(1)}, f32[64,256]{1,0:T(8,128)S(1)}, u32[]{:S(2)}, u32[]{:S(2)}) collective-permute-start(f32[64,256]{1,0:T(8,128)S(1)} %slice_add_fusion.2), channel_id=1, source_target_pairs={{0,4},{1,5},{2,6},{3,7},{4,0},{5,1},{6,2},{7,3},{8,12},{9,13},{10,... | collective-permute-start | bytes 196616 | tf_op jit(solution)/shard_map/ppermute | solution.py:608
  62.0 5.8 %collective-permute-start.7 = (f32[64,256]{1,0:T(8,128)S(1)}, f32[64,256]{1,0:T(8,128)S(1)}, u32[]{:S(2)}, u32[]{:S(2)}) collective-permute-start(f32[64,256]{1,0:T(8,128)S(1)} %slice_add_fusion.3), channel_id=1, source_target_pairs={{0,4},{1,5},{2,6},{3,7},{4,0},{5,1},{6,2},{7,3},{8,12},{9,13},{10,... | collective-permute-start | bytes 196616 | tf_op jit(solution)/shard_map/ppermute | solution.py:608
  64.9 6.8 %collective-permute-start.12 = (f32[64,256]{1,0:T(8,128)S(1)}, f32[64,256]{1,0:T(8,128)S(1)}, u32[]{:S(2)}, u32[]{:S(2)}) collective-permute-start(f32[64,256]{1,0:T(8,128)S(1)} %add.37), channel_id=1, source_target_pairs={{0,8},{1,9},{2,10},{3,11},{4,12},{5,13},{6,14},{7,15},{8,0},{9,1},... | collective-permute-start | bytes 196616 | tf_op jit(solution)/shard_map/ppermute | solution.py:608
  67.8 5.2 %collective-permute-start.8 = (f32[64,256]{1,0:T(8,128)S(1)}, f32[64,256]{1,0:T(8,128)S(1)}, u32[]{:S(2)}, u32[]{:S(2)}) collective-permute-start(f32[64,256]{1,0:T(8,128)S(1)} %add.33), channel_id=1, source_target_pairs={{0,8},{1,9},{2,10},{3,11},{4,12},{5,13},{6,14},{7,15},{8,0},{9,1},... | collective-permute-start | bytes 196616 | tf_op jit(solution)/shard_map/ppermute | solution.py:608
  73.0 4.3 %collective-permute-start.14 = (f32[64,256]{1,0:T(8,128)S(1)}, f32[64,256]{1,0:T(8,128)S(1)}, u32[]{:S(2)}, u32[]{:S(2)}) collective-permute-start(f32[64,256]{1,0:T(8,128)S(1)} %add.34), channel_id=1, source_target_pairs={{0,16},{16,0},{1,17},{17,1},{2,18},{18,2},{3,19},{19,3},{4,20},{20... | collective-permute-start | bytes 196616 | tf_op jit(solution)/shard_map/ppermute | solution.py:619
  73.9 4.3 %collective-permute-start.15 = (f32[64,256]{1,0:T(8,128)S(1)}, f32[64,256]{1,0:T(8,128)S(1)}, u32[]{:S(2)}, u32[]{:S(2)}) collective-permute-start(f32[64,256]{1,0:T(8,128)S(1)} %add.38), channel_id=1, source_target_pairs={{0,16},{16,0},{1,17},{17,1},{2,18},{18,2},{3,19},{19,3},{4,20},{20... | collective-permute-start | bytes 196616 | tf_op jit(solution)/shard_map/ppermute | solution.py:619
  78.2 5.7 %collective-permute-start.16 = (f32[64,768]{1,0:T(8,128)S(1)}, f32[64,768]{1,0:T(8,128)S(1)}, u32[]{:S(2)}, u32[]{:S(2)}) collective-permute-start(f32[64,768]{1,0:T(8,128)S(1)} %pad_maximum_fusion.2), channel_id=1, source_target_pairs={{0,2},{1,3},{2,0},{3,1},{4,6},{5,7},{6,4},{7,5},{8,10},{9,11},{10,... | collective-permute-start | bytes 589832 | tf_op jit(solution)/shard_map/ppermute | solution.py:614
  79.8 20.2 %collective-permute-start.18 = (f32[3,256,256]{2,1,0:T(8,128)S(1)}, f32[3,256,256]{2,1,0:T(8,128)S(1)}, u32[]{:S(2)}, u32[]{:S(2)}) collective-permute-start(f32[3,256,256]{2,1,0:T(8,128)S(1)} %get-tuple-element.44.back_ref.refs_3_), channel_id=1, source_target_pairs={{0,16},{16,0},{1,17},{17,1},{2,18},{18,2},{3,19},{19,3},{4,20},{20... | collective-permute-start | bytes 2359304 | tf_op jit(solution)/shard_map/ppermute | solution.py:619
  83.9 1.8 %collective-permute-start.17 = (f32[128,768]{1,0:T(8,128)S(1)}, f32[128,768]{1,0:T(8,128)S(1)}, u32[]{:S(2)}, u32[]{:S(2)}) collective-permute-start(f32[128,768]{1,0:T(8,128)S(1)} %pad_maximum_fusion.1), channel_id=1, source_target_pairs={{0,1},{1,0},{2,3},{3,2},{4,5},{5,4},{6,7},{7,6},{8,9},{9,8},{10,11... | collective-permute-start | bytes 1179656 | tf_op jit(solution)/shard_map/ppermute | solution.py:614

commit v7 on v6

--- a/solution.py
+++ b/solution.py
@@ -328,10 +328,11 @@
     edges, refs = refs[:bounds], refs[bounds:]
     rest, refs = (refs[:2], refs[2:]) if scale else ((), refs)
     out_refs, refs = refs[:parts], refs[parts:]
-    gram_ref, refs = (refs[0], refs[1:]) if scale else (None, refs)
+    gram_ref, work, refs = (refs[0], refs[-1], refs[1:-1]) if scale else (None, None, refs)
     segment_steps(x_at, coef_at, count, inward, off_ref, x_ref, coef_ref, edges, out_refs, refs)
     if scale:
-        gram_ref[...] = own_products((*out_refs, *rest)) * scale
+        work[...] = own_products((*out_refs, *rest)) * scale
+        in_travelling_order(work, gram_ref)
 
 
 def segment(x_at, coef_at, count, offsets, x, coefs, edges, ends=None, parts=1, inward=False, rest=(), scale=None):
@@ -342,6 +343,7 @@
     shapes = [jax.ShapeDtypeStruct((3, rows, count * TILE // parts), jnp.float32)] * parts
     if scale:
         shapes.append(jax.ShapeDtypeStruct((rows, rows), jnp.float32))
+        scratch.append(pltpu.VMEM((rows, rows), jnp.float32))
     result = pl.pallas_call(
         functools.partial(segment_kernel, x_at, coef_at, count, parts, inward, scale, len(edges)),
         in_specs=[SMEM, pl.BlockSpec(memory_space=pltpu.HBM)] + [VMEM] * (1 + len(edges) + len(rest)),
@@ -366,8 +368,16 @@
     return lax.bitwise_xor(lax.rem(lax.axis_index("slab"), count), jnp.int32(reversed_bits(place, count)))
 
 
-def cross_kernel(scale, count, front_ref, back_ref, raw_ref, ready_ref, gram_ref, own_ref, out_ref, work):
-    rows = gram_ref.shape[0]
+def in_travelling_order(work, out_ref):
+    rows = work.shape[0]
+    count = 1 << len(split_bits("slab")[0])
+    share = rows // count
+    for place in range(count):
+        spot = pl.ds(pl.multiple_of(block_at(place, count) * share, share), share)
+        out_ref[share * place : share * place + share, :] = work[spot, :]
+
+
+def cross_kernel(scale, front_ref, back_ref, raw_ref, ready_ref, out_ref, work):
     is_first = lax.axis_index("probe") == 0
 
     @pl.when(is_first)
@@ -378,23 +388,19 @@
     def _():
         work[...] = products((raw_ref, ready_ref), (front_ref, back_ref)) * scale
 
-    share = rows // count
-    for place in range(count):
-        spot = pl.ds(pl.multiple_of(block_at(place, count) * share, share), share)
-        own_ref[share * place : share * place + share, :] = gram_ref[spot, :]
-        out_ref[share * place : share * place + share, :] = work[spot, :]
-
-
-def cross_of(front, back, raw, ready, gram, scale, count):
-    rows = gram.shape[0]
+    in_travelling_order(work, out_ref)
+
+
+def cross_of(front, back, raw, ready, scale):
+    rows = front.shape[1]
     return pl.pallas_call(
-        functools.partial(cross_kernel, scale, count),
-        in_specs=[VMEM] * 5,
-        out_specs=[VMEM] * 2,
-        out_shape=[jax.ShapeDtypeStruct((rows, rows), jnp.float32)] * 2,
+        functools.partial(cross_kernel, scale),
+        in_specs=[VMEM] * 4,
+        out_specs=VMEM,
+        out_shape=jax.ShapeDtypeStruct((rows, rows), jnp.float32),
         scratch_shapes=[pltpu.VMEM((rows, rows), jnp.float32)],
         compiler_params=PARAMS,
-    )(front, back, raw, ready, gram)
+    )(front, back, raw, ready)
 
 
 def over_lanes(x, j):
@@ -665,8 +671,8 @@
     early = swapped(front)
     raw = run(lambda me: 0, at_raw, tiles, x=theirs, edges=edges, ends=ends)
     count = 1 << len(split_bits("slab")[0])
-    own, cross = cross_of(front, back, raw, ready, gram, scale, count)
-    own, cross = scatter_sum(own, "slab"), scatter_sum(cross, "slab")
+    cross = cross_of(front, back, raw, ready, scale)
+    own, cross = scatter_sum(gram, "slab"), scatter_sum(cross, "slab")
     own, cross, early = lax.optimization_barrier((own, cross, early))
     their_own, their_cross = swapped(own), swapped(cross)
     their_own, their_cross, late = lax.optimization_barrier((their_own, their_cross, back))

time: 104 us -> 104 us (level)
  starting transfers between devices: 27.1 us -> 29.4 us
  waiting for transfers between devices: 19.2 us -> 17.4 us
    ppermute x2, starting transfers between devices: 1.66 us -> 3.24 us  [gather_back(): lax.ppermute(block, axis, partners(axis, bit))]
    ppermute x4, starting transfers between devices: 5.31 us -> 6.45 us  [scatter_sum(): block = block[:half] + lax.ppermute(block[half:], axis, partners(axis, bit))]
    ppermute x4, waiting for transfers between devices: 5.35 us -> 4.24 us  [scatter_sum(): block = block + lax.ppermute(block, axis, partners(axis, bit))]
  transfers between devices with their start and end apart: 19 -> 19, of which waited for: 11 -> 10; matrix products, arithmetic and copies ran while one was open for 1% -> 1% of each run, Pallas kernels for 46% -> 47%
where the time goes in v7:
time: 104 us
  Pallas kernels  53.8 us (52%)
  starting transfers between devices  29.4 us (28%)
  waiting for transfers between devices  17.4 us (17%)
  local copies, waits for them, and re-layouts  1.85 us (2%)
    pallas_call x3, Pallas kernels, segment(): pl.pallas_call(functools.partial(segment_kernel, x_at, coef_at, count, pa...  33 us
    pallas_call x1, Pallas kernels, factorize_pair(): pl.pallas_call(functools.partial(pair_kernel, count), in_specs=[VMEM], ou...  14.2 us
    ppermute x4, starting transfers between devices, scatter_sum(): block = block + lax.ppermute(block, axis, partners(axis, bit))  8.83 us
    ppermute x7, starting transfers between devices, swapped(): return lax.ppermute(block, 'probe', [(0, 1), (1, 0)])  7.08 us
    ppermute x4, starting transfers between devices, scatter_sum(): block = block[:half] + lax.ppermute(block[half:], axis, partners(axis, bit))  6.45 us
    ppermute x2, waiting for transfers between devices, gather_back(): lax.ppermute(block, axis, partners(axis, bit))  4.62 us
    ppermute x4, waiting for transfers between devices, scatter_sum(): block = block + lax.ppermute(block, axis, partners(axis, bit))  4.24 us
    ppermute x7, waiting for transfers between devices, swapped(): return lax.ppermute(block, 'probe', [(0, 1), (1, 0)])  3.8 us
  transfers between devices with their start and end apart: 19, of which 10 were waited for; matrix products, arithmetic and copies ran while one was open for 1% of the time, Pallas kernels for 47%

profile of v7, /device:TPU:0, one launch (start us, length us, event | category | flops | bytes accessed | tf_op | source)
XLA Modules:
  0.0 103.7 jit_solution(12763473481642264198)
XLA Ops:
  0.7 2.6 %shard_map.68 = (f32[64,256]{1,0:T(8,128)}, f32[64,256]{1,0:T(8,128)}, f32[64,256]{1,0:T(8,128)}, f32[40,1024]{1,0:T(8,128)}) custom-call(f32[3,256,1024]{2,1,0:T(8,128)} %x_ref.5, f32[3,3,4,1024]{3,2,1,0:T(4,128)} %bitcast.2, f32[1,1024]{1,0:T(1,128)} %bitcast.3, f32[3,1024]{1,0:T(4,128)} %refs_2_.1), custom_call_target="tpu_custom_call" | custom-call | tf_op jit(solution)/shard_map/pallas_call | solution.py:76
  3.3 2.5 %collective-permute-start = (f32[64,256]{1,0:T(8,128)}, f32[64,256]{1,0:T(8,128)S(1)}, u32[]{:S(2)}, u32[]{:S(2)}) collective-permute-start(f32[64,256]{1,0:T(8,128)} %get-tuple-element.23), channel_id=1, source_target_pairs={{0,1},{1,2},{2,3},{3,4},{4,5},{5,6},{6,7},{7,8},{8,9},{9,10},{10,1... | collective-permute-start | bytes 196616 | tf_op jit(solution)/shard_map/ppermute | solution.py:631
  5.8 1.3 %collective-permute-start.1 = (f32[64,256]{1,0:T(8,128)}, f32[64,256]{1,0:T(8,128)S(1)}, u32[]{:S(2)}, u32[]{:S(2)}) collective-permute-start(f32[64,256]{1,0:T(8,128)} %get-tuple-element.24), channel_id=1, source_target_pairs={{1,0},{2,1},{3,2},{4,3},{5,4},{6,5},{7,6},{8,7},{9,8},{10,9},{11,1... | collective-permute-start | bytes 196616 | tf_op jit(solution)/shard_map/ppermute | solution.py:631
  7.9 3.4 %collective-permute-done.1.refs_1_ = f32[64,256]{1,0:T(8,128)S(1)} collective-permute-done((f32[64,256]{1,0:T(8,128)}, f32[64,256]{1,0:T(8,128)S(1)}, u32[]{:S(2)}, u32[]{:S(2)}) %collective-permute-start.1) | collective-permute-done | bytes 65568 | tf_op jit(solution)/shard_map/ppermute | solution.py:631
  11.3 1.7 %collective-permute-start.2 = (f32[96,256]{1,0:T(8,128)S(1)}, f32[96,256]{1,0:T(8,128)S(1)}, u32[]{:S(2)}, u32[]{:S(2)}) collective-permute-start(f32[96,256]{1,0:T(8,128)S(1)} %maximum_select_fusion), channel_id=1, source_target_pairs={{0,16},{16,0},{1,17},{17,1},{2,18},{18,2},{3,19},{19,3},{4,20},{20... | collective-permute-start | bytes 294920 | tf_op jit(solution)/shard_map/ppermute | solution.py:625
  14.5 12.2 %shard_map.69 = (f32[3,256,256]{2,1,0:T(8,128)S(1)}, f32[3,256,256]{2,1,0:T(8,128)S(1)}) custom-call(s32[4]{0:T(128)S(1)} %copy-done.3, f32[3,256,1024]{2,1,0:T(8,128)S(1)} %copy-done, f32[40,1024]{1,0:T(8,128)S(1)} %copy-done.1, f32[64,256]{1,0:T(8,128)S(1)} %collective-permute-done.refs_0_, f32[64,256]{1,0:T(8,128)S(1)} %collective-permute-done.1.refs_1_), custom_call_target="tpu_custom_call" | custom-call | bytes 42000000 | tf_op jit(solution)/shard_map/pallas_call | solution.py:347
  26.7 1.7 %collective-permute-start.8 = (f32[3,256,256]{2,1,0:T(8,128)S(1)}, f32[3,256,256]{2,1,0:T(8,128)S(1)}, u32[]{:S(2)}, u32[]{:S(2)}) collective-permute-start(f32[3,256,256]{2,1,0:T(8,128)S(1)} %get-tuple-element.27.refs_2_.refs_1_), channel_id=1, source_target_pairs={{0,16},{16,0},{1,17},{17,1},{2,18},{18,2},{3,19},{19,3},{4,20},{20... | collective-permute-start | bytes 2359304 | tf_op jit(solution)/shard_map/ppermute | solution.py:625
  28.4 13.3 %shard_map.70 = (f32[3,256,256]{2,1,0:T(8,128)S(1)}, f32[3,256,256]{2,1,0:T(8,128)S(1)}, f32[256,256]{1,0:T(8,128)S(1)}) custom-call(s32[4]{0:T(128)S(1)} %copy-done.3, f32[3,256,1024]{2,1,0:T(8,128)S(1)} %copy-done, f32[40,1024]{1,0:T(8,128)S(1)} %copy-done.2, f32[64,256]{1,0:T(8,128)S(1)} %collective-permute-done.refs_0_, ...), custom_call_target="tpu_custom_call" | custom-call | bytes 42000000 | tf_op jit(solution)/shard_map/pallas_call | solution.py:347
  41.7 2.2 %collective-permute-start.3 = (f32[128,256]{1,0:T(8,128)S(1)}, f32[128,256]{1,0:T(8,128)S(1)}, u32[]{:S(2)}, u32[]{:S(2)}) collective-permute-start(f32[128,256]{1,0:T(8,128)S(1)} %slice.38), channel_id=1, source_target_pairs={{0,1},{1,0},{2,3},{3,2},{4,5},{5,4},{6,7},{7,6},{8,9},{9,8},{10,11... | collective-permute-start | bytes 393224 | tf_op jit(solution)/shard_map/ppermute | solution.py:612
  44.2 7.5 %shard_map.71.raw_ref.refs_4_ = f32[3,256,256]{2,1,0:T(8,128)S(1)} custom-call(s32[4]{0:T(128)S(1)} %copy-done.3, f32[3,256,256]{2,1,0:T(8,128)S(1)} %collective-permute-done.7.x_ref, f32[40,1024]{1,0:T(8,128)S(1)} %copy-done.2, f32[64,256]{1,0:T(8,128)S(1)} %collective-permute-done.refs_0_, f32[64,256]{1,0:T(8,128)S(1)} %collective-permute-done.1.refs_1_, ...), custom_call_target="tpu_custom_call" | custom-call | bytes 28000000 | tf_op jit(solution)/shard_map/pallas_call | solution.py:347
  54.1 2.2 %collective-permute-start.4 = (f32[64,256]{1,0:T(8,128)S(1)}, f32[64,256]{1,0:T(8,128)S(1)}, u32[]{:S(2)}, u32[]{:S(2)}) collective-permute-start(f32[64,256]{1,0:T(8,128)S(1)} %slice.48), channel_id=1, source_target_pairs={{0,2},{1,3},{2,0},{3,1},{4,6},{5,7},{6,4},{7,5},{8,10},{9,11},{10,... | collective-permute-start | bytes 196616 | tf_op jit(solution)/shard_map/ppermute | solution.py:612
  58.6 2.0 %collective-permute-start.5 = (f32[64,256]{1,0:T(8,128)S(1)}, f32[64,256]{1,0:T(8,128)S(1)}, u32[]{:S(2)}, u32[]{:S(2)}) collective-permute-start(f32[64,256]{1,0:T(8,128)S(1)} %slice_add_fusion.3), channel_id=1, source_target_pairs={{0,4},{1,5},{2,6},{3,7},{4,0},{5,1},{6,2},{7,3},{8,12},{9,13},{10,... | collective-permute-start | bytes 196616 | tf_op jit(solution)/shard_map/ppermute | solution.py:614
  60.7 1.6 %collective-permute-start.11 = (f32[64,256]{1,0:T(8,128)S(1)}, f32[64,256]{1,0:T(8,128)S(1)}, u32[]{:S(2)}, u32[]{:S(2)}) collective-permute-start(f32[64,256]{1,0:T(8,128)S(1)} %slice_add_fusion.2), channel_id=1, source_target_pairs={{0,4},{1,5},{2,6},{3,7},{4,0},{5,1},{6,2},{7,3},{8,12},{9,13},{10,... | collective-permute-start | bytes 196616 | tf_op jit(solution)/shard_map/ppermute | solution.py:614
  63.3 3.3 %collective-permute-start.6 = (f32[64,256]{1,0:T(8,128)S(1)}, f32[64,256]{1,0:T(8,128)S(1)}, u32[]{:S(2)}, u32[]{:S(2)}) collective-permute-start(f32[64,256]{1,0:T(8,128)S(1)} %add.32), channel_id=1, source_target_pairs={{0,8},{1,9},{2,10},{3,11},{4,12},{5,13},{6,14},{7,15},{8,0},{9,1},... | collective-permute-start | bytes 196616 | tf_op jit(solution)/shard_map/ppermute | solution.py:614
  66.6 1.9 %collective-permute-start.12 = (f32[64,256]{1,0:T(8,128)S(1)}, f32[64,256]{1,0:T(8,128)S(1)}, u32[]{:S(2)}, u32[]{:S(2)}) collective-permute-start(f32[64,256]{1,0:T(8,128)S(1)} %add.37), channel_id=1, source_target_pairs={{0,8},{1,9},{2,10},{3,11},{4,12},{5,13},{6,14},{7,15},{8,0},{9,1},... | collective-permute-start | bytes 196616 | tf_op jit(solution)/shard_map/ppermute | solution.py:614
  68.6 2.2 %collective-permute-done.6 = f32[64,256]{1,0:T(8,128)S(1)} collective-permute-done((f32[64,256]{1,0:T(8,128)S(1)}, f32[64,256]{1,0:T(8,128)S(1)}, u32[]{:S(2)}, u32[]{:S(2)}) %collective-permute-start.6) | collective-permute-done | bytes 65568 | tf_op jit(solution)/shard_map/ppermute | solution.py:614
  71.9 1.4 %collective-permute-start.14 = (f32[64,256]{1,0:T(8,128)S(1)}, f32[64,256]{1,0:T(8,128)S(1)}, u32[]{:S(2)}, u32[]{:S(2)}) collective-permute-start(f32[64,256]{1,0:T(8,128)S(1)} %add.33), channel_id=1, source_target_pairs={{0,16},{16,0},{1,17},{17,1},{2,18},{18,2},{3,19},{19,3},{4,20},{20... | collective-permute-start | bytes 196616 | tf_op jit(solution)/shard_map/ppermute | solution.py:625
  74.0 2.2 %collective-permute-done.14 = f32[64,256]{1,0:T(8,128)S(1)} collective-permute-done((f32[64,256]{1,0:T(8,128)S(1)}, f32[64,256]{1,0:T(8,128)S(1)}, u32[]{:S(2)}, u32[]{:S(2)}) %collective-permute-start.14) | collective-permute-done | bytes 65568 | tf_op jit(solution)/shard_map/ppermute | solution.py:625
  76.2 1.5 %collective-permute-done.15 = f32[64,256]{1,0:T(8,128)S(1)} collective-permute-done((f32[64,256]{1,0:T(8,128)S(1)}, f32[64,256]{1,0:T(8,128)S(1)}, u32[]{:S(2)}, u32[]{:S(2)}) %collective-permute-start.15) | collective-permute-done | bytes 65568 | tf_op jit(solution)/shard_map/ppermute | solution.py:625
  77.8 3.2 %collective-permute-start.16 = (f32[64,768]{1,0:T(8,128)S(1)}, f32[64,768]{1,0:T(8,128)S(1)}, u32[]{:S(2)}, u32[]{:S(2)}) collective-permute-start(f32[64,768]{1,0:T(8,128)S(1)} %pad_maximum_fusion.2), channel_id=1, source_target_pairs={{0,2},{1,3},{2,0},{3,1},{4,6},{5,7},{6,4},{7,5},{8,10},{9,11},{10,... | collective-permute-start | bytes 589832 | tf_op jit(solution)/shard_map/ppermute | solution.py:620
  81.7 2.9 %collective-permute-done.16 = f32[64,768]{1,0:T(8,128)S(1)} collective-permute-done((f32[64,768]{1,0:T(8,128)S(1)}, f32[64,768]{1,0:T(8,128)S(1)}, u32[]{:S(2)}, u32[]{:S(2)}) %collective-permute-start.16) | collective-permute-done | bytes 196640 | tf_op jit(solution)/shard_map/ppermute | solution.py:620
  84.7 1.7 %collective-permute-done.17 = f32[128,768]{1,0:T(8,128)S(1)} collective-permute-done((f32[128,768]{1,0:T(8,128)S(1)}, f32[128,768]{1,0:T(8,128)S(1)}, u32[]{:S(2)}, u32[]{:S(2)}) %collective-permute-start.17) | collective-permute-done | bytes 393248 | tf_op jit(solution)/shard_map/ppermute | solution.py:620
  86.5 14.2 %shard_map.73 = (f32[256,512]{1,0:T(8,128)}, f32[256,256]{1,0:T(8,128)S(1)}, f32[256,256]{1,0:T(8,128)S(1)}) custom-call(f32[256,768]{1,0:T(8,128)S(1)} %pad_maximum_fusion.g_ref), custom_call_target="tpu_custom_call" | custom-call | bytes 52500000 | tf_op jit(solution)/shard_map/pallas_call | solution.py:544
  100.7 2.8 %shard_map.74 = f32[3,256,1024]{2,1,0:T(8,128)} custom-call(f32[256,256]{1,0:T(8,128)S(1)} %get-tuple-element.37.own_ref, f32[256,256]{1,0:T(8,128)S(1)} %get-tuple-element.38.other_ref, f32[3,256,256]{2,1,0:T(8,128)S(1)} %get-tuple-element.28.refs_3_.refs_0_, f32[3,256,256]{2,1,0:T(8,128)S(1)} %get-tuple-element.27.refs_2_.refs_1_, ...), custom_call_target="tpu_custom_call" | custom-call | tf_op jit(solution)/shard_map/pallas_call | solution.py:581
  (51 shorter events, 11.1 us)
Async XLA Ops:
  0.6 12.3 %copy-start = (f32[3,256,1024]{2,1,0:T(8,128)S(1)}, f32[3,256,1024]{2,1,0:T(8,128)}, u32[]{:S(2)}) copy-start(f32[3,256,1024]{2,1,0:T(8,128)} %x_ref.5) | copy-start | bytes 9437188
  0.6 12.9 %copy-start.3 = (s32[4]{0:T(128)S(1)}, s32[4]{0:T(128)}, u32[]{:S(2)}) copy-start(s32[4]{0:T(128)} %off_ref.5) | copy-start | bytes 52
  3.3 25.1 %copy-start.2 = (f32[40,1024]{1,0:T(8,128)S(1)}, f32[40,1024]{1,0:T(8,128)}, u32[]{:S(2)}) copy-start(f32[40,1024]{1,0:T(8,128)} %get-tuple-element.22.coef_ref) | copy-start | bytes 491524
  3.3 4.6 %collective-permute-start = (f32[64,256]{1,0:T(8,128)}, f32[64,256]{1,0:T(8,128)S(1)}, u32[]{:S(2)}, u32[]{:S(2)}) collective-permute-start(f32[64,256]{1,0:T(8,128)} %get-tuple-element.23), channel_id=1, source_target_pairs={{0,1},{1,2},{2,3},{3,4},{4,5},{5,6},{6,7},{7,8},{8,9},{9,10},{10,1... | collective-permute-start | bytes 196616 | tf_op jit(solution)/shard_map/ppermute | solution.py:631
  5.8 5.5 %collective-permute-start.1 = (f32[64,256]{1,0:T(8,128)}, f32[64,256]{1,0:T(8,128)S(1)}, u32[]{:S(2)}, u32[]{:S(2)}) collective-permute-start(f32[64,256]{1,0:T(8,128)} %get-tuple-element.24), channel_id=1, source_target_pairs={{1,0},{2,1},{3,2},{4,3},{5,4},{6,5},{7,6},{8,7},{9,8},{10,9},{11,1... | collective-permute-start | bytes 196616 | tf_op jit(solution)/shard_map/ppermute | solution.py:631
  11.3 15.4 %collective-permute-start.2 = (f32[96,256]{1,0:T(8,128)S(1)}, f32[96,256]{1,0:T(8,128)S(1)}, u32[]{:S(2)}, u32[]{:S(2)}) collective-permute-start(f32[96,256]{1,0:T(8,128)S(1)} %maximum_select_fusion), channel_id=1, source_target_pairs={{0,16},{16,0},{1,17},{17,1},{2,18},{18,2},{3,19},{19,3},{4,20},{20... | collective-permute-start | bytes 294920 | tf_op jit(solution)/shard_map/ppermute | solution.py:625
  13.1 31.2 %collective-permute-start.7 = (f32[3,256,256]{2,1,0:T(8,128)S(1)}, f32[3,256,256]{2,1,0:T(8,128)S(1)}, u32[]{:S(2)}, u32[]{:S(2)}) collective-permute-start(f32[3,256,256]{2,1,0:T(8,128)S(1)} %constant_dynamic-slice_fusion), channel_id=1, source_target_pairs={{0,16},{16,0},{1,17},{17,1},{2,18},{18,2},{3,19},{19,3},{4,20},{20... | collective-permute-start | bytes 2359304 | tf_op jit(solution)/shard_map/ppermute | solution.py:625
  13.6 0.9 copy-start.1
  26.7 25.1 %collective-permute-start.8 = (f32[3,256,256]{2,1,0:T(8,128)S(1)}, f32[3,256,256]{2,1,0:T(8,128)S(1)}, u32[]{:S(2)}, u32[]{:S(2)}) collective-permute-start(f32[3,256,256]{2,1,0:T(8,128)S(1)} %get-tuple-element.27.refs_2_.refs_1_), channel_id=1, source_target_pairs={{0,16},{16,0},{1,17},{17,1},{2,18},{18,2},{3,19},{19,3},{4,20},{20... | collective-permute-start | bytes 2359304 | tf_op jit(solution)/shard_map/ppermute | solution.py:625
  41.7 12.4 %collective-permute-start.3 = (f32[128,256]{1,0:T(8,128)S(1)}, f32[128,256]{1,0:T(8,128)S(1)}, u32[]{:S(2)}, u32[]{:S(2)}) collective-permute-start(f32[128,256]{1,0:T(8,128)S(1)} %slice.38), channel_id=1, source_target_pairs={{0,1},{1,0},{2,3},{3,2},{4,5},{5,4},{6,7},{7,6},{8,9},{9,8},{10,11... | collective-permute-start | bytes 393224 | tf_op jit(solution)/shard_map/ppermute | solution.py:612
  43.8 28.1 %collective-permute-start.13 = (f32[3,256,256]{2,1,0:T(8,128)S(1)}, f32[3,256,256]{2,1,0:T(8,128)S(1)}, u32[]{:S(2)}, u32[]{:S(2)}) collective-permute-start(f32[3,256,256]{2,1,0:T(8,128)S(1)} %get-tuple-element.30.front_ref.refs_2_), channel_id=1, source_target_pairs={{0,16},{16,0},{1,17},{17,1},{2,18},{18,2},{3,19},{19,3},{4,20},{20... | collective-permute-start | bytes 2359304 | tf_op jit(solution)/shard_map/ppermute | solution.py:625
  53.0 3.4 %collective-permute-start.9 = (f32[128,256]{1,0:T(8,128)S(1)}, f32[128,256]{1,0:T(8,128)S(1)}, u32[]{:S(2)}, u32[]{:S(2)}) collective-permute-start(f32[128,256]{1,0:T(8,128)S(1)} %slice.50), channel_id=1, source_target_pairs={{0,1},{1,0},{2,3},{3,2},{4,5},{5,4},{6,7},{7,6},{8,9},{9,8},{10,11... | collective-permute-start | bytes 393224 | tf_op jit(solution)/shard_map/ppermute | solution.py:612
  54.1 4.5 %collective-permute-start.4 = (f32[64,256]{1,0:T(8,128)S(1)}, f32[64,256]{1,0:T(8,128)S(1)}, u32[]{:S(2)}, u32[]{:S(2)}) collective-permute-start(f32[64,256]{1,0:T(8,128)S(1)} %slice.48), channel_id=1, source_target_pairs={{0,2},{1,3},{2,0},{3,1},{4,6},{5,7},{6,4},{7,5},{8,10},{9,11},{10,... | collective-permute-start | bytes 196616 | tf_op jit(solution)/shard_map/ppermute | solution.py:612
  56.4 4.3 %collective-permute-start.10 = (f32[64,256]{1,0:T(8,128)S(1)}, f32[64,256]{1,0:T(8,128)S(1)}, u32[]{:S(2)}, u32[]{:S(2)}) collective-permute-start(f32[64,256]{1,0:T(8,128)S(1)} %slice.52), channel_id=1, source_target_pairs={{0,2},{1,3},{2,0},{3,1},{4,6},{5,7},{6,4},{7,5},{8,10},{9,11},{10,... | collective-permute-start | bytes 196616 | tf_op jit(solution)/shard_map/ppermute | solution.py:612
  58.6 4.7 %collective-permute-start.5 = (f32[64,256]{1,0:T(8,128)S(1)}, f32[64,256]{1,0:T(8,128)S(1)}, u32[]{:S(2)}, u32[]{:S(2)}) collective-permute-start(f32[64,256]{1,0:T(8,128)S(1)} %slice_add_fusion.3), channel_id=1, source_target_pairs={{0,4},{1,5},{2,6},{3,7},{4,0},{5,1},{6,2},{7,3},{8,12},{9,13},{10,... | collective-permute-start | bytes 196616 | tf_op jit(solution)/shard_map/ppermute | solution.py:614
  60.7 5.9 %collective-permute-start.11 = (f32[64,256]{1,0:T(8,128)S(1)}, f32[64,256]{1,0:T(8,128)S(1)}, u32[]{:S(2)}, u32[]{:S(2)}) collective-permute-start(f32[64,256]{1,0:T(8,128)S(1)} %slice_add_fusion.2), channel_id=1, source_target_pairs={{0,4},{1,5},{2,6},{3,7},{4,0},{5,1},{6,2},{7,3},{8,12},{9,13},{10,... | collective-permute-start | bytes 196616 | tf_op jit(solution)/shard_map/ppermute | solution.py:614
  63.3 7.5 %collective-permute-start.6 = (f32[64,256]{1,0:T(8,128)S(1)}, f32[64,256]{1,0:T(8,128)S(1)}, u32[]{:S(2)}, u32[]{:S(2)}) collective-permute-start(f32[64,256]{1,0:T(8,128)S(1)} %add.32), channel_id=1, source_target_pairs={{0,8},{1,9},{2,10},{3,11},{4,12},{5,13},{6,14},{7,15},{8,0},{9,1},... | collective-permute-start | bytes 196616 | tf_op jit(solution)/shard_map/ppermute | solution.py:614
  66.6 5.2 %collective-permute-start.12 = (f32[64,256]{1,0:T(8,128)S(1)}, f32[64,256]{1,0:T(8,128)S(1)}, u32[]{:S(2)}, u32[]{:S(2)}) collective-permute-start(f32[64,256]{1,0:T(8,128)S(1)} %add.37), channel_id=1, source_target_pairs={{0,8},{1,9},{2,10},{3,11},{4,12},{5,13},{6,14},{7,15},{8,0},{9,1},... | collective-permute-start | bytes 196616 | tf_op jit(solution)/shard_map/ppermute | solution.py:614
  71.9 4.3 %collective-permute-start.14 = (f32[64,256]{1,0:T(8,128)S(1)}, f32[64,256]{1,0:T(8,128)S(1)}, u32[]{:S(2)}, u32[]{:S(2)}) collective-permute-start(f32[64,256]{1,0:T(8,128)S(1)} %add.33), channel_id=1, source_target_pairs={{0,16},{16,0},{1,17},{17,1},{2,18},{18,2},{3,19},{19,3},{4,20},{20... | collective-permute-start | bytes 196616 | tf_op jit(solution)/shard_map/ppermute | solution.py:625
  73.3 4.4 %collective-permute-start.15 = (f32[64,256]{1,0:T(8,128)S(1)}, f32[64,256]{1,0:T(8,128)S(1)}, u32[]{:S(2)}, u32[]{:S(2)}) collective-permute-start(f32[64,256]{1,0:T(8,128)S(1)} %add.38), channel_id=1, source_target_pairs={{0,16},{16,0},{1,17},{17,1},{2,18},{18,2},{3,19},{19,3},{4,20},{20... | collective-permute-start | bytes 196616 | tf_op jit(solution)/shard_map/ppermute | solution.py:625
  77.8 6.8 %collective-permute-start.16 = (f32[64,768]{1,0:T(8,128)S(1)}, f32[64,768]{1,0:T(8,128)S(1)}, u32[]{:S(2)}, u32[]{:S(2)}) collective-permute-start(f32[64,768]{1,0:T(8,128)S(1)} %pad_maximum_fusion.2), channel_id=1, source_target_pairs={{0,2},{1,3},{2,0},{3,1},{4,6},{5,7},{6,4},{7,5},{8,10},{9,11},{10,... | collective-permute-start | bytes 589832 | tf_op jit(solution)/shard_map/ppermute | solution.py:620
  81.0 19.7 %collective-permute-start.18 = (f32[3,256,256]{2,1,0:T(8,128)S(1)}, f32[3,256,256]{2,1,0:T(8,128)S(1)}, u32[]{:S(2)}, u32[]{:S(2)}) collective-permute-start(f32[3,256,256]{2,1,0:T(8,128)S(1)} %get-tuple-element.40.back_ref.refs_3_), channel_id=1, source_target_pairs={{0,16},{16,0},{1,17},{17,1},{2,18},{18,2},{3,19},{19,3},{4,20},{20... | collective-permute-start | bytes 2359304 | tf_op jit(solution)/shard_map/ppermute | solution.py:625
  84.7 1.8 %collective-permute-start.17 = (f32[128,768]{1,0:T(8,128)S(1)}, f32[128,768]{1,0:T(8,128)S(1)}, u32[]{:S(2)}, u32[]{:S(2)}) collective-permute-start(f32[128,768]{1,0:T(8,128)S(1)} %pad_maximum_fusion.1), channel_id=1, source_target_pairs={{0,1},{1,0},{2,3},{3,2},{4,5},{5,4},{6,7},{7,6},{8,9},{9,8},{10,11... | collective-permute-start | bytes 1179656 | tf_op jit(solution)/shard_map/ppermute | solution.py:620
